TPU v7x, 128 devices: a whole 4x4x4 slice. The times are simulated.
128 devices in a mesh: lon: 16 (over y_hi, z, core), lat: 8 (over y_lo, x).
Axes of the slice: x: 4, y: 4 (y_hi: 2, y_lo: 2; y = y_hi * 2 + y_lo), z: 4, core: 2. Of those that a mesh axis runs over, the one named last changes fastest.
Arguments:
- fine_tokens: bfloat16 [2, 96, 768, 192], P(None, 'lat', 'lon'), may hold values from -6 to 6
- cotangent: bfloat16 [2, 48, 384, 384], P(None, 'lat', 'lon'), may hold values from -6 to 6
- fine_gain: float32 [192], replicated, may hold values from 0.25 to 1.75
- fine_project: bfloat16 [192, 576], replicated, may hold values from -0.4375 to 0.4375
- fine_combine: bfloat16 [192, 192], replicated, may hold values from -0.4375 to 0.4375
- fine_table: float32 [1, 16, 3312, 6], P(None, 'lat'), may hold values from -2 to 303
- fine_types: float32 [3, 6], replicated, may hold values from -3 to 3
- merge_gain: float32 [768], replicated, may hold values from 0.25 to 1.75
- merge_weight: bfloat16 [768, 384], replicated, may hold values from -0.21875 to 0.21875
- coarse_gain: float32 [384], replicated, may hold values from 0.25 to 1.75
- coarse_project: bfloat16 [384, 1152], replicated, may hold values from -0.3125 to 0.3125
- coarse_combine: bfloat16 [384, 384], replicated, may hold values from -0.3125 to 0.3125
- coarse_table: float32 [1, 8, 3312, 12], P(None, 'lat'), may hold values from -2 to 303
- coarse_types: float32 [3, 12], replicated, may hold values from -3 to 3
- surface_type: int32 [96, 768], replicated, may hold values from 0 to 2
- latitude_valid: int32 [96], replicated, may hold values from 0 to 1, as said below
- bias_index: int32 [144, 144], replicated, may hold values from 0 to 3311
Outputs:
- coarse_tokens: bfloat16 [2, 48, 384, 384], P(None, 'lat', 'lon')
- tokens_gradient: bfloat16 [2, 96, 768, 192], P(None, 'lat', 'lon')
- fine_project_gradient: float32 [192, 576], replicated
- fine_combine_gradient: float32 [192, 192], replicated
- merge_gradient: float32 [768, 384], replicated
- coarse_project_gradient: float32 [384, 1152], replicated
- coarse_combine_gradient: float32 [384, 384], replicated
Inputs may be any that keep to these rules, and one draw needn't show every extreme that they name: `latitude_valid`: exactly 6 entries are 0: a run at the start and a run at the end, either of which may be empty.
All inputs are finite; a program needn't handle non-finite values.
Results may differ from a plain program's by a relative error of at most 0.035.
Values may be sent and summed in bfloat16 or wider, within the bound.
No kernel may reach another device: no remote copies, remote signals or barrier semaphores. Data moves between devices by JAX's collectives and lax.ppermute only.
A program may use at most 128 MiB of HBM per device.

v0:
```python
from functools import partial
import math

import jax
import jax.numpy as jnp
from jax import lax
from jax.sharding import PartitionSpec as P

H1 = 6
H2 = 12


EPSILON = 1e-05


def from_behind(value, axis, steps):
    count = lax.axis_size(axis)
    pairs = [(source, (source + steps) % count) for source in range(count)]
    return lax.ppermute(value, axis, pairs)


def normalize(tokens, gain_vector):
    values = tokens.astype(jnp.float32)
    average = jnp.mean(values, axis=-1, keepdims=True)
    centred = values - average
    spread = jnp.mean(centred * centred, axis=-1, keepdims=True)
    return (centred * lax.rsqrt(spread + EPSILON) * gain_vector).astype(jnp.bfloat16)


def merge_norm(tokens, gain_vector):
    levels, row_count, column_count, channels = tokens.shape
    merged = tokens.reshape(levels, row_count // 2, 2, column_count // 2, 2, channels)
    merged = merged.transpose(0, 1, 3, 2, 4, 5).reshape(
        levels, row_count // 2, column_count // 2, 4 * channels
    )
    return normalize(merged, gain_vector)


def surface_codes(surface_type, latitude_valid, stride):
    if stride == 1:
        surface = surface_type
        valid_rows = latitude_valid
    else:
        surface = surface_type[::2, ::2]
        valid_rows = jnp.maximum(latitude_valid[0::2], latitude_valid[1::2])
    return (jnp.roll(surface, (-3, -6), (0, 1)), jnp.roll(valid_rows, -3))


def contract(left, right):
    return lax.dot_general(
        left.reshape(-1, left.shape[-1]),
        right.reshape(-1, right.shape[-1]),
        (((0,), (0,)), ((), ())),
        preferred_element_type=jnp.float32,
    )


def attend(triple, bias_table, type_bias, bias_index, surface, valid_rows, wrap_rows, head_count):
    levels, row_count, column_count, triple_width = triple.shape
    channels = triple_width // 3
    head_size = channels // head_count
    level_windows, row_windows, column_windows = (levels // 2, row_count // 6, column_count // 12)
    blocks = triple.reshape(
        level_windows, 2, row_windows, 6, column_windows, 12, 3, head_count, head_size
    )
    blocks = blocks.transpose(2, 6, 0, 4, 7, 1, 3, 5, 8).reshape(
        row_windows, 3, level_windows, column_windows, head_count, 144, head_size
    )
    key_kinds = surface.reshape(row_windows, 6, column_windows, 12).transpose(0, 2, 1, 3)
    key_kinds = jnp.broadcast_to(
        key_kinds.reshape(row_windows, column_windows, 1, 72), (row_windows, column_windows, 2, 72)
    ).reshape(row_windows, column_windows, 144)
    valid_tokens = (
        jnp.broadcast_to(valid_rows.reshape(row_windows, 1, 6, 1), (row_windows, 2, 6, 12)).reshape(
            row_windows, 144
        )
        == 1
    )
    wrap_tokens = jnp.broadcast_to(
        wrap_rows.reshape(row_windows, 1, 6, 1), (row_windows, 2, 6, 12)
    ).reshape(row_windows, 144)
    level_flag = jnp.broadcast_to(
        (jnp.arange(levels) >= levels - 1).reshape(level_windows, 2, 1), (level_windows, 2, 72)
    ).reshape(level_windows, 144)
    same_level = level_flag[:, :, None] == level_flag[:, None, :]
    diagonal = jnp.eye(144, dtype=bool)
    tables = jnp.moveaxis(bias_table, 1, 0)
    score_scale = head_size ** (-0.5)

    def one_row(inputs):
        window_block, table_rows, kinds_here, valid_keys, wrap_flags = inputs
        queries, key_block, value_block = (window_block[0], window_block[1], window_block[2])
        scores = jnp.einsum(
            "lchqd,lchkd->lchqk", queries, key_block, preferred_element_type=jnp.float32
        )
        positional = jnp.take(table_rows, bias_index.reshape(-1), axis=1)
        positional = positional.reshape(level_windows, 144, 144, head_count).transpose(0, 3, 1, 2)
        one_hot = (kinds_here[..., None] == jnp.arange(3)).astype(jnp.float32)
        type_term = jnp.sum(one_hot[..., None] * type_bias, axis=2).transpose(0, 2, 1)
        scores = scores * score_scale + positional[:, None] + type_term[None, :, :, None, :]
        keep_pairs = (wrap_flags[:, None] == wrap_flags[None, :]) & (valid_keys[None, :] | diagonal)
        allowed = same_level & keep_pairs[None]
        scores = jnp.where(allowed[:, None, None], scores, -jnp.inf)
        row_top = lax.stop_gradient(jnp.max(scores, axis=-1, keepdims=True))
        weights = jnp.exp(scores - row_top)
        weights = (weights / jnp.sum(weights, axis=-1, keepdims=True)).astype(jnp.bfloat16)
        mixture = jnp.einsum(
            "lchqk,lchkd->lchqd", weights, value_block, preferred_element_type=jnp.float32
        )
        return mixture.astype(jnp.bfloat16)

    mixture = lax.map(one_row, (blocks, tables, key_kinds, valid_tokens, wrap_tokens))
    mixture = mixture.reshape(
        row_windows, level_windows, column_windows, head_count, 2, 6, 12, head_size
    )
    return mixture.transpose(1, 4, 0, 5, 2, 6, 3, 7).reshape(
        levels, row_count, column_count, channels
    )


def roll_forward(values):
    values = jnp.roll(values, -1, axis=0)
    arrived = from_behind(values[:, :, :6], "lon", -1)
    values = jnp.concatenate([values[:, :, 6:], arrived], axis=2)
    arrived = from_behind(values[:, :3], "lat", -1)
    return jnp.concatenate([values[:, 3:], arrived], axis=1)


def roll_backward(values):
    row_count = values.shape[1]
    column_count = values.shape[2]
    arrived = from_behind(values[:, row_count - 3 :], "lat", 1)
    values = jnp.concatenate([arrived, values[:, : row_count - 3]], axis=1)
    arrived = from_behind(values[:, :, column_count - 6 :], "lon", 1)
    values = jnp.concatenate([arrived, values[:, :, : column_count - 6]], axis=2)
    return jnp.roll(values, 1, axis=0)


def level_forward(tokens, gain_vector, project, combine, attention):
    normed = normalize(tokens, gain_vector)
    rolled = roll_forward(normed)
    triple = jnp.dot(rolled, project, preferred_element_type=jnp.float32).astype(jnp.bfloat16)
    restored = roll_backward(attention(triple))
    output = tokens.astype(jnp.float32) + jnp.dot(
        restored, combine, preferred_element_type=jnp.float32
    )
    return (output.astype(jnp.bfloat16), (rolled, triple, restored))


def level_backward(tokens, gain_vector, project, combine, attention, kept_arrays, delta_output):
    rolled, triple, restored = kept_arrays
    delta_restored = jnp.dot(delta_output, combine.T, preferred_element_type=jnp.float32).astype(
        jnp.bfloat16
    )
    combine_gradient = contract(restored, delta_output)
    attended, attention_pullback = jax.vjp(attention, triple)
    delta_triple = attention_pullback(roll_forward(delta_restored))[0]
    project_gradient = contract(rolled, delta_triple)
    delta_rolled = jnp.dot(delta_triple, project.T, preferred_element_type=jnp.float32).astype(
        jnp.bfloat16
    )
    delta_normed = roll_backward(delta_rolled)
    normed, norm_pullback = jax.vjp(lambda values: normalize(values, gain_vector), tokens)
    return (delta_output + norm_pullback(delta_normed)[0], project_gradient, combine_gradient)


def local(
    fine_tokens,
    cotangent,
    fine_gain,
    fine_project,
    fine_combine,
    fine_table,
    fine_types,
    merge_gain,
    merge_weight,
    coarse_gain,
    coarse_project,
    coarse_combine,
    coarse_table,
    coarse_types,
    surface_type,
    latitude_valid,
    bias_index,
):
    row_index = lax.axis_index("lat")
    column_index = lax.axis_index("lon")
    row_devices = lax.axis_size("lat")
    column_devices = lax.axis_size("lon")

    def local_attention(stride, bias_table, type_bias, head_count, row_count, column_count):
        surface, valid_rows = surface_codes(surface_type, latitude_valid, stride)
        surface = lax.dynamic_slice(
            surface, (row_index * row_count, column_index * column_count), (row_count, column_count)
        )
        valid_rows = lax.dynamic_slice(valid_rows, (row_index * row_count,), (row_count,))
        positions = row_index * row_count + jnp.arange(row_count, dtype=jnp.int32)
        wrap_rows = positions >= row_count * row_devices - 3
        return partial(
            attend,
            bias_table=bias_table,
            type_bias=type_bias,
            bias_index=bias_index,
            surface=surface,
            valid_rows=valid_rows,
            wrap_rows=wrap_rows,
            head_count=head_count,
        )

    fine_attention = local_attention(
        1, fine_table, fine_types, H1, fine_tokens.shape[1], fine_tokens.shape[2]
    )
    fine_output, fine_kept = level_forward(
        fine_tokens, fine_gain, fine_project, fine_combine, fine_attention
    )
    merged = merge_norm(fine_output, merge_gain)
    coarse_input = jnp.dot(merged, merge_weight, preferred_element_type=jnp.float32).astype(
        jnp.bfloat16
    )
    coarse_attention = local_attention(
        2, coarse_table, coarse_types, H2, coarse_input.shape[1], coarse_input.shape[2]
    )
    coarse_output, coarse_kept = level_forward(
        coarse_input, coarse_gain, coarse_project, coarse_combine, coarse_attention
    )
    delta_coarse, coarse_project_sum, coarse_combine_sum = level_backward(
        coarse_input,
        coarse_gain,
        coarse_project,
        coarse_combine,
        coarse_attention,
        coarse_kept,
        cotangent,
    )
    merge_sum = contract(merged, delta_coarse)
    delta_merged = jnp.dot(delta_coarse, merge_weight.T, preferred_element_type=jnp.float32).astype(
        jnp.bfloat16
    )
    merged_again, merge_pullback = jax.vjp(
        lambda values: merge_norm(values, merge_gain), fine_output
    )
    delta_fine = merge_pullback(delta_merged)[0]
    tokens_gradient, fine_project_sum, fine_combine_sum = level_backward(
        fine_tokens, fine_gain, fine_project, fine_combine, fine_attention, fine_kept, delta_fine
    )
    summed = lax.psum(
        (fine_project_sum, fine_combine_sum, merge_sum, coarse_project_sum, coarse_combine_sum),
        ("lon", "lat"),
    )
    fine_count = (
        fine_tokens.shape[0]
        * fine_tokens.shape[1]
        * fine_tokens.shape[2]
        * row_devices
        * column_devices
    )
    fine_scale = 1.0 / math.sqrt(fine_count)
    coarse_scale = 1.0 / math.sqrt(fine_count // 4)
    return (
        coarse_output,
        tokens_gradient,
        summed[0] * fine_scale,
        summed[1] * fine_scale,
        summed[2] * coarse_scale,
        summed[3] * coarse_scale,
        summed[4] * coarse_scale,
    )


def solution(mesh):
    in_specs = (
        P(None, "lat", "lon", None),
        P(None, "lat", "lon", None),
        P(),
        P(),
        P(),
        P(None, "lat", None, None),
        P(),
        P(),
        P(),
        P(),
        P(),
        P(),
        P(None, "lat", None, None),
        P(),
        P(),
        P(),
        P(),
    )
    out_specs = (P(None, "lat", "lon", None), P(None, "lat", "lon", None), P(), P(), P(), P(), P())
    return jax.shard_map(local, mesh=mesh, in_specs=in_specs, out_specs=out_specs, check_vma=False)
```

profile of v0, /device:TPU:0, one launch (start us, length us, event | category | flops | bytes accessed | tf_op | source)
XLA Modules:
  0.0 780.7 jit_solution(12201277744388792924)
XLA Ops:
  12.4 6.3 collective-permute-start
  32.2 38.9 %gather_fusion.2 = f32[20736,12]{1,0:T(8,128)} fusion(f32[3312,12]{1,0:T(8,128)S(1)} %bitcast.366, s32[21504]{0:T(1024)S(1)} %pad_clamp_fusion.2), kind=kCustom, calls=%fused_computation.2 | custom fusion | bytes 2073600 | tf_op jit(solution)/shard_map/while/body/eval_jaxpr/jit(_take)/gather | solution.py:96
  71.1 12.1 %copy.174 = f32[1,144,144,12]{1,2,3,0:T(8,128)} copy(f32[1,144,144,12]{3,2,1,0:T(8,128)} %bitcast.370) | data formatting | bytes 1990656 | tf_op jit(solution)/shard_map/while/body/eval_jaxpr/jit(_take)/gather | solution.py:96
  83.6 2.9 select_bitcast_fusion.2
  91.4 2.9 collective-permute-start.1
  98.6 7.2 reshape.1161
  105.8 8.1 %copy.161 = bf16[2,3,1,4,6,2,6,12,32]{8,3,7,6,5,4,1,0,2:T(4,128)(2,1)} copy(bf16[2,3,1,4,6,2,6,12,32]{8,4,1,7,3,6,0,5,2:T(8,128)(2,1)} %bitcast.371) | data formatting | bytes 2654208 | tf_op jit(solution)/shard_map/transpose | solution.py:66
  113.8 8.3 %copy.164 = bf16[2,3,1,4,6,144,32]{5,6,4,3,2,1,0:T(8,128)(2,1)} copy(bf16[2,3,1,4,6,144,32]{6,3,5,4,1,0,2:T(4,128)(2,1)} %bitcast.372) | data formatting | bytes 2654208
  123.1 123.6 %while.16 = (s32[]{:T(128)}, bf16[2,1,4,6,144,32]{4,5,3,2,1,0:T(8,128)(2,1)}, pred[2,144]{1,0:T(4,128)(4,1)S(1)}, pred[2,144]{1,0:T(4,128)(4,1)S(1)}, bf16[2,3,1...) while((s32[]{:T(128)}, ...), condition=%wide.wide.region_6.7_spmd.clone, body=%wide.wide.region_2.6_spmd.clone.sunk | while | flops 68270736 | bytes 15366989 | solution.py:112
  125.1 38.9 %gather_fusion.1 = f32[20736,6]{1,0:T(8,128)} fusion(f32[3312,6]{1,0:T(8,128)S(1)} %dynamic-slice_bitcast_fusion.43, s32[21504]{0:T(1024)S(1)} %pad_clamp_fusion.7), kind=kCustom, calls=%fused_computation.clone.clone.clone.1 | custom fusion | bytes 1078272 | tf_op jit(solution)/shard_map/while/body/eval_jaxpr/jit(_take)/gather | solution.py:96
  164.0 11.6 %copy.238 = f32[1,144,144,6]{1,2,3,0:T(8,128)S(1)} copy(f32[1,144,144,6]{3,2,1,0:T(8,128)} %bitcast.367) | data formatting | bytes 995328 | tf_op jit(solution)/shard_map/while/body/eval_jaxpr/jit(_take)/gather | solution.py:96
  176.7 4.7 fusion.263
  181.5 2.6 fusion.264
  186.9 38.9 %gather_fusion.1 = f32[20736,6]{1,0:T(8,128)} fusion(f32[3312,6]{1,0:T(8,128)S(1)} %dynamic-slice_bitcast_fusion.43, s32[21504]{0:T(1024)S(1)} %pad_clamp_fusion.7), kind=kCustom, calls=%fused_computation.clone.clone.clone.1 | custom fusion | bytes 1078272 | tf_op jit(solution)/shard_map/while/body/eval_jaxpr/jit(_take)/gather | solution.py:96
  225.8 11.6 %copy.238 = f32[1,144,144,6]{1,2,3,0:T(8,128)S(1)} copy(f32[1,144,144,6]{3,2,1,0:T(8,128)} %bitcast.367) | data formatting | bytes 995328 | tf_op jit(solution)/shard_map/while/body/eval_jaxpr/jit(_take)/gather | solution.py:96
  238.6 4.7 fusion.263
  243.3 2.5 fusion.264
  246.7 3.5 copy.165
  250.2 2.7 copy.166
  263.5 140.4 %while.15 = (s32[]{:T(128)}, bf16[2,1,4,6,144,32]{4,5,3,2,1,0:T(8,128)(2,1)}, bf16[2,1,4,6,144,32]{4,5,3,2,1,0:T(8,128)(2,1)}, pred[2,1,4,6,144,144]{5,4,3,2,1,0...) while((s32[]{:T(128)}, ...), condition=%wide.region_23.24_spmd.clone, body=%wide.region_19.23_spmd.clone.sunk | while | flops 36192148 | bytes 28220100 | solution.py:112
  266.2 38.8 %gather_fusion = f32[20736,6]{1,0:T(8,128)} fusion(f32[3312,6]{1,0:T(8,128)S(1)} %dynamic-slice_bitcast_fusion.38, s32[21504]{0:T(1024)S(1)} %pad_clamp_fusion.6), kind=kCustom, calls=%fused_computation.1.clone.clone.1 | custom fusion | bytes 1078272 | tf_op jit(solution)/shard_map/jvp()/while/body/eval_jaxpr/jit(_take)/gather | solution.py:96
  305.0 11.6 %copy.235 = f32[1,144,144,6]{1,2,3,0:T(8,128)S(1)} copy(f32[1,144,144,6]{3,2,1,0:T(8,128)} %bitcast.368) | data formatting | bytes 995328 | tf_op jit(solution)/shard_map/jvp()/while/body/eval_jaxpr/jit(_take)/gather | solution.py:96
  318.8 5.6 bitcast_dynamic-update-slice_fusion.10
  326.7 3.8 bitcast_dynamic-update-slice_fusion.11
  336.2 38.8 %gather_fusion = f32[20736,6]{1,0:T(8,128)} fusion(f32[3312,6]{1,0:T(8,128)S(1)} %dynamic-slice_bitcast_fusion.38, s32[21504]{0:T(1024)S(1)} %pad_clamp_fusion.6), kind=kCustom, calls=%fused_computation.1.clone.clone.1 | custom fusion | bytes 1078272 | tf_op jit(solution)/shard_map/jvp()/while/body/eval_jaxpr/jit(_take)/gather | solution.py:96
  375.0 11.6 %copy.235 = f32[1,144,144,6]{1,2,3,0:T(8,128)S(1)} copy(f32[1,144,144,6]{3,2,1,0:T(8,128)} %bitcast.368) | data formatting | bytes 995328 | tf_op jit(solution)/shard_map/jvp()/while/body/eval_jaxpr/jit(_take)/gather | solution.py:96
  388.9 5.8 bitcast_dynamic-update-slice_fusion.10
  397.0 3.8 bitcast_dynamic-update-slice_fusion.11
  412.1 3.2 collective-permute-done.3
  430.1 3.2 collective-permute-start.5
  436.3 4.1 reshape.1167
  440.4 4.0 fusion.179
  446.2 3.0 copy.170
  449.3 3.1 copy.169
  452.4 3.0 copy.171
  455.4 5.2 fusion.191
  464.8 3.2 fusion.110
  472.3 4.8 copy.191
  477.0 4.7 copy.192
  481.8 5.3 reshape.1190
  487.1 5.0 reshape.1178
  505.6 2.9 collective-permute-done.10
  508.7 7.3 collective-permute-done.11
  526.2 5.4 collective-permute-done.13
  532.5 2.8 reshape.1181
  537.4 2.8 copy.196
  541.9 34.4 %while.14 = (s32[]{:T(128)}, bf16[2,3,1,4,6,144,32]{5,6,4,3,1,2,0:T(8,128)(2,1)}, bf16[2,1,4,6,144,32]{4,5,3,2,1,0:T(8,128)(2,1)S(1)}, bf16[2,1,4,6,144,144]{4,5...) while((s32[]{:T(128)}, ...), condition=%wide.region_26.27_spmd, body=%wide.region_24.26_spmd.sunk | while | flops 138184704 | bytes 43998572 | solution.py:112
  543.4 3.1 fusion.250
  547.4 2.7 copy.232
  550.0 3.7 fusion.252
  553.8 3.3 fusion.251
  560.6 3.0 fusion.250
  564.6 2.7 copy.232
  567.2 3.7 fusion.252
  571.0 3.3 fusion.251
  576.3 8.0 %copy.199 = bf16[2,3,1,4,6,144,32]{6,3,5,4,1,0,2:T(4,128)(2,1)} copy(bf16[2,3,1,4,6,144,32]{5,6,4,3,1,2,0:T(8,128)(2,1)} %get-tuple-element.582) | data formatting | bytes 2654208 | tf_op jit(solution)/shard_map/transpose(jvp())/while | solution.py:112
  584.3 9.0 %copy.200 = bf16[1,2,2,6,4,12,3,6,32]{8,7,6,5,4,3,2,1,0:T(8,128)(2,1)} copy(bf16[1,2,2,6,4,12,3,6,32]{8,4,5,3,1,7,6,2,0:T(4,128)(2,1)} %bitcast.373) | data formatting | bytes 2654208 | tf_op jit(solution)/shard_map/transpose(jvp())/transpose | solution.py:66
  593.3 8.6 %reshape.1186 = bf16[1152,576]{1,0:T(8,128)(2,1)} reshape(bf16[1,2,2,6,4,12,3,6,32]{8,7,6,5,4,3,2,1,0:T(8,128)(2,1)} %copy.200) | data formatting | bytes 2654208 | tf_op jit(solution)/shard_map/reshape;transpose(jvp())/reshape | solution.py:52
  601.9 7.9 %reshape.1184 = bf16[2,12,48,576]{3,2,1,0:T(8,128)(2,1)S(1)} reshape(bf16[1,2,2,6,4,12,3,6,32]{8,7,6,5,4,3,2,1,0:T(8,128)(2,1)} %copy.200) | data formatting | bytes 2654208 | tf_op jit(solution)/shard_map/transpose(jvp())/reshape | solution.py:63
  609.8 2.7 fusion.192
  614.6 7.2 collective-permute-done.14
  623.0 7.1 collective-permute-done.15
  633.3 133.8 %all-reduce.9.cloned.1.call-done = (f32[192,576]{1,0:T(8,128)}, f32[192,192]{1,0:T(8,128)}, f32[768,384]{1,0:T(8,128)}, f32[384,1152]{1,0:T(8,128)}, f32[384,384]{1,0:T(8,128)}) async-done(((f32[192,576]{1,0:T(8,128)}, f32[192,192]{1,0:T(8,128)}, f32[768,384]{1,0:T(8,128)}, f32[384,1152]{1,0:T(8,128)}, f32[384,384]{1,0:T(8,128)}), (f32[192,576]{1,0:T(8,128)}, f32[192,192]{1,0:T(8,128)}, ...) | async-done | bytes 4128784 | tf_op jit(solution)/shard_map/psum | solution.py:246
  767.2 3.0 broadcast_multiply_fusion
  (496 shorter events, 150.2 us)
Async XLA Ops:
  7.2 428.6 %copy-start = (bf16[384,1152]{1,0:T(8,128)(2,1)S(1)}, bf16[384,1152]{1,0:T(8,128)(2,1)}, u32[]{:S(2)}) copy-start(bf16[384,1152]{1,0:T(8,128)(2,1)} %param.33) | copy-start | bytes 2654212
  7.2 11.5 %copy-start.37 = (bf16[2,6,24,384]{3,2,1,0:T(8,128)(2,1)S(1)}, bf16[2,6,24,384]{3,2,1,0:T(8,128)(2,1)}, u32[]{:S(2)}) copy-start(bf16[2,6,24,384]{3,2,1,0:T(8,128)(2,1)} %param.24) | copy-start | bytes 663556
  7.2 11.5 %copy-start.30 = (bf16[384,384]{1,0:T(8,128)(2,1)S(1)}, bf16[384,384]{1,0:T(8,128)(2,1)}, u32[]{:S(2)}) copy-start(bf16[384,384]{1,0:T(8,128)(2,1)} %param.34) | copy-start | bytes 884740
  7.2 759.9 %all-reduce.9.cloned.1.call-start = ((), (), s32[]{:S(2)}) async-start(), calls=%async_computation | async-start | bytes 8454144 | tf_op jit(solution)/shard_map/psum | solution.py:246
  11.6 8.9 %copy-start.47 = (s32[96,768]{1,0:T(8,128)S(1)}, s32[96,768]{1,0:T(8,128)}, u32[]{:S(2)}) copy-start(s32[96,768]{1,0:T(8,128)} %param.37) | copy-start | bytes 884740
  12.4 11.8 %copy-start.92 = (s32[96]{0:T(128)S(1)}, s32[96]{0:T(128)}, u32[]{:S(2)}) copy-start(s32[96]{0:T(128)} %param.38) | copy-start | bytes 1156
  12.4 13.2 %copy-start.12 = (s32[144,144]{1,0:T(8,128)S(1)}, s32[144,144]{1,0:T(8,128)}, u32[]{:S(2)}) copy-start(s32[144,144]{1,0:T(8,128)} %param.39) | copy-start | bytes 248836
  12.4 78.9 %collective-permute-start = (bf16[2,12,6,192]{3,2,1,0:T(8,128)(2,1)}, bf16[2,12,6,192]{3,2,1,0:T(8,128)(2,1)S(1)}, u32[]{:S(2)}, u32[]{:S(2)}) collective-permute-start(bf16[2,12,6,192]{3,2,1,0:T(8,128)(2,1)} %pad_maximum_fusion.21), channel_id=1, source_target_pairs={{0,120},{8,0},{16,8},{24,16},{32,24},{40,32},{48,40},{56,48},{64,5... | collective-permute-start | bytes 165896 | tf_op jit(solution)/shard_map/ppermute | solution.py:19
  19.7 74.6 %collective-permute-start.8 = (bf16[2,6,6,384]{3,2,1,0:T(8,128)(2,1)}, bf16[2,6,6,384]{3,2,1,0:T(8,128)(2,1)}, u32[]{:S(2)}, u32[]{:S(2)}) collective-permute-start(bf16[2,6,6,384]{3,2,1,0:T(8,128)(2,1)} %pad_maximum_fusion.23), channel_id=1, source_target_pairs={{0,120},{8,0},{16,8},{24,16},{32,24},{40,32},{48,40},{56,48},{64,5... | collective-permute-start | bytes 165896 | tf_op jit(solution)/shard_map/ppermute | solution.py:19
  71.1 12.2 %copy-start.70 = (pred[144,144]{1,0:T(8,128)(4,1)S(1)}, pred[144,144]{1,0:T(8,128)(4,1)}, u32[]{:S(2)}) copy-start(pred[144,144]{1,0:T(8,128)(4,1)} %compare_and_fusion.1) | copy-start | bytes 62212
  71.1 12.3 %copy-start.93 = (s32[96]{0:T(128)S(1)}, s32[96]{0:T(128)}, u32[]{:S(2)}) copy-start(s32[96]{0:T(128)} %param.38) | copy-start | bytes 1156
  71.1 12.3 %copy-start.94 = (s32[93]{0:T(128)S(1)}, s32[93]{0:T(128)}, u32[]{:S(2)}) copy-start(s32[93]{0:T(128)} %slice.266) | copy-start | bytes 1120
  71.1 12.4 %copy-start.85 = (f32[2,144,3]{1,0,2:T(2,128)S(1)}, f32[2,144,3]{1,0,2:T(2,128)}, u32[]{:S(2)}) copy-start(f32[2,144,3]{1,0,2:T(2,128)} %compare_convert_fusion) | copy-start | bytes 10372
  71.1 12.4 %copy-start.90 = (f32[3,12]{1,0:T(4,128)S(1)}, f32[3,12]{1,0:T(4,128)}, u32[]{:S(2)}) copy-start(f32[3,12]{1,0:T(4,128)} %param.36) | copy-start | bytes 436
  87.6 6.7 copy-start.36
  90.7 7.2 copy-start.34
  91.4 6.6 collective-permute-start.1
  95.8 311.7 %collective-permute-start.9 = (bf16[2,3,24,384]{3,2,1,0:T(8,128)(2,1)}, bf16[2,3,24,384]{3,2,1,0:T(8,128)(2,1)}, u32[]{:S(2)}, u32[]{:S(2)}) collective-permute-start(bf16[2,3,24,384]{3,2,1,0:T(8,128)(2,1)} %get-tuple-element.895), channel_id=1, source_target_pairs={{0,7},{1,0},{2,1},{3,2},{4,3},{5,4},{6,5},{7,6},{8,15},{9,8},{10,9... | collective-permute-start | bytes 331784 | tf_op jit(solution)/shard_map/ppermute | solution.py:19
  97.9 7.8 %copy-start.44 = (bf16[2,3,48,192]{3,2,1,0:T(8,128)(2,1)}, bf16[2,3,48,192]{3,2,1,0:T(8,128)(2,1)S(1)}, u32[]{:S(2)}) copy-start(bf16[2,3,48,192]{3,2,1,0:T(8,128)(2,1)S(1)} %collective-permute-done.1) | copy-start | bytes 331780
  246.7 6.2 copy-start.63
  246.7 16.7 %copy-start.75 = (pred[2,144]{1,0:T(4,128)(4,1)}, pred[2,144]{1,0:T(4,128)(4,1)S(1)}, u32[]{:S(2)}) copy-start(pred[2,144]{1,0:T(4,128)(4,1)S(1)} %get-tuple-element.1394) | copy-start | bytes 868
  246.7 16.7 %copy-start.76 = (pred[2,144]{1,0:T(4,128)(4,1)}, pred[2,144]{1,0:T(4,128)(4,1)S(1)}, u32[]{:S(2)}) copy-start(pred[2,144]{1,0:T(4,128)(4,1)S(1)} %get-tuple-element.1393) | copy-start | bytes 868
  255.1 8.4 %copy-start.11 = (s32[20736,1]{0,1:T(1,128)S(1)}, s32[20736,1]{0,1:T(1,128)}, u32[]{:S(2)}) copy-start(s32[20736,1]{0,1:T(1,128)} %get-tuple-element.1289) | copy-start | bytes 248836
  258.5 147.3 %collective-permute-start.2 = (bf16[2,3,48,192]{3,2,1,0:T(8,128)(2,1)}, bf16[2,3,48,192]{3,2,1,0:T(8,128)(2,1)}, u32[]{:S(2)}, u32[]{:S(2)}) collective-permute-start(bf16[2,3,48,192]{3,2,1,0:T(8,128)(2,1)} %slice.355), channel_id=1, source_target_pairs={{0,1},{1,2},{2,3},{3,4},{4,5},{5,6},{6,7},{7,0},{8,9},{9,10},{10,1... | collective-permute-start | bytes 331784 | tf_op jit(solution)/shard_map/ppermute | solution.py:19
  263.4 140.4 %copy-start.45 = (bf16[2,3,48,192]{3,2,1,0:T(8,128)(2,1)S(1)}, bf16[2,3,48,192]{3,2,1,0:T(8,128)(2,1)}, u32[]{:S(2)}) copy-start(bf16[2,3,48,192]{3,2,1,0:T(8,128)(2,1)} %copy-done.44) | copy-start | bytes 331780
  407.3 8.0 %collective-permute-start.3 = (bf16[2,12,6,192]{3,2,1,0:T(8,128)(2,1)}, bf16[2,12,6,192]{3,2,1,0:T(8,128)(2,1)S(1)}, u32[]{:S(2)}, u32[]{:S(2)}) collective-permute-start(bf16[2,12,6,192]{3,2,1,0:T(8,128)(2,1)} %pad_maximum_fusion.20), channel_id=1, source_target_pairs={{0,8},{8,16},{16,24},{24,32},{32,40},{40,48},{48,56},{56,64},{64,7... | collective-permute-start | bytes 165896 | tf_op jit(solution)/shard_map/ppermute | solution.py:19
  408.5 6.9 copy-start.16
  410.3 7.0 copy-start.2
  410.3 7.0 copy-start.59
  422.6 10.8 %copy-start.21 = (bf16[1,12,48,192]{3,2,1,0:T(8,128)(2,1)S(1)}, bf16[1,12,48,192]{3,2,1,0:T(8,128)(2,1)}, u32[]{:S(2)}) copy-start(bf16[1,12,48,192]{3,2,1,0:T(8,128)(2,1)} %copy-done.20) | copy-start | bytes 663556
  424.3 92.3 %copy-start.8 = (f32[2,6,24,384]{3,2,1,0:T(8,128)}, f32[2,6,24,384]{3,2,1,0:T(8,128)S(1)}, u32[]{:S(2)}) copy-start(f32[2,6,24,384]{3,2,1,0:T(8,128)S(1)} %get-tuple-element.911) | copy-start | bytes 1327108
  425.9 4.1 collective-permute-start.4
  430.1 10.3 %copy-start.32 = (bf16[2,3,24,384]{3,2,1,0:T(8,128)(2,1)}, bf16[2,3,24,384]{3,2,1,0:T(8,128)(2,1)S(1)}, u32[]{:S(2)}) copy-start(bf16[2,3,24,384]{3,2,1,0:T(8,128)(2,1)S(1)} %get-tuple-element.896) | copy-start | bytes 331780
  430.1 5.6 collective-permute-start.5
  446.2 9.2 %copy-start.81 = (pred[144,144]{0,1:T(8,128)(4,1)S(1)}, pred[144,144]{0,1:T(8,128)(4,1)}, u32[]{:S(2)}) copy-start(pred[144,144]{0,1:T(8,128)(4,1)} %fusion.157) | copy-start | bytes 62212
  446.2 9.2 %copy-start.84 = (f32[2,12,144]{2,1,0:T(8,128)S(1)}, f32[2,12,144]{2,1,0:T(8,128)}, u32[]{:S(2)}) copy-start(f32[2,12,144]{2,1,0:T(8,128)} %copy.176) | copy-start | bytes 41476
  495.5 8.1 %copy-start.33 = (bf16[2,3,24,384]{3,2,1,0:T(8,128)(2,1)S(1)}, bf16[2,3,24,384]{3,2,1,0:T(8,128)(2,1)}, u32[]{:S(2)}) copy-start(bf16[2,3,24,384]{3,2,1,0:T(8,128)(2,1)} %copy-done.32) | copy-start | bytes 331780
  497.0 6.6 copy-start.54
  497.0 6.7 copy-start.22
  498.1 10.5 %collective-permute-start.6 = (bf16[2,3,24,384]{3,2,1,0:T(8,128)(2,1)S(1)}, bf16[2,3,24,384]{3,2,1,0:T(8,128)(2,1)S(1)}, u32[]{:S(2)}, u32[]{:S(2)}) collective-permute-start(bf16[2,3,24,384]{3,2,1,0:T(8,128)(2,1)S(1)} %get-tuple-element.906), channel_id=1, source_target_pairs={{0,1},{1,2},{2,3},{3,4},{4,5},{5,6},{6,7},{7,0},{8,9},{9,10},{10,1... | collective-permute-start | bytes 331784 | tf_op jit(solution)/shard_map/ppermute | solution.py:19
  501.5 14.5 %copy-start.83 = (f32[384]{0:T(512)S(1)}, f32[384]{0:T(512)}, u32[]{:S(2)}) copy-start(f32[384]{0:T(512)} %param.32) | copy-start | bytes 4612
  501.5 6.9 collective-permute-start.10
  503.7 12.6 %copy-start.80 = (f32[2,6,24]{2,1,0:T(8,128)S(1)}, f32[2,6,24]{2,1,0:T(8,128)}, u32[]{:S(2)}) copy-start(f32[2,6,24]{2,1,0:T(8,128)} %copy-done.79) | copy-start | bytes 3460
  503.7 12.6 %copy-start.74 = (f32[2,6,24]{2,1,0:T(8,128)S(1)}, f32[2,6,24]{2,1,0:T(8,128)}, u32[]{:S(2)}) copy-start(f32[2,6,24]{2,1,0:T(8,128)} %copy-done.73) | copy-start | bytes 3460
  503.7 12.9 %copy-start.38 = (bf16[2,6,24,384]{3,2,1,0:T(8,128)(2,1)S(1)}, bf16[2,6,24,384]{3,2,1,0:T(8,128)(2,1)}, u32[]{:S(2)}) copy-start(bf16[2,6,24,384]{3,2,1,0:T(8,128)(2,1)} %param.24) | copy-start | bytes 663556
  505.6 11.3 %copy-start.72 = (f32[2,6,24]{2,1,0:T(8,128)S(1)}, f32[2,6,24]{2,1,0:T(8,128)}, u32[]{:S(2)}) copy-start(f32[2,6,24]{2,1,0:T(8,128)} %copy-done.71) | copy-start | bytes 3460
  505.6 11.3 %copy-start.86 = (f32[768]{0:T(1024)S(1)}, f32[768]{0:T(1024)}, u32[]{:S(2)}) copy-start(f32[768]{0:T(1024)} %param.30) | copy-start | bytes 9220
  508.5 7.5 collective-permute-start.11
  508.6 13.5 %collective-permute-start.7 = (bf16[2,6,6,384]{3,2,1,0:T(8,128)(2,1)S(1)}, bf16[2,6,6,384]{3,2,1,0:T(8,128)(2,1)S(1)}, u32[]{:S(2)}, u32[]{:S(2)}) collective-permute-start(bf16[2,6,6,384]{3,2,1,0:T(8,128)(2,1)S(1)} %pad_maximum_fusion.24), channel_id=1, source_target_pairs={{0,8},{8,16},{16,24},{24,32},{32,40},{40,48},{48,56},{56,64},{64,7... | collective-permute-start | bytes 165896 | tf_op jit(solution)/shard_map/ppermute | solution.py:19
  522.7 2.5 collective-permute-start.12
  525.2 6.3 collective-permute-start.13
  601.9 7.9 %copy-start.24 = (bf16[2,12,48,192]{3,2,1,0:T(8,128)(2,1)S(1)}, bf16[2,12,48,192]{3,2,1,0:T(8,128)(2,1)}, u32[]{:S(2)}) copy-start(bf16[2,12,48,192]{3,2,1,0:T(8,128)(2,1)} %pad_maximum_fusion.2) | copy-start | bytes 1327108
  613.5 8.5 %copy-start.9 = (f32[2,6,24,384]{3,2,1,0:T(8,128)S(1)}, f32[2,6,24,384]{3,2,1,0:T(8,128)}, u32[]{:S(2)}) copy-start(f32[2,6,24,384]{3,2,1,0:T(8,128)} %copy-done.8) | copy-start | bytes 1327108
  613.5 8.5 %copy-start.31 = (bf16[384,384]{1,0:T(8,128)(2,1)S(1)}, bf16[384,384]{1,0:T(8,128)(2,1)}, u32[]{:S(2)}) copy-start(bf16[384,384]{1,0:T(8,128)(2,1)} %param.34) | copy-start | bytes 884740
  613.5 8.5 %copy-start.50 = (bf16[1,6,24,384]{3,2,1,0:T(8,128)(2,1)S(1)}, bf16[1,6,24,384]{3,2,1,0:T(8,128)(2,1)}, u32[]{:S(2)}) copy-start(bf16[1,6,24,384]{3,2,1,0:T(8,128)(2,1)} %copy-done.49) | copy-start | bytes 331780
  613.5 8.5 %copy-start.52 = (bf16[1,6,24,384]{3,2,1,0:T(8,128)(2,1)S(1)}, bf16[1,6,24,384]{3,2,1,0:T(8,128)(2,1)}, u32[]{:S(2)}) copy-start(bf16[1,6,24,384]{3,2,1,0:T(8,128)(2,1)} %copy-done.51) | copy-start | bytes 331780
  614.2 7.7 collective-permute-start.14
  614.6 15.9 %copy-start.3 = (bf16[2,12,48,192]{3,2,1,0:T(8,128)(2,1)S(1)}, bf16[2,12,48,192]{3,2,1,0:T(8,128)(2,1)}, u32[]{:S(2)}) copy-start(bf16[2,12,48,192]{3,2,1,0:T(8,128)(2,1)} %param.23) | copy-start | bytes 1327108
  614.6 15.9 %copy-start.43 = (f32[2,12,48]{2,1,0:T(8,128)S(1)}, f32[2,12,48]{2,1,0:T(8,128)}, u32[]{:S(2)}) copy-start(f32[2,12,48]{2,1,0:T(8,128)} %copy-done.42) | copy-start | bytes 13828
  614.6 15.9 %copy-start.87 = (f32[192]{0:T(256)S(1)}, f32[192]{0:T(256)}, u32[]{:S(2)}) copy-start(f32[192]{0:T(256)} %param.25) | copy-start | bytes 2308
  621.9 9.2 %copy-start.69 = (f32[2,12,48]{2,1,0:T(8,128)S(1)}, f32[2,12,48]{2,1,0:T(8,128)}, u32[]{:S(2)}) copy-start(f32[2,12,48]{2,1,0:T(8,128)} %copy-done.68) | copy-start | bytes 13828
  621.9 9.2 %copy-start.65 = (f32[2,12,48]{2,1,0:T(8,128)S(1)}, f32[2,12,48]{2,1,0:T(8,128)}, u32[]{:S(2)}) copy-start(f32[2,12,48]{2,1,0:T(8,128)} %copy-done.64) | copy-start | bytes 13828
  621.9 8.3 %collective-permute-start.15 = (bf16[2,12,6,192]{3,2,1,0:T(8,128)(2,1)S(1)}, bf16[2,12,6,192]{3,2,1,0:T(8,128)(2,1)S(1)}, u32[]{:S(2)}, u32[]{:S(2)}) collective-permute-start(bf16[2,12,6,192]{3,2,1,0:T(8,128)(2,1)S(1)} %pad_maximum_fusion.18), channel_id=1, source_target_pairs={{0,8},{8,16},{16,24},{24,32},{32,40},{40,48},{48,56},{56,64},{64,7... | collective-permute-start | bytes 165896 | tf_op jit(solution)/shard_map/ppermute | solution.py:19
  623.0 8.8 %copy-start.15 = (bf16[2,12,48,192]{3,2,1,0:T(8,128)(2,1)S(1)}, bf16[2,12,48,192]{3,2,1,0:T(8,128)(2,1)}, u32[]{:S(2)}) copy-start(bf16[2,12,48,192]{3,2,1,0:T(8,128)(2,1)} %copy-done.14) | copy-start | bytes 1327108
  (65 other events, 187.5 us)
Sparse Core Ops, SparseCore 0:
  612.7 154.4 all-reduce.8
where the time goes:
time: 791 us; the launch traced here: 781 us
  local copies, waits for them, and re-layouts  434 us (55%)
  waiting for transfers between devices  171 us (22%)
  matrix products  75.8 us (10%)
  other arithmetic  59.7 us (8%)
  starting transfers between devices  23.9 us (3%)
  between operations  15.7 us (2%)
    gather x10, local copies, waits for them, and re-layouts, one_row(): positional = jnp.take(table_rows, bias_index.reshape(-1), axis=1)  253 us
    psum x1, waiting for transfers between devices, local(): lax.psum((fine_project_sum, fine_combine_sum, merge_sum, coarse_project_s...  134 us
    ppermute x16, waiting for transfers between devices, from_behind(): return lax.ppermute(value, axis, pairs)  37.4 us
    sub x5, matrix products, one_row(): weights = jnp.exp(scores - row_top)  26 us
    reshape x4, local copies, waits for them, and re-layouts, attend(): triple.reshape(level_windows, 2, row_windows, 6, column_windows, 12, 3, h...  24.2 us
    ppermute x16, starting transfers between devices, from_behind(): return lax.ppermute(value, axis, pairs)  23.9 us
    transpose x3, local copies, waits for them, and re-layouts, attend(): blocks.transpose(2, 6, 0, 4, 7, 1, 3, 5, 8)  21.8 us
    dot_general x9, matrix products, one_row(): jnp.einsum('lchqk,lchkd->lchqd', weights, value_block, preferred_element_...  17.5 us
  transfers between devices with their start and end apart: 17, of which 10 were waited for; matrix products, arithmetic and copies ran while one was open for 51% of the time, Pallas kernels for 0%

commit v1 on v0

v1 whole, which is shorter than its diff:
```python
import math
from functools import partial

import numpy as np
import jax
import jax.numpy as jnp
from jax import lax
from jax.experimental import pallas as pl
from jax.experimental.pallas import tpu as pltpu
from jax.sharding import PartitionSpec as P

F32 = jnp.float32
BF16 = jnp.bfloat16
EPSILON = 1e-05
HEAD = 32
SCALE = HEAD ** (-0.5)
BLOCKED = -1e30
NT = (((1,), (1,)), ((), ()))
TN = (((0,), (0,)), ((), ()))
NN = (((1,), (0,)), ((), ()))


def pad16(n):
    return (n + 15) // 16 * 16


class Shift:
    def __init__(self, rows, cols, dr, dc, source, target, forward):
        if forward:
            ranges = (
                (range(0, dr), range(dc, cols)),
                (range(dr, rows), range(0, dc)),
                (range(0, dr), range(0, dc)),
            )
        else:
            ranges = (
                (range(rows - dr, rows), range(0, cols - dc)),
                (range(0, rows - dr), range(cols - dc, cols)),
                (range(rows - dr, rows), range(cols - dc, cols)),
            )
        lists = [[(r, c) for r in rr for c in cc] for rr, cc in ranges]
        self.sizes = [pad16(len(x)) for x in lists]
        self.own = rows * cols
        send = []
        for x, size in zip(lists, self.sizes):
            send += [source(r, c) for r, c in x] + [0] * (size - len(x))
        self.send = np.array(send, np.int32)[:, None]
        offsets = [self.own, self.own + self.sizes[0], self.own + self.sizes[0] + self.sizes[1]]
        places = [{rc: o + n for n, rc in enumerate(x)} for x, o in zip(lists, offsets)]
        take = np.zeros((self.own, 1), np.int32)
        sign = 1 if forward else -1
        for r in range(rows):
            for c in range(cols):
                a, b = r + sign * dr, c + sign * dc
                out_row, out_col = not 0 <= a < rows, not 0 <= b < cols
                a, b = a % rows, b % cols
                if out_row or out_col:
                    which = 2 if out_row and out_col else (0 if out_row else 1)
                    place = places[which][(a, b)]
                else:
                    place = source(a, b)
                take[target(r, c), 0] = place
        self.take = take
        self.total = self.own + sum(self.sizes)


def pad8(n):
    return (n + 7) // 8 * 8


def raster(cols):
    return lambda r, c: r * cols + c


def windowed(cols):
    per_row = cols // 12
    return lambda r, c: ((r // 6) * per_row + c // 12) * 72 + (r % 6) * 12 + c % 12


def merging(cols):
    coarse = windowed(cols // 2)
    quarter = lambda rows: rows
    return lambda r, c: ((r % 2) * 2 + c % 2) * 144 + coarse(r // 2, c // 2)


def one_hot(index, width):
    lanes = lax.broadcasted_iota(jnp.int32, (index.shape[0], width), 1)
    return jnp.where(lanes == index, 1.0, 0.0).astype(BF16)


def mm(a, b, dims=NN):
    return lax.dot_general(a, b, dims, preferred_element_type=F32)


def round16(x):
    return x.astype(BF16).astype(F32)


def pick(take, total, own, parts):
    return mm(one_hot(take, total), jnp.concatenate([own] + parts, axis=0))


def head_masks(channels):
    lanes = lax.broadcasted_iota(jnp.int32, (1, channels), 1)
    return [
        jnp.where((lanes >= HEAD * h) & (lanes < HEAD * (h + 1)), 1.0, 0.0)
        for h in range(channels // HEAD)
    ]


def spread_heads(x, masks):
    return jnp.concatenate([x * m for m in masks], axis=0).astype(BF16)


def fold_heads(x, masks):
    out = x[0:72] * masks[0]
    for h in range(1, len(masks)):
        out = out + x[72 * h : 72 * (h + 1)] * masks[h]
    return out


def weights_of(k16, qbig, kinds16, types16, bias):
    x = mm(k16, qbig, NT) * SCALE + (mm(kinds16, types16, NT) + bias)
    e = jnp.exp(x - jnp.max(x, axis=0, keepdims=True))
    return (e * (1.0 / jnp.sum(e, axis=0, keepdims=True))).astype(BF16)


def attention_back(q, k, v, p16, do, masks):
    k16 = k.astype(BF16)
    dobig = spread_heads(do, masks)
    qbig = spread_heads(q, masks)
    p = p16.astype(F32)
    dv = mm(p16, dobig)
    dp = round16(mm(v.astype(BF16), dobig, NT))
    pd = p * dp
    ds = ((pd - p * jnp.sum(pd, axis=0, keepdims=True)) * SCALE).astype(BF16)
    dq = fold_heads(mm(ds, k16, TN), masks)
    dk = mm(ds, qbig)
    return dq, dk, dv


def moments(parts):
    count = sum(x.shape[-1] for x in parts)
    mean = sum(jnp.sum(x, axis=-1, keepdims=True) for x in parts) * (1.0 / count)
    centred = [x - mean for x in parts]
    spread = sum(jnp.sum(c * c, axis=-1, keepdims=True) for c in centred) * (1.0 / count)
    return centred, lax.rsqrt(spread + EPSILON)


def norm_back(centred, inverse, gains, deltas):
    count = sum(x.shape[-1] for x in centred)
    scaled = [d * g for d, g in zip(deltas, gains)]
    unit = [c * inverse for c in centred]
    mean = sum(jnp.sum(s, axis=-1, keepdims=True) for s in scaled) * (1.0 / count)
    along = sum(jnp.sum(s * u, axis=-1, keepdims=True) for s, u in zip(scaled, unit)) * (1.0 / count)
    return [(s - mean - u * along) * inverse for s, u in zip(scaled, unit)]


def send_out(index, own, refs, level):
    rows = mm(one_hot(index, own.shape[0]), own).astype(BF16)
    at = 0
    for ref in refs:
        n = ref.shape[1]
        ref[level] = rows[at : at + n]
        at += n


def prepare_kernel(fsel, csel, tokens, cot, fa, fb, fc, ca, cb, cc):
    nf, nc = tokens.shape[0] // 2, cot.shape[0] // 2
    for level in range(2):
        send_out(fsel[...], tokens[level * nf : (level + 1) * nf, :], (fa, fb, fc), level)
        send_out(csel[...], cot[level * nc : (level + 1) * nc, :], (ca, cb, cc), level)


def bias_kernel(
    level_rows, place, valid, index, table, surface, types, row, col,
    bias, kinds, typed, raw, parts,
):
    lat, lon, lats = place[0], place[1], place[2]
    windows, heads = bias.shape[1], bias.shape[3] // 72
    chunks = table.shape[1] // 128
    count = table.shape[0]
    pieces = [table[:, c * 128 : (c + 1) * 128] for c in range(chunks)]
    pad = [jnp.zeros((-count % 8, 128), F32)] if count % 8 else []
    whole = count + (-count % 8)
    high_part = jnp.concatenate([x for p in pieces for x in [round16(p)] + pad], axis=0)
    low_part = jnp.concatenate([x for p in pieces for x in [p - round16(p)] + pad], axis=0)
    parts[:, 0:128] = high_part.astype(BF16)
    parts[:, 128:256] = low_part.astype(BF16)
    lanes_down = lax.broadcasted_iota(jnp.int32, (128, 128), 0)

    def two_rows(i, carry):
        places = [index[2 * i + j] for j in range(2)]
        hot = jnp.concatenate(
            [jnp.where(lanes_down == (x & 127), 1.0, 0.0) for x in places], axis=1
        ).astype(BF16)
        found = mm(parts[...], jnp.concatenate([hot, hot], axis=0))
        for j in range(2):
            chunk = jnp.broadcast_to(places[j] >> 7, (8, 128))
            for g in range(0, whole, 8):
                total = jnp.zeros((8, 128), F32)
                for c in range(chunks):
                    at = c * whole + g
                    total = jnp.where(chunk == c, found[at : at + 8, 128 * j : 128 * (j + 1)], total)
                raw[pl.ds(g * 144 + 2 * i + j, 8, stride=144), :] = total
        return carry

    lax.fori_loop(0, 72, two_rows, 0, unroll=4)

    key = lax.broadcasted_iota(jnp.int32, (72, 72), 0)
    query = lax.broadcasted_iota(jnp.int32, (72, 72), 1)
    key_row = sum(jnp.where(key >= 12 * r, 1, 0) for r in range(1, 6))
    apart = jnp.where((key >= 36) != (query >= 36), 1, 0)
    rows, columns = surface.shape[0] // level_rows, surface.shape[1] // level_rows
    at_end = jnp.where(lat == lats - 1, 1, 0)
    for rw in range(windows):
        real = jnp.zeros((72, 72), jnp.int32)
        for r in range(6):
            spot = lax.rem(lat * (6 * windows) + (6 * rw + r + 3), rows) * level_rows
            here = valid[spot]
            for more in range(1, level_rows):
                here = jnp.maximum(here, valid[spot + more])
            real = jnp.where(key_row == r, here, real)
        good = (real == 1) | (key == query)
        if rw == windows - 1:
            good = good & (apart * at_end == 0)
        for level in range(2):
            for h in range(heads):
                at = (rw * heads + h) * 144 + level * 72
                bias[level, rw, :, 72 * h : 72 * (h + 1)] = jnp.where(
                    good, raw[at : at + 72, :][:, :72], BLOCKED
                )

    codes = surface[...].astype(F32).astype(BF16)
    tokens = kinds.shape[0]
    line = row[...] + lat * (6 * windows)
    line = jnp.where(line >= rows, line - rows, line) * level_rows
    spot = col[...] + lon * (12 * (tokens // 72 // windows))
    spot = jnp.where(spot >= columns, spot - columns, spot) * level_rows
    lines = mm(one_hot(line, surface.shape[0]), codes)
    lanes = lax.broadcasted_iota(jnp.int32, lines.shape, 1)
    code = jnp.sum(jnp.where(lanes == spot, lines, 0.0), axis=1, keepdims=True).astype(jnp.int32)
    lanes = lax.broadcasted_iota(jnp.int32, (tokens, 128), 1)
    kinds[...] = jnp.where((lanes == code) | (lanes == code + 3) | (lanes == code + 6), 1.0, 0.0)

    t = types[...]
    high = round16(t)
    middle = round16(t - high)
    lanes = lax.broadcasted_iota(jnp.int32, t.shape, 1)
    split = jnp.where(lanes < 3, high, jnp.where(lanes < 6, middle, t - high - middle))
    typed[...] = jnp.concatenate(
        [jnp.broadcast_to(split[h : h + 1], (72, 128)) for h in range(heads)], axis=0
    ).astype(BF16)


def fine_forward_kernel(
    take, sel, tokens, ra, rb, rc, gain, project, combine, bias, kinds, types,
    output, sa, sb, sc, kept_x, kept_p, kept_o,
    q_s, k_s, v_s, o_s,
):
    n = take.shape[0]
    width = tokens.shape[1]
    total = n + ra.shape[1] + rb.shape[1] + rc.shape[1]
    hot = one_hot(take[...], total)
    rolled = []
    for level in range(2):
        o = 1 - level
        source = jnp.concatenate([tokens[o * n : (o + 1) * n, :], ra[o], rb[o], rc[o]], axis=0)
        rolled.append(mm(hot, source))
    x = jnp.concatenate(rolled, axis=0)
    kept_x[...] = x.astype(BF16)
    (centred,), inverse = moments([x])
    u = (centred * inverse * gain[...]).astype(BF16)
    for i, scratch in enumerate((q_s, k_s, v_s)):
        scratch[...] = round16(mm(u, project[:, i * width : (i + 1) * width]))
    masks = head_masks(width)
    windows = n // 72
    across = windows // bias.shape[1]
    types16 = types[...]

    def window(w, carry):
        kinds16 = kinds[pl.ds(pl.multiple_of(w * 72, 8), 72), :].astype(BF16)
        for level in range(2):
            b = level * windows + w
            rows = pl.ds(pl.multiple_of(b * 72, 8), 72)
            qbig = spread_heads(q_s[rows, :], masks)
            p = weights_of(k_s[rows, :].astype(BF16), qbig, kinds16, types16, bias[level, w // across])
            kept_p[b] = p
            o_s[rows, :] = fold_heads(mm(p, v_s[rows, :].astype(BF16), TN), masks)
        return carry

    lax.fori_loop(0, windows, window, 0)
    o16 = o_s[...].astype(BF16)
    kept_o[...] = o16
    out = (x + mm(o16, combine[...])).astype(BF16)
    output[...] = out
    for level in range(2):
        send_out(sel[...], out[level * n : (level + 1) * n], (sa, sb, sc), level)


def coarse_kernel(
    take, ctake, csel, fsel, fine, ra, rb, rc, cot, da, db, dc,
    merge_gain, merge_weight, gain, project, combine, bias, kinds, types,
    output, oa, ob, oc, delta_fine, sa, sb, sc, gradients,
    q_s, k_s, v_s, o_s, do_s, dq_s, dk_s, dv_s, p_s,
):
    n = take.shape[0]
    quarter = n // 4
    thin = fine.shape[1]
    width = combine.shape[0]
    total = n + ra.shape[1] + rb.shape[1] + rc.shape[1]
    hot = one_hot(take[...], total)
    ctotal = quarter + da.shape[1] + db.shape[1] + dc.shape[1]
    chot = one_hot(ctake[...], ctotal)
    levels, cot_levels = [], []
    for level in range(2):
        source = jnp.concatenate([fine[level * n : (level + 1) * n, :], ra[level], rb[level], rc[level]], axis=0)
        levels.append(mm(hot, source))
        o = 1 - level
        source = jnp.concatenate([cot[o * quarter : (o + 1) * quarter, :], da[o], db[o], dc[o]], axis=0)
        cot_levels.append(mm(chot, source))
    cells = [
        jnp.concatenate([x[s * quarter : (s + 1) * quarter] for x in levels], axis=0) for s in range(4)
    ]
    d = jnp.concatenate(cot_levels, axis=0)
    d16 = d.astype(BF16)
    merge_gains = [merge_gain[s : s + 1, :] for s in range(4)]
    m_centred, m_inverse = moments(cells)
    merged = [(c * m_inverse * g).astype(BF16) for c, g in zip(m_centred, merge_gains)]
    weight = [merge_weight[s * thin : (s + 1) * thin, :] for s in range(4)]
    entered = sum(mm(a, w) for a, w in zip(merged, weight))
    x = round16(entered)
    (centred,), inverse = moments([x])
    u = (centred * inverse * gain[...]).astype(BF16)
    wq, wk, wv = (project[:, i * width : (i + 1) * width] for i in range(3))
    q_s[...] = round16(mm(u, wq))
    k_s[...] = round16(mm(u, wk))
    v_s[...] = round16(mm(u, wv))
    do_s[...] = round16(mm(d16, combine[...], NT))
    masks = head_masks(width)
    windows = quarter // 72
    types16 = types[...]

    def window(w, carry):
        kinds16 = kinds[pl.ds(pl.multiple_of(w * 72, 8), 72), :].astype(BF16)
        for level in range(2):
            rows = pl.ds(pl.multiple_of((level * windows + w) * 72, 8), 72)
            q, k, v = q_s[rows, :], k_s[rows, :], v_s[rows, :]
            p = weights_of(k.astype(BF16), spread_heads(q, masks), kinds16, types16, bias[level, 0])
            o_s[rows, :] = fold_heads(mm(p, v.astype(BF16), TN), masks)
            dq, dk, dv = attention_back(q, k, v, p, do_s[rows, :], masks)
            dq_s[rows, :] = dq
            dk_s[rows, :] = dk
            dv_s[rows, :] = dv
        return carry

    lax.fori_loop(0, windows, window, 0)
    o16 = o_s[...].astype(BF16)
    out = (x + mm(o16, combine[...])).astype(BF16)
    output[...] = out
    for level in range(2):
        send_out(csel[...], out[level * quarter : (level + 1) * quarter], (oa, ob, oc), level)
    dq16, dk16, dv16 = dq_s[...].astype(BF16), dk_s[...].astype(BF16), dv_s[...].astype(BF16)
    delta_rolled = round16(mm(dq16, wq, NT) + mm(dk16, wk, NT) + mm(dv16, wv, NT))
    (dx,) = norm_back([centred], inverse, [gain[...]], [delta_rolled])
    delta = (d + round16(dx)).astype(BF16)
    deltas = [round16(mm(delta, w, NT)) for w in weight]
    back = norm_back(m_centred, m_inverse, merge_gains, deltas)
    back = [b.astype(BF16) for b in back]
    for level in range(2):
        own = jnp.concatenate([b[level * quarter : (level + 1) * quarter] for b in back], axis=0)
        delta_fine[level * n : (level + 1) * n, :] = own
        send_out(fsel[...], own, (sa, sb, sc), level)
    sums = [jnp.concatenate([mm(m, delta, TN) for m in merged], axis=0)]
    sums += [mm(left, right, TN) for left, right in ((u, dq16), (u, dk16), (u, dv16), (o16, d16))]
    at = 0
    for block in sums:
        for j in range(width // 128):
            gradients[at : at + block.shape[0], :] = block[:, j * 128 : (j + 1) * 128].astype(BF16)
            at += block.shape[0]


def fine_backward_kernel(
    take, sel, own, ra, rb, rc, kept_x, kept_p, kept_o,
    gain, project, combine,
    output, sa, sb, sc, gradients,
    q_s, k_s, v_s, do_s, dq_s, dk_s, dv_s,
):
    n = take.shape[0]
    width = kept_x.shape[1]
    total = n + ra.shape[1] + rb.shape[1] + rc.shape[1]
    hot = one_hot(take[...], total)
    d = jnp.concatenate(
        [
            mm(hot, jnp.concatenate([own[l * n : (l + 1) * n, :], ra[l], rb[l], rc[l]], axis=0))
            for l in range(2)
        ],
        axis=0,
    )
    d16 = d.astype(BF16)
    do_s[...] = round16(mm(d16, combine[...], NT))
    (centred,), inverse = moments([kept_x[...].astype(F32)])
    u = (centred * inverse * gain[...]).astype(BF16)
    for i, scratch in enumerate((q_s, k_s, v_s)):
        scratch[...] = round16(mm(u, project[:, i * width : (i + 1) * width]))
    masks = head_masks(width)
    windows = n // 72

    def window(w, carry):
        for level in range(2):
            b = level * windows + w
            rows = pl.ds(pl.multiple_of(b * 72, 8), 72)
            dq, dk, dv = attention_back(
                q_s[rows, :], k_s[rows, :], v_s[rows, :], kept_p[b], do_s[rows, :], masks
            )
            dq_s[rows, :] = dq
            dk_s[rows, :] = dk
            dv_s[rows, :] = dv
        return carry

    lax.fori_loop(0, windows, window, 0)
    parts = [dq_s[...].astype(BF16), dk_s[...].astype(BF16), dv_s[...].astype(BF16)]
    delta_rolled = round16(
        sum(mm(a, project[:, i * width : (i + 1) * width], NT) for i, a in enumerate(parts))
    )
    (dx,) = norm_back([centred], inverse, [gain[...]], [delta_rolled])
    out = (d + round16(dx)).astype(BF16)
    output[...] = out
    for level in range(2):
        send_out(sel[...], out[level * n : (level + 1) * n], (sa, sb, sc), level)
    pieces = [mm(u, a, TN) for a in parts] + [mm(kept_o[...], d16, TN)]
    pieces = jnp.concatenate(pieces, axis=1).astype(BF16)
    for j in range(pieces.shape[1] // 128):
        gradients[j * width : (j + 1) * width, :] = pieces[:, j * 128 : (j + 1) * 128]


def restore_kernel(take, own, ra, rb, rc, output):
    n = take.shape[0]
    hot = one_hot(take[...], n + ra.shape[1] + rb.shape[1] + rc.shape[1])
    for level in range(2):
        o = 1 - level
        source = jnp.concatenate([own[o * n : (o + 1) * n, :], ra[o], rb[o], rc[o]], axis=0)
        output[level * n : (level + 1) * n, :] = mm(hot, source).astype(BF16)


VMEM = pl.BlockSpec(memory_space=pltpu.VMEM)
SMEM = pl.BlockSpec(memory_space=pltpu.SMEM)


def call(kernel, name, outs, scratch, args, smem=0, flops=10**9, limit=20):
    return pl.pallas_call(
        kernel,
        name=name,
        out_shape=[jax.ShapeDtypeStruct(s, d) for s, d in outs],
        in_specs=[SMEM] * smem + [VMEM] * (len(args) - smem),
        out_specs=[VMEM] * len(outs),
        scratch_shapes=[pltpu.VMEM(s, d) for s, d in scratch],
        cost_estimate=pl.CostEstimate(flops=flops, bytes_accessed=4 << 20, transcendentals=0),
        compiler_params=pltpu.CompilerParams(vmem_limit_bytes=limit << 20),
    )(*args)


def move(value, lat_step, lon_step):
    lons, lats = lax.axis_size("lon"), lax.axis_size("lat")
    if lat_step == 0:
        return lax.ppermute(value, "lon", [(s, (s + lon_step) % lons) for s in range(lons)])
    if lon_step == 0:
        return lax.ppermute(value, "lat", [(s, (s + lat_step) % lats) for s in range(lats)])
    pairs = [
        (a * lats + b, ((a + lon_step) % lons) * lats + (b + lat_step) % lats)
        for a in range(lons)
        for b in range(lats)
    ]
    return lax.ppermute(value, ("lon", "lat"), pairs)


def exchange(parts, step):
    a, b, c = parts
    return [move(a, step, 0), move(b, 0, step), move(c, step, step)]


def summed(blocks):
    count = lax.axis_size("lon") * lax.axis_size("lat")
    block = jnp.concatenate(blocks, axis=0)
    chunk = pad16(-(-block.shape[0] // count))
    block = jnp.pad(block, ((0, count * chunk - block.shape[0]), (0, 0))).reshape(count, chunk, 128)
    terms = lax.all_to_all(block, ("lon", "lat"), 0, 0, tiled=True)
    total = jnp.sum(terms.astype(F32), axis=0).astype(BF16)
    total = jnp.broadcast_to(total[None], terms.shape)
    return lax.all_to_all(total, ("lon", "lat"), 0, 0, tiled=True).reshape(count * chunk, 128)


def finish_kernel(fine_scale, coarse_scale, sums, project1, combine1, merge, project2, combine2):
    thin, width = combine1.shape[0], combine2.shape[0]
    at = 0

    def take(rows):
        nonlocal at
        at += rows
        return sums[at - rows : at, :].astype(F32)

    for j in range(width // 128):
        merge[:, j * 128 : (j + 1) * 128] = take(merge.shape[0]) * coarse_scale
    for i in range(3):
        for j in range(width // 128):
            lane = i * width + j * 128
            project2[:, lane : lane + 128] = take(width) * coarse_scale
    for j in range(width // 128):
        combine2[:, j * 128 : (j + 1) * 128] = take(width) * coarse_scale
    fine = jnp.concatenate([take(thin) for _ in range(4 * thin // 128)], axis=1) * fine_scale
    project1[...] = fine[:, : 3 * thin]
    combine1[...] = fine[:, 3 * thin :]


def local(
    fine_tokens, cotangent, fine_gain, fine_project, fine_combine, fine_table, fine_types,
    merge_gain, merge_weight, coarse_gain, coarse_project, coarse_combine, coarse_table,
    coarse_types, surface_type, latitude_valid, bias_index,
):
    _, rows1, cols1, d1 = fine_tokens.shape
    _, rows2, cols2, d2 = cotangent.shape
    n1, n2 = rows1 * cols1, rows2 * cols2
    h1, h2 = d1 // HEAD, d2 // HEAD
    lons, lats = lax.axis_size("lon"), lax.axis_size("lat")
    enter = Shift(rows1, cols1, 3, 6, raster(cols1), windowed(cols1), True)
    middle = Shift(rows1, cols1, 3, 6, windowed(cols1), merging(cols1), True)
    return_middle = Shift(rows1, cols1, 3, 6, merging(cols1), windowed(cols1), False)
    leave = Shift(rows1, cols1, 3, 6, windowed(cols1), raster(cols1), False)
    centre = Shift(rows2, cols2, 3, 6, raster(cols2), windowed(cols2), True)
    cleave = Shift(rows2, cols2, 3, 6, windowed(cols2), raster(cols2), False)
    fine_halo = [((2, s, d1), BF16) for s in enter.sizes]
    coarse_halo = [((2, s, d2), BF16) for s in centre.sizes]
    tokens = fine_tokens.reshape(2 * n1, d1)
    cot = cotangent.reshape(2 * n2, d2)

    halos = call(
        prepare_kernel, "prepare", fine_halo + coarse_halo, [],
        [enter.send, centre.send, tokens, cot], flops=10**9,
    )
    token_halo = exchange(halos[:3], -1)
    cot_halo = exchange(halos[3:], -1)

    place = jnp.stack([lax.axis_index("lat"), lax.axis_index("lon"), jnp.int32(lats)]).astype(jnp.int32)
    pairs = jnp.concatenate([bias_index[:72, :72].T, bias_index[72:, 72:].T], axis=0)
    pairs = jnp.pad(pairs, ((0, 0), (0, 56)))[:, None]

    def level_bias(name, where, table, types, level_rows, rows, cols):
        lists = jnp.swapaxes(table[0], 1, 2).reshape(-1, table.shape[2])
        lists = jnp.pad(lists, ((0, 0), (0, -lists.shape[1] % 128)))
        t = types.T
        t = jnp.pad(jnp.concatenate([t, t, t], axis=1), ((0, 0), (0, 128 - 9)))
        order = windowed(cols)
        r, c = np.zeros((rows * cols, 1), np.int32), np.zeros((rows * cols, 1), np.int32)
        for a in range(rows):
            for b in range(cols):
                r[order(a, b), 0], c[order(a, b), 0] = a + 3, b + 6
        heads = types.shape[1]
        count = pad8(lists.shape[0])
        return call(
            partial(bias_kernel, level_rows), name,
            [((2, rows // 6, 72, 72 * heads), F32), ((rows * cols, 128), F32), ((72 * heads, 128), BF16)],
            [((count * 144, 128), F32), ((count * lists.shape[1] // 128, 256), BF16)],
            [where, latitude_valid, pairs, lists, surface_type, t, r, c],
            smem=2, flops=4 * 10**9,
        )

    fbias, fkinds, ftyped = level_bias("fine_bias", place, fine_table, fine_types, 1, rows1, cols1)

    token16 = lambda width: ((2 * n1, width), BF16)
    blocks1 = 2 * n1 // 72
    forward = call(
        fine_forward_kernel, "fine_forward",
        [token16(d1)] + fine_halo + [token16(d1), ((blocks1, 72, 72 * h1), BF16), token16(d1)],
        [((2 * n1, d1), F32)] * 4,
        [enter.take, middle.send, tokens, *token_halo, fine_gain[None], fine_project, fine_combine,
         fbias, fkinds, ftyped],
        flops=4 * 10**9,
    )
    fine_output, kept = forward[0], forward[4:]
    halo = exchange(forward[1:4], -1)
    later, _ = lax.optimization_barrier((place, forward[1]))
    cbias, ckinds, ctyped = level_bias("coarse_bias", later, coarse_table, coarse_types, 2, rows2, cols2)

    rows = (4 * d1 + 4 * d2) * d2 // 128
    coarse = call(
        coarse_kernel, "coarse",
        [((2 * n2, d2), BF16)] + coarse_halo + [token16(d1)] + fine_halo + [((rows, 128), BF16)],
        [((2 * n2, d2), F32)] * 8 + [((8, 128), F32)],
        [middle.take, centre.take, cleave.send, return_middle.send, fine_output, *halo, cot, *cot_halo,
         merge_gain.reshape(4, d1), merge_weight, coarse_gain[None], coarse_project, coarse_combine,
         cbias, ckinds, ctyped],
        flops=6 * 10**9,
    )
    delta_halo = exchange(coarse[5:8], 1)
    out_halo = exchange(coarse[1:4], 1)

    backward = call(
        fine_backward_kernel, "fine_backward",
        [token16(d1)] + fine_halo + [((4 * d1 * d1 // 128, 128), BF16)],
        [((2 * n1, d1), F32)] * 7,
        [return_middle.take, leave.send, coarse[4], *delta_halo, *kept,
         fine_gain[None], fine_project, fine_combine],
        flops=6 * 10**9,
    )
    last_halo = exchange(backward[1:4], 1)

    (coarse_out,) = call(
        restore_kernel, "restore_coarse", [((2 * n2, d2), BF16)], [],
        [cleave.take, coarse[0], *out_halo],
    )
    (gradient,) = call(
        restore_kernel, "restore_fine", [token16(d1)], [],
        [leave.take, backward[0], *last_halo],
    )

    count = 2 * n1 * lons * lats
    fine_scale, coarse_scale = 1.0 / math.sqrt(count), 1.0 / math.sqrt(count // 4)
    sums = summed([coarse[8], backward[4]])
    gradients = call(
        partial(finish_kernel, fine_scale, coarse_scale), "finish",
        [((d1, 3 * d1), F32), ((d1, d1), F32), ((4 * d1, d2), F32), ((d2, 3 * d2), F32), ((d2, d2), F32)],
        [], [sums],
    )
    return (coarse_out.reshape(cotangent.shape), gradient.reshape(fine_tokens.shape), *gradients)


def solution(mesh):
    split = P(None, "lat", "lon", None)
    table = P(None, "lat", None, None)
    in_specs = (
        split, split, P(), P(), P(), table, P(), P(), P(), P(), P(), P(), table, P(), P(), P(), P(),
    )
    out_specs = (split, split, P(), P(), P(), P(), P())
    return jax.shard_map(local, mesh=mesh, in_specs=in_specs, out_specs=out_specs, check_vma=False)
```

time: 791 us -> 167 us (0.21); the launches traced: 781 us -> 167 us
  local copies, waits for them, and re-layouts: 434 us -> 9.19 us
  waiting for transfers between devices: 171 us -> 38.4 us
  matrix products: 75.8 us -> 0 us
  other arithmetic: 59.7 us -> 0.74 us
  Pallas kernels: 0 us -> 54.5 us
  blocking collectives: 0 us -> 33.9 us
  between operations: 15.7 us -> 1.18 us
    gather x10 -> x0, local copies, waits for them, and re-layouts: 253 us -> none  [one_row(): positional = jnp.take(table_rows, bias_index.reshape(-1), axis=1)]
    psum x1 -> x0, waiting for transfers between devices: 134 us -> none  [local(): lax.psum((fine_project_sum, fine_combine_sum, merge_sum, coarse_project_s...]
    pallas_call x0 -> x9, Pallas kernels: none -> 54.5 us  [call(): pl.pallas_call(kernel, name=name, out_shape=[jax.ShapeDtypeStruct(s, d) f...]
    dot_general x30 -> x0, matrix products: 49.8 us -> none  [the longest x9 17.5 us: one_row(): jnp.einsum('lchqk,lchkd->lchqd', weights, value_block, preferred_element_...]
    reshape x20 -> x2, local copies, waits for them, and re-layouts: 48.1 us -> 0.1 us  [the longest x1 0.08 us: local(): merge_gain.reshape(4, d1)]
    all_to_all x0 -> x1, blocking collectives: none -> 33.9 us  [summed(): terms = lax.all_to_all(block, ('lon', 'lat'), 0, 0, tiled=True)]
    transpose x14 -> x1, local copies, waits for them, and re-layouts: 29.7 us -> 0.03 us  [level_bias(): lists = jnp.swapaxes(table[0], 1, 2).reshape(-1, table.shape[2])]
    sub x5 -> x0, matrix products: 26 us -> none  [one_row(): weights = jnp.exp(scores - row_top)]
  transfers between devices with their start and end apart: 17 -> 19, of which waited for: 10 -> 5; matrix products, arithmetic and copies ran while one was open for 51% -> 1% of each run, Pallas kernels for 0% -> 18%
where the time goes in v1:
time: 167 us
  Pallas kernels  54.5 us (33%)
  waiting for transfers between devices  38.4 us (23%)
  blocking collectives  33.9 us (20%)
  starting transfers between devices  28.8 us (17%)
  local copies, waits for them, and re-layouts  9.19 us (6%)
    pallas_call x9, Pallas kernels, call(): pl.pallas_call(kernel, name=name, out_shape=[jax.ShapeDtypeStruct(s, d) f...  54.5 us
    all_to_all x1, blocking collectives, summed(): terms = lax.all_to_all(block, ('lon', 'lat'), 0, 0, tiled=True)  33.9 us
    ppermute x6, waiting for transfers between devices, move(): lax.ppermute(value, 'lon', [(s, (s + lon_step) % lons) for s in range(lon...  21.3 us
    ppermute x6, waiting for transfers between devices, move(): return lax.ppermute(value, ('lon', 'lat'), pairs)  17.1 us
    ppermute x6, starting transfers between devices, move(): return lax.ppermute(value, ('lon', 'lat'), pairs)  12.8 us
    ppermute x6, starting transfers between devices, move(): lax.ppermute(value, 'lat', [(s, (s + lat_step) % lats) for s in range(lat...  7.01 us
    unnamed x76, local copies, waits for them, and re-layouts  6.12 us
    all_to_all x1, starting transfers between devices, summed(): lax.all_to_all(total, ('lon', 'lat'), 0, 0, tiled=True)  4.8 us
  transfers between devices with their start and end apart: 19, of which 5 were waited for; matrix products, arithmetic and copies ran while one was open for 1% of the time, Pallas kernels for 18%

profile of v1, /device:TPU:0, one launch (start us, length us, event | category | flops | bytes accessed | tf_op | source)
XLA Modules:
  0.0 166.7 jit_solution(5898216152515068939)
XLA Ops:
  0.6 0.0 copy-start.1
  0.7 1.1 copy-done.1
  1.7 0.9 copy-done.7
  2.7 0.9 copy-done.21
  3.6 0.8 copy-done.27
  4.4 0.0 copy-start.16
  4.4 0.0 copy-start.17
  4.4 0.5 prepare.1
  4.9 8.3 %collective-permute-start.2 = (bf16[2,32,192]{2,1,0:T(8,128)(2,1)S(1)}, bf16[2,32,192]{2,1,0:T(8,128)(2,1)S(1)}, u32[]{:S(2)}, u32[]{:S(2)}) collective-permute-start(bf16[2,32,192]{2,1,0:T(8,128)(2,1)S(1)} %get-tuple-element.48), channel_id=1, source_target_pairs={{0,127},{1,120},{2,121},{3,122},{4,123},{5,124},{6,125},{7,126},{8... | collective-permute-start | bytes 73736 | tf_op jit(solution)/shard_map/ppermute | solution.py:474
  13.2 1.7 %collective-permute-start.7 = (bf16[2,32,384]{2,1,0:T(8,128)(2,1)S(1)}, bf16[2,32,384]{2,1,0:T(8,128)(2,1)S(1)}, u32[]{:S(2)}, u32[]{:S(2)}) collective-permute-start(bf16[2,32,384]{2,1,0:T(8,128)(2,1)S(1)} %get-tuple-element.57), channel_id=1, source_target_pairs={{0,120},{8,0},{16,8},{24,16},{32,24},{40,32},{48,40},{56,48},{64,5... | collective-permute-start | bytes 147464 | tf_op jit(solution)/shard_map/ppermute | solution.py:466
  14.9 0.9 collective-permute-start.1
  15.9 0.1 copy.48
  16.0 0.1 select_maximum_fusion.2.types
  16.1 0.1 copy.50
  16.2 0.1 fusion.3
  16.3 0.1 copy.51
  16.3 0.1 copy.52
  16.6 0.1 pad_add_fusion.1.place
  16.7 0.0 copy-start.35
  16.7 0.0 copy-start.2
  16.7 0.0 copy-start.6
  16.7 0.0 copy-start.15
  16.7 0.0 copy-start.20
  16.8 8.6 %fine_bias.1 = (f32[2,2,72,432]{3,2,1,0:T(8,128)S(1)}, f32[576,128]{1,0:T(8,128)S(1)}, bf16[432,128]{1,0:T(8,128)(2,1)S(1)}) custom-call(s32[3]{0:T(128)S(1)} %pad_add_fusion.1.place, s32[96]{0:T(128)S(1)} %copy-done.11, s32[144,1,128]{2,1,0:T(1,128)S(1)} %bitcast.24, f32[12,3328]{1,0:T(8,128)S(1)} %pad.24.table, s32[96,768]{1,0:T(8,128)S(1)} %copy-done.4, ...), custom_call_target="tpu_custom_call" | custom-call | flops 4000000000 | bytes 4194304 | tf_op jit(solution)/shard_map/fine_bias/pallas_call | solution.py:451
  25.4 0.0 copy-start.28
  25.4 0.8 copy-done.28
  26.2 0.1 select_maximum_fusion.types
  26.3 0.1 reshape.45.merge_gain
  26.4 0.9 copy.54
  27.4 0.5 collective-permute-start.6
  28.0 0.0 copy-start.29
  28.0 1.1 copy-done.29
  29.0 9.3 %fine_forward.1 = (bf16[1152,192]{1,0:T(8,128)(2,1)S(1)}, bf16[2,128,192]{2,1,0:T(8,128)(2,1)S(1)}, bf16[2,64,192]{2,1,0:T(8,128)(2,1)S(1)}, bf16[2,32,192]{2,1,...) custom-call(s32[576,1]{1,0:T(8,128)S(1)} %copy-done.15, ...), custom_call_target="tpu_custom_call" | custom-call | flops 4000000000 | bytes 4194304 | tf_op jit(solution)/shard_map/fine_forward/pallas_call | solution.py:451
  38.4 3.0 %collective-permute-start.3 = (bf16[2,128,192]{2,1,0:T(8,128)(2,1)S(1)}, bf16[2,128,192]{2,1,0:T(8,128)(2,1)S(1)}, u32[]{:S(2)}, u32[]{:S(2)}) collective-permute-start(bf16[2,128,192]{2,1,0:T(8,128)(2,1)S(1)} %get-tuple-element.53), channel_id=1, source_target_pairs={{0,7},{1,0},{2,1},{3,2},{4,3},{5,4},{6,5},{7,6},{8,15},{9,8},{10,9... | collective-permute-start | bytes 294920 | tf_op jit(solution)/shard_map/ppermute | solution.py:468
  41.4 0.0 copy-start.14
  41.5 0.0 copy-start.19
  41.5 0.0 copy-start.23
  41.5 0.0 copy-start.26
  41.5 1.5 collective-permute-start.4
  43.0 8.4 %coarse_bias.1 = (f32[2,1,72,864]{3,2,1,0:T(8,128)S(1)}, f32[144,128]{1,0:T(8,128)S(1)}, bf16[864,128]{1,0:T(8,128)(2,1)S(1)}) custom-call(s32[3]{0:T(128)S(1)} %pad_add_fusion.1.place, s32[96]{0:T(128)S(1)} %copy-done.11, s32[144,1,128]{2,1,0:T(1,128)S(1)} %bitcast.25, f32[12,3328]{1,0:T(8,128)S(1)} %pad.26.table, s32[96,768]{1,0:T(8,128)S(1)} %copy-done.4, ...), custom_call_target="tpu_custom_call" | custom-call | flops 4000000000 | bytes 4194304 | tf_op jit(solution)/shard_map/coarse_bias/pallas_call | solution.py:451
  51.5 0.0 copy-start.13
  51.5 0.0 copy-start.18
  51.5 11.4 %coarse.1 = (bf16[288,384]{1,0:T(8,128)(2,1)S(1)}, bf16[2,64,384]{2,1,0:T(8,128)(2,1)S(1)}, bf16[2,32,384]{2,1,0:T(8,128)(2,1)S(1)}, bf16[2,32,384]{2,1,0:T(8,12...) custom-call(s32[576,1]{1,0:T(8,128)S(1)} %copy-done.14, ...), custom_call_target="tpu_custom_call" | custom-call | flops 6000000000 | bytes 4194304 | tf_op jit(solution)/shard_map/coarse/pallas_call | solution.py:451
  63.0 1.3 collective-permute-start.12
  64.2 1.1 collective-permute-start.14
  65.3 7.9 %collective-permute-done.14.rc = bf16[2,32,192]{2,1,0:T(8,128)(2,1)S(1)} collective-permute-done((bf16[2,32,192]{2,1,0:T(8,128)(2,1)S(1)}, bf16[2,32,192]{2,1,0:T(8,128)(2,1)S(1)}, u32[]{:S(2)}, u32[]{:S(2)}) %collective-permute-start.14) | collective-permute-done | bytes 24608 | tf_op jit(solution)/shard_map/ppermute | solution.py:474
  73.3 11.3 %fine_backward.1 = (bf16[1152,192]{1,0:T(8,128)(2,1)S(1)}, bf16[2,128,192]{2,1,0:T(8,128)(2,1)S(1)}, bf16[2,64,192]{2,1,0:T(8,128)(2,1)S(1)}, bf16[2,32,192]{2,1,0:T(8,128)(2,1)S(1)}, bf16[1152,128]{1,0:T(8,128)(2,1)S(1)}) custom-call(s32[576,1]{1,0:T(8,128)S(1)} %copy-done.13, s32[224,1]{1,0:T(8,128)S(1)} %copy-done.18, ...), custom_call_target="tpu_custom_call" | custom-call | flops 6000000000 | bytes 4194304 | tf_op jit(solution)/shard_map/fine_backward/pallas_call | solution.py:451
  84.6 0.1 fusion.2
  84.7 33.9 %all_to_all.10 = bf16[128,64,128]{2,1,0:T(8,128)(2,1)S(1)} all-to-all(bf16[128,64,128]{2,1,0:T(8,128)(2,1)S(1)} %bitcast.32), channel_id=1, replica_groups=mesh['lon'=16,'lat'=8] {'lon','lat'}, dimensions={0} | all-to-all | bytes 4194304 | tf_op jit(solution)/shard_map/all_to_all | solution.py:487
  118.6 0.4 reduce_sum.12
  118.9 1.9 %broadcast_in_dim.19 = bf16[128,64,128]{2,1,0:T(8,128)(2,1)} broadcast(bf16[64,128]{1,0:T(8,128)(2,1)S(1)} %reduce_sum.12), dimensions={1,2} | broadcast | bytes 2113536 | tf_op jit(solution)/shard_map/broadcast_in_dim | solution.py:489
  120.8 4.8 %all-to-all-start.1 = ((bf16[128,64,128]{2,1,0:T(8,128)(2,1)}), bf16[128,64,128]{2,1,0:T(8,128)(2,1)S(1)}, u32[]{:S(2)}, u32[]{:S(2)}) async-start(bf16[128,64,128]{2,1,0:T(8,128)(2,1)} %broadcast_in_dim.19), calls=%async_computation.1 | async-start | bytes 4194304 | tf_op jit(solution)/shard_map/all_to_all | solution.py:490
  125.6 0.0 copy-start.12
  125.6 1.0 collective-permute-start.9
  126.7 2.8 %collective-permute-start.11 = (bf16[2,32,384]{2,1,0:T(8,128)(2,1)S(1)}, bf16[2,32,384]{2,1,0:T(8,128)(2,1)S(1)}, u32[]{:S(2)}, u32[]{:S(2)}) collective-permute-start(bf16[2,32,384]{2,1,0:T(8,128)(2,1)S(1)} %get-tuple-element.66), channel_id=1, source_target_pairs={{0,9},{1,10},{2,11},{3,12},{4,13},{5,14},{6,15},{7,8},{8,17},{9,18... | collective-permute-start | bytes 147464 | tf_op jit(solution)/shard_map/ppermute | solution.py:474
  129.5 1.2 collective-permute-start.15
  130.6 0.6 collective-permute-start.17
  131.3 20.4 %collective-permute-done.10.rb = bf16[2,32,384]{2,1,0:T(8,128)(2,1)S(1)} collective-permute-done((bf16[2,32,384]{2,1,0:T(8,128)(2,1)S(1)}, bf16[2,32,384]{2,1,0:T(8,128)(2,1)S(1)}, u32[]{:S(2)}, u32[]{:S(2)}) %collective-permute-start.10) | collective-permute-done | bytes 49184 | tf_op jit(solution)/shard_map/ppermute | solution.py:466
  151.7 6.7 %collective-permute-done.11.rc = bf16[2,32,384]{2,1,0:T(8,128)(2,1)S(1)} collective-permute-done((bf16[2,32,384]{2,1,0:T(8,128)(2,1)S(1)}, bf16[2,32,384]{2,1,0:T(8,128)(2,1)S(1)}, u32[]{:S(2)}, u32[]{:S(2)}) %collective-permute-start.11) | collective-permute-done | bytes 49184 | tf_op jit(solution)/shard_map/ppermute | solution.py:474
  158.4 1.1 restore_coarse.1
  159.5 2.4 %collective-permute-done.17.rc = bf16[2,32,192]{2,1,0:T(8,128)(2,1)S(1)} collective-permute-done((bf16[2,32,192]{2,1,0:T(8,128)(2,1)S(1)}, bf16[2,32,192]{2,1,0:T(8,128)(2,1)S(1)}, u32[]{:S(2)}, u32[]{:S(2)}) %collective-permute-start.17) | collective-permute-done | bytes 24608 | tf_op jit(solution)/shard_map/ppermute | solution.py:474
  161.9 0.9 collective-permute-done.16.rb
  162.8 1.7 %restore_fine.1 = bf16[1152,192]{1,0:T(8,128)(2,1)} custom-call(s32[576,1]{1,0:T(8,128)S(1)} %copy-done.12, bf16[1152,192]{1,0:T(8,128)(2,1)S(1)} %get-tuple-element.74.own, bf16[2,128,192]{2,1,0:T(8,128)(2,1)S(1)} %collective-permute-done.15.ra, bf16[2,64,192]{2,1,0:T(8,128)(2,1)S(1)} %collective-permute-done.16.rb, ...), custom_call_target="tpu_custom_call" | custom-call | flops 1000000000 | bytes 4194304 | tf_op jit(solution)/shard_map/restore_fine/pallas_call | solution.py:451
  164.6 2.1 %finish.1 = (f32[192,576]{1,0:T(8,128)}, f32[192,192]{1,0:T(8,128)}, f32[768,384]{1,0:T(8,128)}, f32[384,1152]{1,0:T(8,128)}, f32[384,384]{1,0:T(8,128)}) custom-call(bf16[8192,128]{1,0:T(8,128)(2,1)S(1)} %bitcast.23), custom_call_target="tpu_custom_call" | custom-call | flops 1000000000 | bytes 4194304 | tf_op jit(solution)/shard_map/finish/pallas_call | solution.py:451
  (76 shorter events, 0.3 us)
Async XLA Ops:
  0.6 15.3 %copy-start.33 = (f32[3,6]{1,0:T(4,128)S(1)}, f32[3,6]{1,0:T(4,128)}, u32[]{:S(2)}) copy-start(f32[3,6]{1,0:T(4,128)} %param.39) | copy-start | bytes 220
  0.6 1.1 copy-start.1
  1.7 0.9 copy-start.7
  2.7 0.9 copy-start.21
  3.6 0.8 copy-start.27
  4.4 11.7 %copy-start.34 = (f32[3,12]{1,0:T(4,128)S(1)}, f32[3,12]{1,0:T(4,128)}, u32[]{:S(2)}) copy-start(f32[3,12]{1,0:T(4,128)} %param.46) | copy-start | bytes 436
  4.4 11.8 %copy-start.31 = (s32[144,144]{1,0:T(8,128)S(1)}, s32[144,144]{1,0:T(8,128)}, u32[]{:S(2)}) copy-start(s32[144,144]{1,0:T(8,128)} %param.49) | copy-start | bytes 248836
  4.4 12.0 %copy-start.30 = (f32[1,2,3312,6]{2,1,3,0:T(2,128)S(1)}, f32[1,2,3312,6]{2,1,3,0:T(2,128)}, u32[]{:S(2)}) copy-start(f32[1,2,3312,6]{2,1,3,0:T(2,128)} %param.38) | copy-start | bytes 476932
  4.4 12.2 %copy-start.4 = (s32[96,768]{1,0:T(8,128)S(1)}, s32[96,768]{1,0:T(8,128)}, u32[]{:S(2)}) copy-start(s32[96,768]{1,0:T(8,128)} %surface.3) | copy-start | bytes 884740
  4.4 12.2 %copy-start.11 = (s32[96]{0:T(128)S(1)}, s32[96]{0:T(128)}, u32[]{:S(2)}) copy-start(s32[96]{0:T(128)} %valid.3) | copy-start | bytes 1156
  4.4 12.2 %copy-start.16 = (s32[576,1]{1,0:T(8,128)S(1)}, s32[576,1]{1,0:T(8,128)}, u32[]{:S(2)}) copy-start(s32[576,1]{1,0:T(8,128)} %constant.54.clone.col) | copy-start | bytes 6916
  4.4 12.2 %copy-start.17 = (s32[576,1]{1,0:T(8,128)S(1)}, s32[576,1]{1,0:T(8,128)}, u32[]{:S(2)}) copy-start(s32[576,1]{1,0:T(8,128)} %constant.53.clone.row) | copy-start | bytes 6916
  4.9 22.4 %collective-permute-start.2 = (bf16[2,32,192]{2,1,0:T(8,128)(2,1)S(1)}, bf16[2,32,192]{2,1,0:T(8,128)(2,1)S(1)}, u32[]{:S(2)}, u32[]{:S(2)}) collective-permute-start(bf16[2,32,192]{2,1,0:T(8,128)(2,1)S(1)} %get-tuple-element.48), channel_id=1, source_target_pairs={{0,127},{1,120},{2,121},{3,122},{4,123},{5,124},{6,125},{7,126},{8... | collective-permute-start | bytes 73736 | tf_op jit(solution)/shard_map/ppermute | solution.py:474
  13.2 28.2 %collective-permute-start.7 = (bf16[2,32,384]{2,1,0:T(8,128)(2,1)S(1)}, bf16[2,32,384]{2,1,0:T(8,128)(2,1)S(1)}, u32[]{:S(2)}, u32[]{:S(2)}) collective-permute-start(bf16[2,32,384]{2,1,0:T(8,128)(2,1)S(1)} %get-tuple-element.57), channel_id=1, source_target_pairs={{0,120},{8,0},{16,8},{24,16},{32,24},{40,32},{48,40},{56,48},{64,5... | collective-permute-start | bytes 147464 | tf_op jit(solution)/shard_map/ppermute | solution.py:466
  14.9 36.4 %collective-permute-start.8 = (bf16[2,32,384]{2,1,0:T(8,128)(2,1)S(1)}, bf16[2,32,384]{2,1,0:T(8,128)(2,1)S(1)}, u32[]{:S(2)}, u32[]{:S(2)}) collective-permute-start(bf16[2,32,384]{2,1,0:T(8,128)(2,1)S(1)} %get-tuple-element.58), channel_id=1, source_target_pairs={{0,127},{1,120},{2,121},{3,122},{4,123},{5,124},{6,125},{7,126},{8... | collective-permute-start | bytes 147464 | tf_op jit(solution)/shard_map/ppermute | solution.py:474
  14.9 12.9 %collective-permute-start.1 = (bf16[2,64,192]{2,1,0:T(8,128)(2,1)S(1)}, bf16[2,64,192]{2,1,0:T(8,128)(2,1)S(1)}, u32[]{:S(2)}, u32[]{:S(2)}) collective-permute-start(bf16[2,64,192]{2,1,0:T(8,128)(2,1)S(1)} %get-tuple-element.47), channel_id=1, source_target_pairs={{0,120},{8,0},{16,8},{24,16},{32,24},{40,32},{48,40},{56,48},{64,5... | collective-permute-start | bytes 147464 | tf_op jit(solution)/shard_map/ppermute | solution.py:466
  15.9 12.0 %collective-permute-start = (bf16[2,128,192]{2,1,0:T(8,128)(2,1)S(1)}, bf16[2,128,192]{2,1,0:T(8,128)(2,1)S(1)}, u32[]{:S(2)}, u32[]{:S(2)}) collective-permute-start(bf16[2,128,192]{2,1,0:T(8,128)(2,1)S(1)} %get-tuple-element.46), channel_id=1, source_target_pairs={{0,7},{1,0},{2,1},{3,2},{4,3},{5,4},{6,5},{7,6},{8,15},{9,8},{10,9... | collective-permute-start | bytes 294920 | tf_op jit(solution)/shard_map/ppermute | solution.py:468
  16.7 9.7 %copy-start.35 = (f32[384]{0:T(512)S(1)}, f32[384]{0:T(512)}, u32[]{:S(2)}) copy-start(f32[384]{0:T(512)} %param.42) | copy-start | bytes 4612
  16.7 9.6 %copy-start.32 = (f32[768]{0:T(1024)S(1)}, f32[768]{0:T(1024)}, u32[]{:S(2)}) copy-start(f32[768]{0:T(1024)} %param.40) | copy-start | bytes 9220
  16.7 11.2 %copy-start.2 = (bf16[2,12,48,192]{3,2,1,0:T(8,128)(2,1)S(1)}, bf16[2,12,48,192]{3,2,1,0:T(8,128)(2,1)}, u32[]{:S(2)}) copy-start(bf16[2,12,48,192]{3,2,1,0:T(8,128)(2,1)} %param.33) | copy-start | bytes 1327108
  16.7 11.2 %copy-start.6 = (bf16[192,576]{1,0:T(8,128)(2,1)S(1)}, bf16[192,576]{1,0:T(8,128)(2,1)}, u32[]{:S(2)}) copy-start(bf16[192,576]{1,0:T(8,128)(2,1)} %project.5) | copy-start | bytes 663556
  16.7 11.2 %copy-start.9 = (bf16[192,192]{1,0:T(8,128)(2,1)S(1)}, bf16[192,192]{1,0:T(8,128)(2,1)}, u32[]{:S(2)}) copy-start(bf16[192,192]{1,0:T(8,128)(2,1)} %combine.5) | copy-start | bytes 221188
  16.7 11.2 %copy-start.10 = (f32[192]{0:T(256)S(1)}, f32[192]{0:T(256)}, u32[]{:S(2)}) copy-start(f32[192]{0:T(256)} %param.35) | copy-start | bytes 2308
  16.7 11.2 %copy-start.15 = (s32[576,1]{1,0:T(8,128)S(1)}, s32[576,1]{1,0:T(8,128)}, u32[]{:S(2)}) copy-start(s32[576,1]{1,0:T(8,128)} %constant.55.clone.take) | copy-start | bytes 6916
  16.7 11.2 %copy-start.20 = (s32[224,1]{1,0:T(8,128)S(1)}, s32[224,1]{1,0:T(8,128)}, u32[]{:S(2)}) copy-start(s32[224,1]{1,0:T(8,128)} %constant.56.clone.sel) | copy-start | bytes 2692
  25.4 0.8 copy-start.28
  27.4 24.0 %collective-permute-start.6 = (bf16[2,64,384]{2,1,0:T(8,128)(2,1)S(1)}, bf16[2,64,384]{2,1,0:T(8,128)(2,1)S(1)}, u32[]{:S(2)}, u32[]{:S(2)}) collective-permute-start(bf16[2,64,384]{2,1,0:T(8,128)(2,1)S(1)} %get-tuple-element.56), channel_id=1, source_target_pairs={{0,7},{1,0},{2,1},{3,2},{4,3},{5,4},{6,5},{7,6},{8,15},{9,8},{10,9... | collective-permute-start | bytes 294920 | tf_op jit(solution)/shard_map/ppermute | solution.py:468
  28.0 1.1 copy-start.29
  29.0 14.0 %copy-start.24 = (s32[144,1]{1,0:T(8,128)S(1)}, s32[144,1]{1,0:T(8,128)}, u32[]{:S(2)}) copy-start(s32[144,1]{1,0:T(8,128)} %constant.58.clone.col) | copy-start | bytes 1732
  29.0 14.0 %copy-start.25 = (s32[144,1]{1,0:T(8,128)S(1)}, s32[144,1]{1,0:T(8,128)}, u32[]{:S(2)}) copy-start(s32[144,1]{1,0:T(8,128)} %constant.57.clone.row) | copy-start | bytes 1732
  38.4 13.0 %collective-permute-start.3 = (bf16[2,128,192]{2,1,0:T(8,128)(2,1)S(1)}, bf16[2,128,192]{2,1,0:T(8,128)(2,1)S(1)}, u32[]{:S(2)}, u32[]{:S(2)}) collective-permute-start(bf16[2,128,192]{2,1,0:T(8,128)(2,1)S(1)} %get-tuple-element.53), channel_id=1, source_target_pairs={{0,7},{1,0},{2,1},{3,2},{4,3},{5,4},{6,5},{7,6},{8,15},{9,8},{10,9... | collective-permute-start | bytes 294920 | tf_op jit(solution)/shard_map/ppermute | solution.py:468
  41.4 10.0 %collective-permute-start.5 = (bf16[2,32,192]{2,1,0:T(8,128)(2,1)S(1)}, bf16[2,32,192]{2,1,0:T(8,128)(2,1)S(1)}, u32[]{:S(2)}, u32[]{:S(2)}) collective-permute-start(bf16[2,32,192]{2,1,0:T(8,128)(2,1)S(1)} %get-tuple-element.55), channel_id=1, source_target_pairs={{0,127},{1,120},{2,121},{3,122},{4,123},{5,124},{6,125},{7,126},{8... | collective-permute-start | bytes 73736 | tf_op jit(solution)/shard_map/ppermute | solution.py:474
  41.4 10.0 %copy-start = (bf16[384,1152]{1,0:T(8,128)(2,1)S(1)}, bf16[384,1152]{1,0:T(8,128)(2,1)}, u32[]{:S(2)}) copy-start(bf16[384,1152]{1,0:T(8,128)(2,1)} %project.4) | copy-start | bytes 2654212
  41.4 10.0 %copy-start.3 = (bf16[768,384]{1,0:T(8,128)(2,1)S(1)}, bf16[768,384]{1,0:T(8,128)(2,1)}, u32[]{:S(2)}) copy-start(bf16[768,384]{1,0:T(8,128)(2,1)} %merge_weight.1) | copy-start | bytes 1769476
  41.4 10.0 %copy-start.5 = (bf16[384,384]{1,0:T(8,128)(2,1)S(1)}, bf16[384,384]{1,0:T(8,128)(2,1)}, u32[]{:S(2)}) copy-start(bf16[384,384]{1,0:T(8,128)(2,1)} %combine.4) | copy-start | bytes 884740
  41.4 10.0 %copy-start.8 = (bf16[2,6,24,384]{3,2,1,0:T(8,128)(2,1)S(1)}, bf16[2,6,24,384]{3,2,1,0:T(8,128)(2,1)}, u32[]{:S(2)}) copy-start(bf16[2,6,24,384]{3,2,1,0:T(8,128)(2,1)} %param.34) | copy-start | bytes 663556
  41.4 10.0 %copy-start.14 = (s32[576,1]{1,0:T(8,128)S(1)}, s32[576,1]{1,0:T(8,128)}, u32[]{:S(2)}) copy-start(s32[576,1]{1,0:T(8,128)} %constant.59.clone.take) | copy-start | bytes 6916
  41.5 10.0 %copy-start.19 = (s32[224,1]{1,0:T(8,128)S(1)}, s32[224,1]{1,0:T(8,128)}, u32[]{:S(2)}) copy-start(s32[224,1]{1,0:T(8,128)} %constant.62.clone.fsel) | copy-start | bytes 2692
  41.5 10.0 %copy-start.23 = (s32[144,1]{1,0:T(8,128)S(1)}, s32[144,1]{1,0:T(8,128)}, u32[]{:S(2)}) copy-start(s32[144,1]{1,0:T(8,128)} %constant.60.clone.ctake) | copy-start | bytes 1732
  41.5 10.0 %copy-start.26 = (s32[128,1]{1,0:T(8,128)S(1)}, s32[128,1]{1,0:T(8,128)}, u32[]{:S(2)}) copy-start(s32[128,1]{1,0:T(8,128)} %constant.61.clone.csel) | copy-start | bytes 1540
  41.5 9.9 %collective-permute-start.4 = (bf16[2,64,192]{2,1,0:T(8,128)(2,1)S(1)}, bf16[2,64,192]{2,1,0:T(8,128)(2,1)S(1)}, u32[]{:S(2)}, u32[]{:S(2)}) collective-permute-start(bf16[2,64,192]{2,1,0:T(8,128)(2,1)S(1)} %get-tuple-element.54), channel_id=1, source_target_pairs={{0,120},{8,0},{16,8},{24,16},{32,24},{40,32},{48,40},{56,48},{64,5... | collective-permute-start | bytes 147464 | tf_op jit(solution)/shard_map/ppermute | solution.py:466
  51.5 21.8 %copy-start.13 = (s32[576,1]{1,0:T(8,128)S(1)}, s32[576,1]{1,0:T(8,128)}, u32[]{:S(2)}) copy-start(s32[576,1]{1,0:T(8,128)} %constant.63.clone.take) | copy-start | bytes 6916
  51.5 21.8 %copy-start.18 = (s32[224,1]{1,0:T(8,128)S(1)}, s32[224,1]{1,0:T(8,128)}, u32[]{:S(2)}) copy-start(s32[224,1]{1,0:T(8,128)} %constant.64.clone.sel) | copy-start | bytes 2692
  63.0 10.3 %collective-permute-start.12 = (bf16[2,128,192]{2,1,0:T(8,128)(2,1)S(1)}, bf16[2,128,192]{2,1,0:T(8,128)(2,1)S(1)}, u32[]{:S(2)}, u32[]{:S(2)}) collective-permute-start(bf16[2,128,192]{2,1,0:T(8,128)(2,1)S(1)} %get-tuple-element.68), channel_id=1, source_target_pairs={{0,1},{1,2},{2,3},{3,4},{4,5},{5,6},{6,7},{7,0},{8,9},{9,10},{10,1... | collective-permute-start | bytes 294920 | tf_op jit(solution)/shard_map/ppermute | solution.py:468
  64.2 9.0 %collective-permute-start.13 = (bf16[2,64,192]{2,1,0:T(8,128)(2,1)S(1)}, bf16[2,64,192]{2,1,0:T(8,128)(2,1)S(1)}, u32[]{:S(2)}, u32[]{:S(2)}) collective-permute-start(bf16[2,64,192]{2,1,0:T(8,128)(2,1)S(1)} %get-tuple-element.69), channel_id=1, source_target_pairs={{0,8},{8,16},{16,24},{24,32},{32,40},{40,48},{48,56},{56,64},{64,7... | collective-permute-start | bytes 147464 | tf_op jit(solution)/shard_map/ppermute | solution.py:466
  64.2 9.0 %collective-permute-start.14 = (bf16[2,32,192]{2,1,0:T(8,128)(2,1)S(1)}, bf16[2,32,192]{2,1,0:T(8,128)(2,1)S(1)}, u32[]{:S(2)}, u32[]{:S(2)}) collective-permute-start(bf16[2,32,192]{2,1,0:T(8,128)(2,1)S(1)} %get-tuple-element.70), channel_id=1, source_target_pairs={{0,9},{1,10},{2,11},{3,12},{4,13},{5,14},{6,15},{7,8},{8,17},{9,18... | collective-permute-start | bytes 73736 | tf_op jit(solution)/shard_map/ppermute | solution.py:474
  120.8 37.6 %copy-start.22 = (s32[144,1]{1,0:T(8,128)S(1)}, s32[144,1]{1,0:T(8,128)}, u32[]{:S(2)}) copy-start(s32[144,1]{1,0:T(8,128)} %constant.65.clone.take) | copy-start | bytes 1732
  120.8 43.8 %all-to-all-start.1 = ((bf16[128,64,128]{2,1,0:T(8,128)(2,1)}), bf16[128,64,128]{2,1,0:T(8,128)(2,1)S(1)}, u32[]{:S(2)}, u32[]{:S(2)}) async-start(bf16[128,64,128]{2,1,0:T(8,128)(2,1)} %broadcast_in_dim.19), calls=%async_computation.1 | async-start | bytes 4194304 | tf_op jit(solution)/shard_map/all_to_all | solution.py:490
  125.6 37.2 %copy-start.12 = (s32[576,1]{1,0:T(8,128)S(1)}, s32[576,1]{1,0:T(8,128)}, u32[]{:S(2)}) copy-start(s32[576,1]{1,0:T(8,128)} %constant.66.clone.take) | copy-start | bytes 6916
  125.6 32.8 %collective-permute-start.9 = (bf16[2,64,384]{2,1,0:T(8,128)(2,1)S(1)}, bf16[2,64,384]{2,1,0:T(8,128)(2,1)S(1)}, u32[]{:S(2)}, u32[]{:S(2)}) collective-permute-start(bf16[2,64,384]{2,1,0:T(8,128)(2,1)S(1)} %get-tuple-element.64), channel_id=1, source_target_pairs={{0,1},{1,2},{2,3},{3,4},{4,5},{5,6},{6,7},{7,0},{8,9},{9,10},{10,1... | collective-permute-start | bytes 294920 | tf_op jit(solution)/shard_map/ppermute | solution.py:468
  126.7 25.1 %collective-permute-start.10 = (bf16[2,32,384]{2,1,0:T(8,128)(2,1)S(1)}, bf16[2,32,384]{2,1,0:T(8,128)(2,1)S(1)}, u32[]{:S(2)}, u32[]{:S(2)}) collective-permute-start(bf16[2,32,384]{2,1,0:T(8,128)(2,1)S(1)} %get-tuple-element.65), channel_id=1, source_target_pairs={{0,8},{8,16},{16,24},{24,32},{32,40},{40,48},{48,56},{56,64},{64,7... | collective-permute-start | bytes 147464 | tf_op jit(solution)/shard_map/ppermute | solution.py:466
  126.7 31.8 %collective-permute-start.11 = (bf16[2,32,384]{2,1,0:T(8,128)(2,1)S(1)}, bf16[2,32,384]{2,1,0:T(8,128)(2,1)S(1)}, u32[]{:S(2)}, u32[]{:S(2)}) collective-permute-start(bf16[2,32,384]{2,1,0:T(8,128)(2,1)S(1)} %get-tuple-element.66), channel_id=1, source_target_pairs={{0,9},{1,10},{2,11},{3,12},{4,13},{5,14},{6,15},{7,8},{8,17},{9,18... | collective-permute-start | bytes 147464 | tf_op jit(solution)/shard_map/ppermute | solution.py:474
  129.5 33.4 %collective-permute-start.15 = (bf16[2,128,192]{2,1,0:T(8,128)(2,1)S(1)}, bf16[2,128,192]{2,1,0:T(8,128)(2,1)S(1)}, u32[]{:S(2)}, u32[]{:S(2)}) collective-permute-start(bf16[2,128,192]{2,1,0:T(8,128)(2,1)S(1)} %get-tuple-element.75), channel_id=1, source_target_pairs={{0,1},{1,2},{2,3},{3,4},{4,5},{5,6},{6,7},{7,0},{8,9},{9,10},{10,1... | collective-permute-start | bytes 294920 | tf_op jit(solution)/shard_map/ppermute | solution.py:468
  130.6 31.3 %collective-permute-start.17 = (bf16[2,32,192]{2,1,0:T(8,128)(2,1)S(1)}, bf16[2,32,192]{2,1,0:T(8,128)(2,1)S(1)}, u32[]{:S(2)}, u32[]{:S(2)}) collective-permute-start(bf16[2,32,192]{2,1,0:T(8,128)(2,1)S(1)} %get-tuple-element.77), channel_id=1, source_target_pairs={{0,9},{1,10},{2,11},{3,12},{4,13},{5,14},{6,15},{7,8},{8,17},{9,18... | collective-permute-start | bytes 73736 | tf_op jit(solution)/shard_map/ppermute | solution.py:474
  151.7 11.1 %collective-permute-start.16 = (bf16[2,64,192]{2,1,0:T(8,128)(2,1)S(1)}, bf16[2,64,192]{2,1,0:T(8,128)(2,1)S(1)}, u32[]{:S(2)}, u32[]{:S(2)}) collective-permute-start(bf16[2,64,192]{2,1,0:T(8,128)(2,1)S(1)} %get-tuple-element.76), channel_id=1, source_target_pairs={{0,8},{8,16},{16,24},{24,32},{32,40},{40,48},{48,56},{56,64},{64,7... | collective-permute-start | bytes 147464 | tf_op jit(solution)/shard_map/ppermute | solution.py:466

commit v2 on v1

--- a/solution.py
+++ b/solution.py
@@ -15,6 +15,7 @@
 HEAD = 32
 SCALE = HEAD ** (-0.5)
 BLOCKED = -1e30
+UNROLL = 4
 NT = (((1,), (1,)), ((), ()))
 TN = (((0,), (0,)), ((), ()))
 NN = (((1,), (0,)), ((), ()))
@@ -120,7 +121,7 @@
 
 
 def weights_of(k16, qbig, kinds16, types16, bias):
-    x = mm(k16, qbig, NT) * SCALE + (mm(kinds16, types16, NT) + bias)
+    x = mm(k16, qbig, NT) * SCALE + (mm(kinds16, types16) + bias)
     e = jnp.exp(x - jnp.max(x, axis=0, keepdims=True))
     return (e * (1.0 / jnp.sum(e, axis=0, keepdims=True))).astype(BF16)
 
@@ -147,10 +148,9 @@
     return centred, lax.rsqrt(spread + EPSILON)
 
 
-def norm_back(centred, inverse, gains, deltas):
-    count = sum(x.shape[-1] for x in centred)
+def norm_back(unit, inverse, gains, deltas):
+    count = sum(x.shape[-1] for x in unit)
     scaled = [d * g for d, g in zip(deltas, gains)]
-    unit = [c * inverse for c in centred]
     mean = sum(jnp.sum(s, axis=-1, keepdims=True) for s in scaled) * (1.0 / count)
     along = sum(jnp.sum(s * u, axis=-1, keepdims=True) for s, u in zip(scaled, unit)) * (1.0 / count)
     return [(s - mean - u * along) * inverse for s, u in zip(scaled, unit)]
@@ -165,11 +165,22 @@
         at += n
 
 
-def prepare_kernel(fsel, csel, tokens, cot, fa, fb, fc, ca, cb, cc):
+def prepare_kernel(fsel, csel, tokens, cot, fa, fb, fc, ca, cb, cc, fsel_s, csel_s, tokens_s, cot_s, sems):
+    copies = [
+        pltpu.make_async_copy(src, dst, sems.at[i])
+        for i, (src, dst) in enumerate(((fsel, fsel_s), (tokens, tokens_s), (csel, csel_s), (cot, cot_s)))
+    ]
+    for copy in copies:
+        copy.start()
     nf, nc = tokens.shape[0] // 2, cot.shape[0] // 2
-    for level in range(2):
-        send_out(fsel[...], tokens[level * nf : (level + 1) * nf, :], (fa, fb, fc), level)
-        send_out(csel[...], cot[level * nc : (level + 1) * nc, :], (ca, cb, cc), level)
+    copies[0].wait()
+    copies[1].wait()
+    for level in range(2):
+        send_out(fsel_s[...], tokens_s[level * nf : (level + 1) * nf, :], (fa, fb, fc), level)
+    copies[2].wait()
+    copies[3].wait()
+    for level in range(2):
+        send_out(csel_s[...], cot_s[level * nc : (level + 1) * nc, :], (ca, cb, cc), level)
 
 
 def bias_kernel(
@@ -178,34 +189,50 @@
 ):
     lat, lon, lats = place[0], place[1], place[2]
     windows, heads = bias.shape[1], bias.shape[3] // 72
-    chunks = table.shape[1] // 128
-    count = table.shape[0]
-    pieces = [table[:, c * 128 : (c + 1) * 128] for c in range(chunks)]
-    pad = [jnp.zeros((-count % 8, 128), F32)] if count % 8 else []
-    whole = count + (-count % 8)
-    high_part = jnp.concatenate([x for p in pieces for x in [round16(p)] + pad], axis=0)
-    low_part = jnp.concatenate([x for p in pieces for x in [p - round16(p)] + pad], axis=0)
-    parts[:, 0:128] = high_part.astype(BF16)
-    parts[:, 128:256] = low_part.astype(BF16)
-    lanes_down = lax.broadcasted_iota(jnp.int32, (128, 128), 0)
-
-    def two_rows(i, carry):
-        places = [index[2 * i + j] for j in range(2)]
-        hot = jnp.concatenate(
-            [jnp.where(lanes_down == (x & 127), 1.0, 0.0) for x in places], axis=1
-        ).astype(BF16)
+    entries = table.shape[2]
+    chunks = -(-entries // 128)
+    count = windows * heads
+    eights, half = count // 8, chunks // 2
+    pieces = []
+    for c in range(chunks):
+        lanes = slice(c * 128, min(c * 128 + 128, entries))
+        rows = [table[h, rw : rw + 1, lanes] for rw in range(windows) for h in range(heads)]
+        piece = jnp.concatenate(rows, axis=0)
+        if piece.shape[1] < 128:
+            piece = jnp.concatenate([piece, jnp.zeros((count, 128 - piece.shape[1]), F32)], axis=1)
+        pieces.append(piece)
+    groups = [p[8 * g : 8 * g + 8] for g in range(eights) for p in pieces]
+    if count % 8:
+        groups += [jnp.concatenate([pieces[c][8 * eights :], pieces[c + half][8 * eights :]], axis=0) for c in range(half)]
+    whole = jnp.concatenate(groups, axis=0)
+    parts[:, 0:128] = whole.astype(BF16)
+    parts[:, 128:256] = (whole - round16(whole)).astype(BF16)
+    lanes_down = lax.broadcasted_iota(jnp.int32, (128, 256), 0)
+    lower = jnp.where(lax.broadcasted_iota(jnp.int32, (8, 256), 0) >= 4, half, 0)
+
+    def three_rows(i, carry):
+        place = index[i]
+        hot = jnp.where(lanes_down == (place & 127), 1.0, 0.0).astype(BF16)
         found = mm(parts[...], jnp.concatenate([hot, hot], axis=0))
-        for j in range(2):
-            chunk = jnp.broadcast_to(places[j] >> 7, (8, 128))
-            for g in range(0, whole, 8):
-                total = jnp.zeros((8, 128), F32)
-                for c in range(chunks):
-                    at = c * whole + g
-                    total = jnp.where(chunk == c, found[at : at + 8, 128 * j : 128 * (j + 1)], total)
-                raw[pl.ds(g * 144 + 2 * i + j, 8, stride=144), :] = total
+        chunk = jnp.broadcast_to(place >> 7, (8, 256))
+
+        def chosen(at, steps, chunk):
+            total = jnp.zeros((8, 256), F32)
+            for c in range(steps):
+                total = jnp.where(chunk == c, found[at + 8 * c : at + 8 * c + 8, :], total)
+            return total
+
+        totals = [chosen(8 * chunks * g, chunks, chunk) for g in range(eights)]
+        if count % 8:
+            total = chosen(8 * chunks * eights, half, chunk - lower)
+            totals.append(total + jnp.concatenate([total[4:], total[:4]], axis=0))
+        for g, total in enumerate(totals):
+            for r in range(3):
+                row = jnp.concatenate([total[:, 72 * r : 72 * r + 72], jnp.zeros((8, 56), F32)], axis=1)
+                raw[pl.ds(g * 1152 + 3 * i + r, 8, stride=144), :] = row
         return carry
 
-    lax.fori_loop(0, 72, two_rows, 0, unroll=4)
+    lax.fori_loop(0, 48, three_rows, 0, unroll=4)
 
     key = lax.broadcasted_iota(jnp.int32, (72, 72), 0)
     query = lax.broadcasted_iota(jnp.int32, (72, 72), 1)
@@ -250,7 +277,7 @@
     split = jnp.where(lanes < 3, high, jnp.where(lanes < 6, middle, t - high - middle))
     typed[...] = jnp.concatenate(
         [jnp.broadcast_to(split[h : h + 1], (72, 128)) for h in range(heads)], axis=0
-    ).astype(BF16)
+    ).T.astype(BF16)
 
 
 def fine_forward_kernel(
@@ -289,7 +316,7 @@
             o_s[rows, :] = fold_heads(mm(p, v_s[rows, :].astype(BF16), TN), masks)
         return carry
 
-    lax.fori_loop(0, windows, window, 0)
+    lax.fori_loop(0, windows, window, 0, unroll=UNROLL)
     o16 = o_s[...].astype(BF16)
     kept_o[...] = o16
     out = (x + mm(o16, combine[...])).astype(BF16)
@@ -301,8 +328,8 @@
 def coarse_kernel(
     take, ctake, csel, fsel, fine, ra, rb, rc, cot, da, db, dc,
     merge_gain, merge_weight, gain, project, combine, bias, kinds, types,
-    output, oa, ob, oc, delta_fine, sa, sb, sc, gradients,
-    q_s, k_s, v_s, o_s, do_s, dq_s, dk_s, dv_s, p_s,
+    output, oa, ob, oc, delta_fine, sa, sb, sc, kept_merged, kept,
+    q_s, k_s, v_s, o_s, do_s, dq_s, dk_s, dv_s,
 ):
     n = take.shape[0]
     quarter = n // 4
@@ -354,7 +381,7 @@
             dv_s[rows, :] = dv
         return carry
 
-    lax.fori_loop(0, windows, window, 0)
+    lax.fori_loop(0, windows, window, 0, unroll=2)
     o16 = o_s[...].astype(BF16)
     out = (x + mm(o16, combine[...])).astype(BF16)
     output[...] = out
@@ -362,32 +389,51 @@
         send_out(csel[...], out[level * quarter : (level + 1) * quarter], (oa, ob, oc), level)
     dq16, dk16, dv16 = dq_s[...].astype(BF16), dk_s[...].astype(BF16), dv_s[...].astype(BF16)
     delta_rolled = round16(mm(dq16, wq, NT) + mm(dk16, wk, NT) + mm(dv16, wv, NT))
-    (dx,) = norm_back([centred], inverse, [gain[...]], [delta_rolled])
+    (dx,) = norm_back([centred * inverse], inverse, [gain[...]], [delta_rolled])
     delta = (d + round16(dx)).astype(BF16)
     deltas = [round16(mm(delta, w, NT)) for w in weight]
-    back = norm_back(m_centred, m_inverse, merge_gains, deltas)
+    back = norm_back([c * m_inverse for c in m_centred], m_inverse, merge_gains, deltas)
     back = [b.astype(BF16) for b in back]
     for level in range(2):
         own = jnp.concatenate([b[level * quarter : (level + 1) * quarter] for b in back], axis=0)
         delta_fine[level * n : (level + 1) * n, :] = own
         send_out(fsel[...], own, (sa, sb, sc), level)
-    sums = [jnp.concatenate([mm(m, delta, TN) for m in merged], axis=0)]
+    for s in range(4):
+        kept_merged[s] = merged[s]
+    for i, x in enumerate((u, dq16, dk16, dv16, o16, d16, delta)):
+        kept[i] = x
+
+
+def coarse_gradient_kernel(merged, kept, gradients):
+    u, dq16, dk16, dv16, o16, d16, delta = (kept[i] for i in range(7))
+    sums = [jnp.concatenate([mm(merged[s], delta, TN) for s in range(4)], axis=0)]
     sums += [mm(left, right, TN) for left, right in ((u, dq16), (u, dk16), (u, dv16), (o16, d16))]
     at = 0
     for block in sums:
-        for j in range(width // 128):
+        for j in range(block.shape[1] // 128):
             gradients[at : at + block.shape[0], :] = block[:, j * 128 : (j + 1) * 128].astype(BF16)
             at += block.shape[0]
 
 
+def fine_again_kernel(kept_x, gain, project, kept_u, unit, inverse_out, q, k, v):
+    width = kept_x.shape[1]
+    (centred,), inverse = moments([kept_x[...].astype(F32)])
+    scaled = centred * inverse
+    u = (scaled * gain[...]).astype(BF16)
+    kept_u[...] = u
+    unit[...] = scaled
+    inverse_out[...] = jnp.broadcast_to(inverse, inverse_out.shape)
+    for i, out in enumerate((q, k, v)):
+        out[...] = round16(mm(u, project[:, i * width : (i + 1) * width]))
+
+
 def fine_backward_kernel(
-    take, sel, own, ra, rb, rc, kept_x, kept_p, kept_o,
-    gain, project, combine,
-    output, sa, sb, sc, gradients,
-    q_s, k_s, v_s, do_s, dq_s, dk_s, dv_s,
+    take, sel, own, ra, rb, rc, unit, inverse, q_s, k_s, v_s, kept_p, gain, project, combine,
+    output, sa, sb, sc, kept,
+    do_s, dq_s, dk_s, dv_s,
 ):
     n = take.shape[0]
-    width = kept_x.shape[1]
+    width = unit.shape[1]
     total = n + ra.shape[1] + rb.shape[1] + rc.shape[1]
     hot = one_hot(take[...], total)
     d = jnp.concatenate(
@@ -399,10 +445,6 @@
     )
     d16 = d.astype(BF16)
     do_s[...] = round16(mm(d16, combine[...], NT))
-    (centred,), inverse = moments([kept_x[...].astype(F32)])
-    u = (centred * inverse * gain[...]).astype(BF16)
-    for i, scratch in enumerate((q_s, k_s, v_s)):
-        scratch[...] = round16(mm(u, project[:, i * width : (i + 1) * width]))
     masks = head_masks(width)
     windows = n // 72
 
@@ -418,20 +460,29 @@
             dv_s[rows, :] = dv
         return carry
 
-    lax.fori_loop(0, windows, window, 0)
+    lax.fori_loop(0, windows, window, 0, unroll=UNROLL)
     parts = [dq_s[...].astype(BF16), dk_s[...].astype(BF16), dv_s[...].astype(BF16)]
     delta_rolled = round16(
         sum(mm(a, project[:, i * width : (i + 1) * width], NT) for i, a in enumerate(parts))
     )
-    (dx,) = norm_back([centred], inverse, [gain[...]], [delta_rolled])
+    (dx,) = norm_back([unit[...]], inverse[:, 0:1], [gain[...]], [delta_rolled])
     out = (d + round16(dx)).astype(BF16)
     output[...] = out
     for level in range(2):
         send_out(sel[...], out[level * n : (level + 1) * n], (sa, sb, sc), level)
-    pieces = [mm(u, a, TN) for a in parts] + [mm(kept_o[...], d16, TN)]
+    for i, x in enumerate(parts + [d16]):
+        kept[i] = x
+
+
+def fine_gradient_kernel(kept_u, kept_o, kept, coarse, gradients):
+    width, at = kept_u.shape[1], coarse.shape[0]
+    gradients[:at, :] = coarse[...]
+    pieces = [mm(kept_u[...], kept[i], TN) for i in range(3)] + [mm(kept_o[...], kept[3], TN)]
     pieces = jnp.concatenate(pieces, axis=1).astype(BF16)
     for j in range(pieces.shape[1] // 128):
-        gradients[j * width : (j + 1) * width, :] = pieces[:, j * 128 : (j + 1) * 128]
+        gradients[at : at + width, :] = pieces[:, j * 128 : (j + 1) * 128]
+        at += width
+    gradients[at:, :] = jnp.zeros((gradients.shape[0] - at, 128), BF16)
 
 
 def restore_kernel(take, own, ra, rb, rc, output):
@@ -447,14 +498,20 @@
 SMEM = pl.BlockSpec(memory_space=pltpu.SMEM)
 
 
-def call(kernel, name, outs, scratch, args, smem=0, flops=10**9, limit=20):
+LIMITS = {"fine_bias": 6, "coarse_bias": 6, "fine_again": 8, "coarse_gradients": 6, "fine_gradients": 6, "restore_coarse": 4, "restore_fine": 6, "add": 4, "finish": 6}
+
+
+def call(kernel, name, outs, scratch, args, smem=0, flops=10**9, limit=16, space=pltpu.VMEM, copies=0):
+    limit = LIMITS.get(name, limit)
+    given = pl.BlockSpec(memory_space=space)
+    semaphores = [pltpu.SemaphoreType.DMA((copies,))] if copies else []
     return pl.pallas_call(
         kernel,
         name=name,
         out_shape=[jax.ShapeDtypeStruct(s, d) for s, d in outs],
-        in_specs=[SMEM] * smem + [VMEM] * (len(args) - smem),
+        in_specs=[SMEM] * smem + [given] * (len(args) - smem),
         out_specs=[VMEM] * len(outs),
-        scratch_shapes=[pltpu.VMEM(s, d) for s, d in scratch],
+        scratch_shapes=[pltpu.VMEM(s, d) for s, d in scratch] + semaphores,
         cost_estimate=pl.CostEstimate(flops=flops, bytes_accessed=4 << 20, transcendentals=0),
         compiler_params=pltpu.CompilerParams(vmem_limit_bytes=limit << 20),
     )(*args)
@@ -479,37 +536,44 @@
     return [move(a, step, 0), move(b, 0, step), move(c, step, step)]
 
 
-def summed(blocks):
+def add_kernel(terms, repeated):
+    count = terms.shape[0]
+
+    def eight(i, total):
+        return total + sum(terms[8 * i + j].astype(F32) for j in range(8))
+
+    total = lax.fori_loop(0, count // 8, eight, jnp.zeros(terms.shape[1:], F32)).astype(BF16)
+
+    def store(i, carry):
+        for j in range(8):
+            repeated[8 * i + j] = total
+        return carry
+
+    lax.fori_loop(0, count // 8, store, 0)
+
+
+def summed(block, before):
     count = lax.axis_size("lon") * lax.axis_size("lat")
-    block = jnp.concatenate(blocks, axis=0)
-    chunk = pad16(-(-block.shape[0] // count))
-    block = jnp.pad(block, ((0, count * chunk - block.shape[0]), (0, 0))).reshape(count, chunk, 128)
+    block = block.reshape(count, -1, 128)
     terms = lax.all_to_all(block, ("lon", "lat"), 0, 0, tiled=True)
-    total = jnp.sum(terms.astype(F32), axis=0).astype(BF16)
-    total = jnp.broadcast_to(total[None], terms.shape)
-    return lax.all_to_all(total, ("lon", "lat"), 0, 0, tiled=True).reshape(count * chunk, 128)
+    terms, *before = lax.optimization_barrier((terms, *before))
+    (total,) = call(add_kernel, "add", [(block.shape, BF16)], [], [terms])
+    return lax.all_to_all(total, ("lon", "lat"), 0, 0, tiled=True).reshape(-1, 128), before
 
 
 def finish_kernel(fine_scale, coarse_scale, sums, project1, combine1, merge, project2, combine2):
     thin, width = combine1.shape[0], combine2.shape[0]
     at = 0
-
-    def take(rows):
-        nonlocal at
-        at += rows
-        return sums[at - rows : at, :].astype(F32)
-
-    for j in range(width // 128):
-        merge[:, j * 128 : (j + 1) * 128] = take(merge.shape[0]) * coarse_scale
-    for i in range(3):
-        for j in range(width // 128):
-            lane = i * width + j * 128
-            project2[:, lane : lane + 128] = take(width) * coarse_scale
-    for j in range(width // 128):
-        combine2[:, j * 128 : (j + 1) * 128] = take(width) * coarse_scale
-    fine = jnp.concatenate([take(thin) for _ in range(4 * thin // 128)], axis=1) * fine_scale
-    project1[...] = fine[:, : 3 * thin]
-    combine1[...] = fine[:, 3 * thin :]
+    for block, lanes in ((merge, range(1)), (project2, range(3)), (combine2, range(1))):
+        for i in lanes:
+            for j in range(width // 128):
+                rows, lane = block.shape[0], i * width + j * 128
+                block[:, lane : lane + 128] = sums[at : at + rows, :].astype(F32) * coarse_scale
+                at += rows
+    pieces = [sums[at + j * thin : at + (j + 1) * thin, :].astype(F32) for j in range(4 * thin // 128)]
+    whole = jnp.concatenate(pieces, axis=1) * fine_scale
+    project1[...] = whole[:, : 3 * thin]
+    combine1[...] = whole[:, 3 * thin :]
 
 
 def local(
@@ -534,19 +598,19 @@
     cot = cotangent.reshape(2 * n2, d2)
 
     halos = call(
-        prepare_kernel, "prepare", fine_halo + coarse_halo, [],
-        [enter.send, centre.send, tokens, cot], flops=10**9,
+        prepare_kernel, "prepare", fine_halo + coarse_halo,
+        [(x.shape, x.dtype) for x in (enter.send, centre.send, tokens, cot)],
+        [enter.send, centre.send, tokens, cot], limit=60, space=pltpu.HBM, copies=4,
     )
     token_halo = exchange(halos[:3], -1)
     cot_halo = exchange(halos[3:], -1)
 
     place = jnp.stack([lax.axis_index("lat"), lax.axis_index("lon"), jnp.int32(lats)]).astype(jnp.int32)
     pairs = jnp.concatenate([bias_index[:72, :72].T, bias_index[72:, 72:].T], axis=0)
-    pairs = jnp.pad(pairs, ((0, 0), (0, 56)))[:, None]
+    pairs = jnp.pad(pairs.reshape(48, 216), ((0, 0), (0, 40)))[:, None]
 
     def level_bias(name, where, table, types, level_rows, rows, cols):
-        lists = jnp.swapaxes(table[0], 1, 2).reshape(-1, table.shape[2])
-        lists = jnp.pad(lists, ((0, 0), (0, -lists.shape[1] % 128)))
+        lists = jnp.transpose(table[0], (2, 0, 1))
         t = types.T
         t = jnp.pad(jnp.concatenate([t, t, t], axis=1), ((0, 0), (0, 128 - 9)))
         order = windowed(cols)
@@ -555,11 +619,12 @@
             for b in range(cols):
                 r[order(a, b), 0], c[order(a, b), 0] = a + 3, b + 6
         heads = types.shape[1]
-        count = pad8(lists.shape[0])
+        count = lists.shape[0] * lists.shape[1]
+        chunks = -(-lists.shape[2] // 128)
         return call(
             partial(bias_kernel, level_rows), name,
-            [((2, rows // 6, 72, 72 * heads), F32), ((rows * cols, 128), F32), ((72 * heads, 128), BF16)],
-            [((count * 144, 128), F32), ((count * lists.shape[1] // 128, 256), BF16)],
+            [((2, rows // 6, 72, 72 * heads), F32), ((rows * cols, 128), F32), ((128, 72 * heads), BF16)],
+            [((pad8(count) * 144, 128), F32), ((count * chunks, 256), BF16)],
             [where, latitude_valid, pairs, lists, surface_type, t, r, c],
             smem=2, flops=4 * 10**9,
         )
@@ -584,8 +649,9 @@
     rows = (4 * d1 + 4 * d2) * d2 // 128
     coarse = call(
         coarse_kernel, "coarse",
-        [((2 * n2, d2), BF16)] + coarse_halo + [token16(d1)] + fine_halo + [((rows, 128), BF16)],
-        [((2 * n2, d2), F32)] * 8 + [((8, 128), F32)],
+        [((2 * n2, d2), BF16)] + coarse_halo + [token16(d1)] + fine_halo
+        + [((4, 2 * n2, d1), BF16), ((7, 2 * n2, d2), BF16)],
+        [((2 * n2, d2), F32)] * 8,
         [middle.take, centre.take, cleave.send, return_middle.send, fine_output, *halo, cot, *cot_halo,
          merge_gain.reshape(4, d1), merge_weight, coarse_gain[None], coarse_project, coarse_combine,
          cbias, ckinds, ctyped],
@@ -593,29 +659,43 @@
     )
     delta_halo = exchange(coarse[5:8], 1)
     out_halo = exchange(coarse[1:4], 1)
-
+    kept_x, kept_p, kept_o, after = lax.optimization_barrier((*kept, coarse[8]))
+    (coarse_sums,) = call(
+        coarse_gradient_kernel, "coarse_gradients", [((rows, 128), BF16)], [], [after, coarse[9]], flops=2 * 10**9,
+    )
+    wide = ((2 * n1, d1), F32)
+    u, unit, inverse, q, k, v = call(
+        fine_again_kernel, "fine_again", [token16(d1), wide, ((2 * n1, 128), F32), wide, wide, wide], [],
+        [kept_x, fine_gain[None], fine_project], flops=2 * 10**9,
+    )
     backward = call(
         fine_backward_kernel, "fine_backward",
-        [token16(d1)] + fine_halo + [((4 * d1 * d1 // 128, 128), BF16)],
-        [((2 * n1, d1), F32)] * 7,
-        [return_middle.take, leave.send, coarse[4], *delta_halo, *kept,
+        [token16(d1)] + fine_halo + [((4, 2 * n1, d1), BF16)],
+        [wide] * 4,
+        [return_middle.take, leave.send, coarse[4], *delta_halo, unit, inverse, q, k, v, kept_p,
          fine_gain[None], fine_project, fine_combine],
         flops=6 * 10**9,
     )
     last_halo = exchange(backward[1:4], 1)
+    count = lons * lats
+    chunk = pad16(-(-(rows + 4 * d1 * d1 // 128) // count))
+    (sums,) = call(
+        fine_gradient_kernel, "fine_gradients", [((count * chunk, 128), BF16)], [],
+        [u, kept_o, backward[4], coarse_sums], flops=2 * 10**9,
+    )
+    sums, *out_halo = lax.optimization_barrier((sums, *out_halo))
+    sums, last_halo = summed(sums, last_halo)
 
     (coarse_out,) = call(
         restore_kernel, "restore_coarse", [((2 * n2, d2), BF16)], [],
         [cleave.take, coarse[0], *out_halo],
     )
+    count = 2 * n1 * lons * lats
+    fine_scale, coarse_scale = 1.0 / math.sqrt(count), 1.0 / math.sqrt(count // 4)
     (gradient,) = call(
         restore_kernel, "restore_fine", [token16(d1)], [],
         [leave.take, backward[0], *last_halo],
     )
-
-    count = 2 * n1 * lons * lats
-    fine_scale, coarse_scale = 1.0 / math.sqrt(count), 1.0 / math.sqrt(count // 4)
-    sums = summed([coarse[8], backward[4]])
     gradients = call(
         partial(finish_kernel, fine_scale, coarse_scale), "finish",
         [((d1, 3 * d1), F32), ((d1, d1), F32), ((4 * d1, d2), F32), ((d2, 3 * d2), F32), ((d2, d2), F32)],

time: 167 us -> 157 us (0.940)
  blocking collectives: 33.9 us -> 0 us
  waiting for transfers between devices: 38.4 us -> 59.8 us
  starting transfers between devices: 28.8 us -> 36.8 us
  local copies, waits for them, and re-layouts: 9.19 us -> 6.23 us
  Pallas kernels: 54.5 us -> 52.3 us
    all_to_all x1 -> x0, blocking collectives: 33.9 us -> none  [summed(): terms = lax.all_to_all(block, ('lon', 'lat'), 0, 0, tiled=True)]
    all_to_all x1 -> x2, waiting for transfers between devices: 0.01 us -> 26.1 us  [the longest x1 26.1 us: summed(): lax.all_to_all(total, ('lon', 'lat'), 0, 0, tiled=True).reshape(-1, 128)]
    ppermute x6, waiting for transfers between devices: 21.3 us -> 0.02 us  [move(): lax.ppermute(value, 'lon', [(s, (s + lon_step) % lons) for s in range(lon...]
    ppermute x6, waiting for transfers between devices: 17.1 us -> 31.9 us  [move(): return lax.ppermute(value, ('lon', 'lat'), pairs)]
    all_to_all x1 -> x2, starting transfers between devices: 4.8 us -> 12.2 us  [the longest x1 7.39 us: summed(): terms = lax.all_to_all(block, ('lon', 'lat'), 0, 0, tiled=True)]
    pallas_call x9 -> x13, Pallas kernels: 54.5 us -> 52.3 us  [call(): pl.pallas_call(kernel, name=name, out_shape=[jax.ShapeDtypeStruct(s, d) f...]
    broadcast_in_dim x1, local copies, waits for them, and re-layouts: 1.89 us -> 0.04 us  [local(): pairs = jnp.pad(pairs.reshape(48, 216), ((0, 0), (0, 40)))[:, None]]
    ppermute x6, waiting for transfers between devices: 0.02 us -> 1.83 us  [move(): lax.ppermute(value, 'lat', [(s, (s + lat_step) % lats) for s in range(lat...]
  transfers between devices with their start and end apart: 19 -> 20, of which waited for: 5 -> 4; matrix products, arithmetic and copies ran while one was open for 1% -> 1% of each run, Pallas kernels for 18% -> 24%
where the time goes in v2:
time: 157 us
  waiting for transfers between devices  59.8 us (38%)
  Pallas kernels  52.3 us (33%)
  starting transfers between devices  36.8 us (23%)
  local copies, waits for them, and re-layouts  6.23 us (4%)
    pallas_call x13, Pallas kernels, call(): pl.pallas_call(kernel, name=name, out_shape=[jax.ShapeDtypeStruct(s, d) f...  52.3 us
    ppermute x6, waiting for transfers between devices, move(): return lax.ppermute(value, ('lon', 'lat'), pairs)  31.9 us
    all_to_all x1, waiting for transfers between devices, summed(): lax.all_to_all(total, ('lon', 'lat'), 0, 0, tiled=True).reshape(-1, 128)  26.1 us
    ppermute x6, starting transfers between devices, move(): return lax.ppermute(value, ('lon', 'lat'), pairs)  11.9 us
    all_to_all x1, starting transfers between devices, summed(): terms = lax.all_to_all(block, ('lon', 'lat'), 0, 0, tiled=True)  7.39 us
    ppermute x6, starting transfers between devices, move(): lax.ppermute(value, 'lat', [(s, (s + lat_step) % lats) for s in range(lat...  7.17 us
    unnamed x80, local copies, waits for them, and re-layouts  5.86 us
    ppermute x6, starting transfers between devices, move(): lax.ppermute(value, 'lon', [(s, (s + lon_step) % lons) for s in range(lon...  5.52 us
  transfers between devices with their start and end apart: 20, of which 4 were waited for; matrix products, arithmetic and copies ran while one was open for 1% of the time, Pallas kernels for 24%

profile of v2, /device:TPU:0, one launch (start us, length us, event | category | flops | bytes accessed | tf_op | source)
XLA Modules:
  0.0 156.7 jit_solution(18226497884572836529)
XLA Ops:
  0.7 0.0 copy-start.17
  0.7 0.0 copy-start.18
  0.7 2.6 %prepare.1 = (bf16[2,128,192]{2,1,0:T(8,128)(2,1)}, bf16[2,64,192]{2,1,0:T(8,128)(2,1)}, bf16[2,32,192]{2,1,0:T(8,128)(2,1)}, bf16[2,64,384]{2,1,0:T(8,128)(2,1)...) custom-call(s32[224,1]{1,0:T(8,128)} %constant.47.clone.fsel, s32[128,1]{1,0:T(8,128)} %constant.48.clone.csel, ...), custom_call_target="tpu_custom_call" | custom-call | flops 1000000000 | bytes 4194304 | tf_op jit(solution)/shard_map/prepare/pallas_call | solution.py:508
  3.3 8.3 %collective-permute-start.2 = (bf16[2,32,192]{2,1,0:T(8,128)(2,1)}, bf16[2,32,192]{2,1,0:T(8,128)(2,1)S(1)}, u32[]{:S(2)}, u32[]{:S(2)}) collective-permute-start(bf16[2,32,192]{2,1,0:T(8,128)(2,1)} %get-tuple-element.67), channel_id=1, source_target_pairs={{0,127},{1,120},{2,121},{3,122},{4,123},{5,124},{6,125},{7,126},{8... | collective-permute-start | bytes 73736 | tf_op jit(solution)/shard_map/ppermute | solution.py:531
  11.6 1.7 %collective-permute-start.7 = (bf16[2,32,384]{2,1,0:T(8,128)(2,1)}, bf16[2,32,384]{2,1,0:T(8,128)(2,1)S(1)}, u32[]{:S(2)}, u32[]{:S(2)}) collective-permute-start(bf16[2,32,384]{2,1,0:T(8,128)(2,1)} %get-tuple-element.76), channel_id=1, source_target_pairs={{0,120},{8,0},{16,8},{24,16},{32,24},{40,32},{48,40},{56,48},{64,5... | collective-permute-start | bytes 147464 | tf_op jit(solution)/shard_map/ppermute | solution.py:523
  13.3 0.9 collective-permute-start.1
  14.3 0.1 copy.41
  14.4 0.1 select_maximum_fusion.2.types
  14.5 0.1 copy.42
  14.6 0.1 slice_bitcast_fusion.1
  14.6 0.1 pad_add_fusion
  14.7 0.1 copy.40
  14.8 0.1 reshape.40
  15.0 0.1 pad_add_fusion.1.place
  15.1 0.0 copy-start.37
  15.1 0.0 copy-start.38
  15.1 0.0 copy-start.2
  15.2 0.0 copy-start.11
  15.2 0.0 copy-start.16
  15.2 0.0 copy-start.21
  15.2 6.6 %fine_bias.1 = (f32[2,2,72,432]{3,2,1,0:T(8,128)S(1)}, f32[576,128]{1,0:T(8,128)S(1)}, bf16[128,432]{1,0:T(8,128)(2,1)S(1)}) custom-call(s32[3]{0:T(128)S(1)} %pad_add_fusion.1.place, s32[96]{0:T(128)S(1)} %copy-done.12, s32[48,1,256]{2,1,0:T(1,128)S(1)} %broadcast_in_dim.12.index, f32[6,2,3312]{2,1,0:T(2,128)S(1)} %bitcast.26, s32[96,768]{1,0:T(8,128)S(1)} %copy-done.4, ...), custom_call_target="tpu_custom_call" | custom-call | flops 4000000000 | bytes 4194304 | tf_op jit(solution)/shard_map/fine_bias/pallas_call | solution.py:508
  21.8 0.0 copy-start.29
  21.9 0.7 copy-done.29
  22.6 0.7 copy-done.31
  23.2 0.1 select_maximum_fusion.types
  23.3 0.1 reshape.41.merge_gain
  23.4 0.5 collective-permute-start.6
  24.0 1.0 copy-done.30
  24.9 0.9 copy-done.32
  25.8 8.2 %fine_forward.1 = (bf16[1152,192]{1,0:T(8,128)(2,1)S(1)}, bf16[2,128,192]{2,1,0:T(8,128)(2,1)S(1)}, bf16[2,64,192]{2,1,0:T(8,128)(2,1)S(1)}, bf16[2,32,192]{2,1,...) custom-call(s32[576,1]{1,0:T(8,128)S(1)} %copy-done.16, ...), custom_call_target="tpu_custom_call" | custom-call | flops 4000000000 | bytes 4194304 | tf_op jit(solution)/shard_map/fine_forward/pallas_call | solution.py:508
  34.1 3.0 %collective-permute-start.3 = (bf16[2,128,192]{2,1,0:T(8,128)(2,1)S(1)}, bf16[2,128,192]{2,1,0:T(8,128)(2,1)S(1)}, u32[]{:S(2)}, u32[]{:S(2)}) collective-permute-start(bf16[2,128,192]{2,1,0:T(8,128)(2,1)S(1)} %get-tuple-element.72), channel_id=1, source_target_pairs={{0,7},{1,0},{2,1},{3,2},{4,3},{5,4},{6,5},{7,6},{8,15},{9,8},{10,9... | collective-permute-start | bytes 294920 | tf_op jit(solution)/shard_map/ppermute | solution.py:525
  37.1 1.3 collective-permute-start.4
  38.4 0.0 copy-start.15
  38.4 0.0 copy-start.20
  38.4 0.0 copy-start.23
  38.5 0.0 copy-start.26
  38.5 6.4 %coarse_bias.1 = (f32[2,1,72,864]{3,2,1,0:T(8,128)S(1)}, f32[144,128]{1,0:T(8,128)S(1)}, bf16[128,864]{1,0:T(8,128)(2,1)S(1)}) custom-call(s32[3]{0:T(128)S(1)} %pad_add_fusion.1.place, s32[96]{0:T(128)S(1)} %copy-done.12, s32[48,1,256]{2,1,0:T(1,128)S(1)} %broadcast_in_dim.12.index, f32[12,1,3312]{2,1,0:T(1,128)S(1)} %bitcast.27, s32[96,768]{1,0:T(8,128)S(1)} %copy-done.4, ...), custom_call_target="tpu_custom_call" | custom-call | flops 4000000000 | bytes 4194304 | tf_op jit(solution)/shard_map/coarse_bias/pallas_call | solution.py:508
  45.0 9.8 %coarse.1 = (bf16[288,384]{1,0:T(8,128)(2,1)S(1)}, bf16[2,64,384]{2,1,0:T(8,128)(2,1)S(1)}, bf16[2,32,384]{2,1,0:T(8,128)(2,1)S(1)}, bf16[2,32,384]{2,1,0:T(8,12...) custom-call(s32[576,1]{1,0:T(8,128)S(1)} %copy-done.15, ...), custom_call_target="tpu_custom_call" | custom-call | flops 6000000000 | bytes 4194304 | tf_op jit(solution)/shard_map/coarse/pallas_call | solution.py:508
  54.8 0.6 collective-permute-start.11
  55.4 1.6 collective-permute-start.13
  56.9 0.2 collective-permute-start.14
  57.2 0.0 collective-permute-start.10
  57.2 1.5 collective-permute-start.9
  58.7 1.0 fine_again.1
  59.8 0.0 copy-start.14
  59.8 0.0 copy-start.19
  59.8 1.3 coarse_gradients.1.coarse
  61.1 2.6 %collective-permute-done.11.rc = bf16[2,32,192]{2,1,0:T(8,128)(2,1)S(1)} collective-permute-done((bf16[2,32,192]{2,1,0:T(8,128)(2,1)S(1)}, bf16[2,32,192]{2,1,0:T(8,128)(2,1)S(1)}, u32[]{:S(2)}, u32[]{:S(2)}) %collective-permute-start.11) | collective-permute-done | bytes 24608 | tf_op jit(solution)/shard_map/ppermute | solution.py:531
  63.7 1.1 collective-permute-start.12
  64.8 1.8 %collective-permute-done.9.ra = bf16[2,128,192]{2,1,0:T(8,128)(2,1)S(1)} collective-permute-done((bf16[2,128,192]{2,1,0:T(8,128)(2,1)S(1)}, bf16[2,128,192]{2,1,0:T(8,128)(2,1)S(1)}, u32[]{:S(2)}, u32[]{:S(2)}) %collective-permute-start.9) | collective-permute-done | bytes 98336 | tf_op jit(solution)/shard_map/ppermute | solution.py:525
  66.6 8.7 %fine_backward.1 = (bf16[1152,192]{1,0:T(8,128)(2,1)S(1)}, bf16[2,128,192]{2,1,0:T(8,128)(2,1)S(1)}, bf16[2,64,192]{2,1,0:T(8,128)(2,1)S(1)}, bf16[2,32,192]{2,1,0:T(8,128)(2,1)S(1)}, bf16[4,1152,192]{2,1,0:T(8,128)(2,1)S(1)}) custom-call(s32[576,1]{1,0:T(8,128)S(1)} %copy-done.14, s32[224,1]{1,0:T(8,128)S(1)} %copy-done.19, ...), custom_call_target="tpu_custom_call" | custom-call | flops 6000000000 | bytes 4194304 | tf_op jit(solution)/shard_map/fine_backward/pallas_call | solution.py:508
  75.3 2.2 %fine_gradients.1 = bf16[8192,128]{1,0:T(8,128)(2,1)} custom-call(bf16[1152,192]{1,0:T(8,128)(2,1)S(1)} %get-tuple-element.88.kept_u, bf16[1152,192]{1,0:T(8,128)(2,1)S(1)} %get-tuple-element.89.kept_o, bf16[4,1152,192]{2,1,0:T(8,128)(2,1)S(1)} %get-tuple-element.100.kept, bf16[6912,128]{1,0:T(8,128)(2,1)S(1)} %coarse_gradients.1.coarse), custom_call_target="tpu_custom_call" | custom-call | flops 2000000000 | bytes 4194304 | tf_op jit(solution)/shard_map/fine_gradients/pallas_call | solution.py:508
  77.5 7.4 %all-to-all-start = ((bf16[128,64,128]{2,1,0:T(8,128)(2,1)}), bf16[128,64,128]{2,1,0:T(8,128)(2,1)S(1)}, u32[]{:S(2)}, u32[]{:S(2)}) async-start(bf16[128,64,128]{2,1,0:T(8,128)(2,1)} %bitcast.14), calls=%async_computation | async-start | bytes 4194304 | tf_op jit(solution)/shard_map/all_to_all | solution.py:558
  84.9 1.0 collective-permute-start.15
  85.9 2.8 %collective-permute-start.17 = (bf16[2,32,192]{2,1,0:T(8,128)(2,1)S(1)}, bf16[2,32,192]{2,1,0:T(8,128)(2,1)S(1)}, u32[]{:S(2)}, u32[]{:S(2)}) collective-permute-start(bf16[2,32,192]{2,1,0:T(8,128)(2,1)S(1)} %get-tuple-element.113), channel_id=1, source_target_pairs={{0,9},{1,10},{2,11},{3,12},{4,13},{5,14},{6,15},{7,8},{8,17},{9,18... | collective-permute-start | bytes 73736 | tf_op jit(solution)/shard_map/ppermute | solution.py:531
  88.7 29.3 %collective-permute-done.17.rc = bf16[2,32,192]{2,1,0:T(8,128)(2,1)S(1)} collective-permute-done((bf16[2,32,192]{2,1,0:T(8,128)(2,1)S(1)}, bf16[2,32,192]{2,1,0:T(8,128)(2,1)S(1)}, u32[]{:S(2)}, u32[]{:S(2)}) %collective-permute-start.17) | collective-permute-done | bytes 24608 | tf_op jit(solution)/shard_map/ppermute | solution.py:531
  118.1 0.5 add.13
  118.6 1.3 copy-done
  119.9 4.8 %all-to-all-start.1 = ((bf16[128,64,128]{2,1,0:T(8,128)(2,1)}), bf16[128,64,128]{2,1,0:T(8,128)(2,1)S(1)}, u32[]{:S(2)}, u32[]{:S(2)}) async-start(bf16[128,64,128]{2,1,0:T(8,128)(2,1)} %copy-done), calls=%async_computation.1 | async-start | bytes 4194304 | tf_op jit(solution)/shard_map/all_to_all | solution.py:561
  124.7 0.9 copy-done.28
  125.6 1.1 restore_coarse.1
  126.7 1.7 %restore_fine.1 = bf16[1152,192]{1,0:T(8,128)(2,1)} custom-call(s32[576,1]{1,0:T(8,128)S(1)} %copy-done.13, bf16[1152,192]{1,0:T(8,128)(2,1)S(1)} %get-tuple-element.109.own, bf16[2,128,192]{2,1,0:T(8,128)(2,1)S(1)} %collective-permute-done.15.ra, bf16[2,64,192]{2,1,0:T(8,128)(2,1)S(1)} %collective-permute-done.16.rb, ...), custom_call_target="tpu_custom_call" | custom-call | flops 1000000000 | bytes 4194304 | tf_op jit(solution)/shard_map/restore_fine/pallas_call | solution.py:508
  128.4 26.1 %all-to-all-done.1 = bf16[128,64,128]{2,1,0:T(8,128)(2,1)S(1)} async-done(((bf16[128,64,128]{2,1,0:T(8,128)(2,1)}), bf16[128,64,128]{2,1,0:T(8,128)(2,1)S(1)}, u32[]{:S(2)}, u32[]{:S(2)}) %all-to-all-start.1) | async-done | bytes 2097184 | tf_op jit(solution)/shard_map/all_to_all | solution.py:561
  154.5 2.1 %finish.1 = (f32[192,576]{1,0:T(8,128)}, f32[192,192]{1,0:T(8,128)}, f32[768,384]{1,0:T(8,128)}, f32[384,1152]{1,0:T(8,128)}, f32[384,384]{1,0:T(8,128)}) custom-call(bf16[8192,128]{1,0:T(8,128)(2,1)S(1)} %bitcast.21), custom_call_target="tpu_custom_call" | custom-call | flops 1000000000 | bytes 4194304 | tf_op jit(solution)/shard_map/finish/pallas_call | solution.py:508
  (80 shorter events, 0.2 us)
Async XLA Ops:
  0.6 13.7 %copy-start.35 = (f32[3,6]{1,0:T(4,128)S(1)}, f32[3,6]{1,0:T(4,128)}, u32[]{:S(2)}) copy-start(f32[3,6]{1,0:T(4,128)} %param.39) | copy-start | bytes 220
  0.6 13.8 %copy-start.36 = (f32[3,12]{1,0:T(4,128)S(1)}, f32[3,12]{1,0:T(4,128)}, u32[]{:S(2)}) copy-start(f32[3,12]{1,0:T(4,128)} %param.46) | copy-start | bytes 436
  0.7 13.9 %copy-start.33 = (s32[144,144]{1,0:T(8,128)S(1)}, s32[144,144]{1,0:T(8,128)}, u32[]{:S(2)}) copy-start(s32[144,144]{1,0:T(8,128)} %param.49) | copy-start | bytes 248836
  0.7 14.4 %copy-start.4 = (s32[96,768]{1,0:T(8,128)S(1)}, s32[96,768]{1,0:T(8,128)}, u32[]{:S(2)}) copy-start(s32[96,768]{1,0:T(8,128)} %surface.3) | copy-start | bytes 884740
  0.7 14.4 %copy-start.8 = (f32[1,2,3312,6]{2,1,3,0:T(2,128)S(1)}, f32[1,2,3312,6]{2,1,3,0:T(2,128)}, u32[]{:S(2)}) copy-start(f32[1,2,3312,6]{2,1,3,0:T(2,128)} %param.38) | copy-start | bytes 476932
  0.7 14.4 %copy-start.12 = (s32[96]{0:T(128)S(1)}, s32[96]{0:T(128)}, u32[]{:S(2)}) copy-start(s32[96]{0:T(128)} %valid.3) | copy-start | bytes 1156
  0.7 14.4 %copy-start.17 = (s32[576,1]{1,0:T(8,128)S(1)}, s32[576,1]{1,0:T(8,128)}, u32[]{:S(2)}) copy-start(s32[576,1]{1,0:T(8,128)} %constant.50.clone.col) | copy-start | bytes 6916
  0.7 14.4 %copy-start.18 = (s32[576,1]{1,0:T(8,128)S(1)}, s32[576,1]{1,0:T(8,128)}, u32[]{:S(2)}) copy-start(s32[576,1]{1,0:T(8,128)} %constant.49.clone.row) | copy-start | bytes 6916
  3.3 20.1 %collective-permute-start.2 = (bf16[2,32,192]{2,1,0:T(8,128)(2,1)}, bf16[2,32,192]{2,1,0:T(8,128)(2,1)S(1)}, u32[]{:S(2)}, u32[]{:S(2)}) collective-permute-start(bf16[2,32,192]{2,1,0:T(8,128)(2,1)} %get-tuple-element.67), channel_id=1, source_target_pairs={{0,127},{1,120},{2,121},{3,122},{4,123},{5,124},{6,125},{7,126},{8... | collective-permute-start | bytes 73736 | tf_op jit(solution)/shard_map/ppermute | solution.py:531
  11.6 25.5 %collective-permute-start.7 = (bf16[2,32,384]{2,1,0:T(8,128)(2,1)}, bf16[2,32,384]{2,1,0:T(8,128)(2,1)S(1)}, u32[]{:S(2)}, u32[]{:S(2)}) collective-permute-start(bf16[2,32,384]{2,1,0:T(8,128)(2,1)} %get-tuple-element.76), channel_id=1, source_target_pairs={{0,120},{8,0},{16,8},{24,16},{32,24},{40,32},{48,40},{56,48},{64,5... | collective-permute-start | bytes 147464 | tf_op jit(solution)/shard_map/ppermute | solution.py:523
  13.3 31.5 %collective-permute-start.8 = (bf16[2,32,384]{2,1,0:T(8,128)(2,1)}, bf16[2,32,384]{2,1,0:T(8,128)(2,1)S(1)}, u32[]{:S(2)}, u32[]{:S(2)}) collective-permute-start(bf16[2,32,384]{2,1,0:T(8,128)(2,1)} %get-tuple-element.77), channel_id=1, source_target_pairs={{0,127},{1,120},{2,121},{3,122},{4,123},{5,124},{6,125},{7,126},{8... | collective-permute-start | bytes 147464 | tf_op jit(solution)/shard_map/ppermute | solution.py:531
  13.3 10.6 %collective-permute-start.1 = (bf16[2,64,192]{2,1,0:T(8,128)(2,1)}, bf16[2,64,192]{2,1,0:T(8,128)(2,1)S(1)}, u32[]{:S(2)}, u32[]{:S(2)}) collective-permute-start(bf16[2,64,192]{2,1,0:T(8,128)(2,1)} %get-tuple-element.66), channel_id=1, source_target_pairs={{0,120},{8,0},{16,8},{24,16},{32,24},{40,32},{48,40},{56,48},{64,5... | collective-permute-start | bytes 147464 | tf_op jit(solution)/shard_map/ppermute | solution.py:523
  14.3 9.6 %collective-permute-start = (bf16[2,128,192]{2,1,0:T(8,128)(2,1)}, bf16[2,128,192]{2,1,0:T(8,128)(2,1)S(1)}, u32[]{:S(2)}, u32[]{:S(2)}) collective-permute-start(bf16[2,128,192]{2,1,0:T(8,128)(2,1)} %get-tuple-element.65), channel_id=1, source_target_pairs={{0,7},{1,0},{2,1},{3,2},{4,3},{5,4},{6,5},{7,6},{8,15},{9,8},{10,9... | collective-permute-start | bytes 294920 | tf_op jit(solution)/shard_map/ppermute | solution.py:525
  15.1 8.2 %copy-start.37 = (f32[384]{0:T(512)S(1)}, f32[384]{0:T(512)}, u32[]{:S(2)}) copy-start(f32[384]{0:T(512)} %param.42) | copy-start | bytes 4612
  15.1 8.2 %copy-start.34 = (f32[768]{0:T(1024)S(1)}, f32[768]{0:T(1024)}, u32[]{:S(2)}) copy-start(f32[768]{0:T(1024)} %param.40) | copy-start | bytes 9220
  15.1 8.3 %copy-start.38 = (bf16[2,64,384]{2,1,0:T(8,128)(2,1)S(1)}, bf16[2,64,384]{2,1,0:T(8,128)(2,1)}, u32[]{:S(2)}) copy-start(bf16[2,64,384]{2,1,0:T(8,128)(2,1)} %get-tuple-element.75) | copy-start | bytes 294916
  15.1 8.8 %copy-start.2 = (bf16[2,12,48,192]{3,2,1,0:T(8,128)(2,1)S(1)}, bf16[2,12,48,192]{3,2,1,0:T(8,128)(2,1)}, u32[]{:S(2)}) copy-start(bf16[2,12,48,192]{3,2,1,0:T(8,128)(2,1)} %param.33) | copy-start | bytes 1327108
  15.1 8.8 %copy-start.6 = (bf16[192,576]{1,0:T(8,128)(2,1)S(1)}, bf16[192,576]{1,0:T(8,128)(2,1)}, u32[]{:S(2)}) copy-start(bf16[192,576]{1,0:T(8,128)(2,1)} %project.7) | copy-start | bytes 663556
  15.2 8.8 %copy-start.10 = (bf16[192,192]{1,0:T(8,128)(2,1)S(1)}, bf16[192,192]{1,0:T(8,128)(2,1)}, u32[]{:S(2)}) copy-start(bf16[192,192]{1,0:T(8,128)(2,1)} %combine.5) | copy-start | bytes 221188
  15.2 8.8 %copy-start.11 = (f32[192]{0:T(256)S(1)}, f32[192]{0:T(256)}, u32[]{:S(2)}) copy-start(f32[192]{0:T(256)} %param.35) | copy-start | bytes 2308
  15.2 8.8 %copy-start.16 = (s32[576,1]{1,0:T(8,128)S(1)}, s32[576,1]{1,0:T(8,128)}, u32[]{:S(2)}) copy-start(s32[576,1]{1,0:T(8,128)} %constant.51.clone.take) | copy-start | bytes 6916
  15.2 8.8 %copy-start.21 = (s32[224,1]{1,0:T(8,128)S(1)}, s32[224,1]{1,0:T(8,128)}, u32[]{:S(2)}) copy-start(s32[224,1]{1,0:T(8,128)} %constant.52.clone.sel) | copy-start | bytes 2692
  21.8 0.7 copy-start.29
  22.6 0.7 copy-start.31
  23.4 21.5 %collective-permute-start.6 = (bf16[2,64,384]{2,1,0:T(8,128)(2,1)S(1)}, bf16[2,64,384]{2,1,0:T(8,128)(2,1)S(1)}, u32[]{:S(2)}, u32[]{:S(2)}) collective-permute-start(bf16[2,64,384]{2,1,0:T(8,128)(2,1)S(1)} %copy-done.38), channel_id=1, source_target_pairs={{0,7},{1,0},{2,1},{3,2},{4,3},{5,4},{6,5},{7,6},{8,15},{9,8},{10,9... | collective-permute-start | bytes 294920 | tf_op jit(solution)/shard_map/ppermute | solution.py:525
  24.0 1.0 copy-start.30
  24.9 0.9 copy-start.32
  25.8 12.5 %copy-start.9 = (f32[1,1,3312,12]{2,1,3,0:T(1,128)S(1)}, f32[1,1,3312,12]{2,1,3,0:T(1,128)}, u32[]{:S(2)}) copy-start(f32[1,1,3312,12]{2,1,3,0:T(1,128)} %param.45) | copy-start | bytes 476932
  25.8 12.5 %copy-start.24 = (s32[144,1]{1,0:T(8,128)S(1)}, s32[144,1]{1,0:T(8,128)}, u32[]{:S(2)}) copy-start(s32[144,1]{1,0:T(8,128)} %constant.54.clone.col) | copy-start | bytes 1732
  25.8 12.5 %copy-start.25 = (s32[144,1]{1,0:T(8,128)S(1)}, s32[144,1]{1,0:T(8,128)}, u32[]{:S(2)}) copy-start(s32[144,1]{1,0:T(8,128)} %constant.53.clone.row) | copy-start | bytes 1732
  34.1 10.8 %collective-permute-start.3 = (bf16[2,128,192]{2,1,0:T(8,128)(2,1)S(1)}, bf16[2,128,192]{2,1,0:T(8,128)(2,1)S(1)}, u32[]{:S(2)}, u32[]{:S(2)}) collective-permute-start(bf16[2,128,192]{2,1,0:T(8,128)(2,1)S(1)} %get-tuple-element.72), channel_id=1, source_target_pairs={{0,7},{1,0},{2,1},{3,2},{4,3},{5,4},{6,5},{7,6},{8,15},{9,8},{10,9... | collective-permute-start | bytes 294920 | tf_op jit(solution)/shard_map/ppermute | solution.py:525
  37.1 7.8 %collective-permute-start.5 = (bf16[2,32,192]{2,1,0:T(8,128)(2,1)S(1)}, bf16[2,32,192]{2,1,0:T(8,128)(2,1)S(1)}, u32[]{:S(2)}, u32[]{:S(2)}) collective-permute-start(bf16[2,32,192]{2,1,0:T(8,128)(2,1)S(1)} %get-tuple-element.74), channel_id=1, source_target_pairs={{0,127},{1,120},{2,121},{3,122},{4,123},{5,124},{6,125},{7,126},{8... | collective-permute-start | bytes 73736 | tf_op jit(solution)/shard_map/ppermute | solution.py:531
  37.1 7.8 %collective-permute-start.4 = (bf16[2,64,192]{2,1,0:T(8,128)(2,1)S(1)}, bf16[2,64,192]{2,1,0:T(8,128)(2,1)S(1)}, u32[]{:S(2)}, u32[]{:S(2)}) collective-permute-start(bf16[2,64,192]{2,1,0:T(8,128)(2,1)S(1)} %get-tuple-element.73), channel_id=1, source_target_pairs={{0,120},{8,0},{16,8},{24,16},{32,24},{40,32},{48,40},{56,48},{64,5... | collective-permute-start | bytes 147464 | tf_op jit(solution)/shard_map/ppermute | solution.py:523
  38.4 6.6 %copy-start.1 = (bf16[384,1152]{1,0:T(8,128)(2,1)S(1)}, bf16[384,1152]{1,0:T(8,128)(2,1)}, u32[]{:S(2)}) copy-start(bf16[384,1152]{1,0:T(8,128)(2,1)} %project.5) | copy-start | bytes 2654212
  38.4 6.6 %copy-start.3 = (bf16[768,384]{1,0:T(8,128)(2,1)S(1)}, bf16[768,384]{1,0:T(8,128)(2,1)}, u32[]{:S(2)}) copy-start(bf16[768,384]{1,0:T(8,128)(2,1)} %merge_weight.1) | copy-start | bytes 1769476
  38.4 6.6 %copy-start.5 = (bf16[384,384]{1,0:T(8,128)(2,1)S(1)}, bf16[384,384]{1,0:T(8,128)(2,1)}, u32[]{:S(2)}) copy-start(bf16[384,384]{1,0:T(8,128)(2,1)} %combine.4) | copy-start | bytes 884740
  38.4 6.6 %copy-start.7 = (bf16[2,6,24,384]{3,2,1,0:T(8,128)(2,1)S(1)}, bf16[2,6,24,384]{3,2,1,0:T(8,128)(2,1)}, u32[]{:S(2)}) copy-start(bf16[2,6,24,384]{3,2,1,0:T(8,128)(2,1)} %param.34) | copy-start | bytes 663556
  38.4 6.6 %copy-start.15 = (s32[576,1]{1,0:T(8,128)S(1)}, s32[576,1]{1,0:T(8,128)}, u32[]{:S(2)}) copy-start(s32[576,1]{1,0:T(8,128)} %constant.55.clone.take) | copy-start | bytes 6916
  38.4 6.6 %copy-start.20 = (s32[224,1]{1,0:T(8,128)S(1)}, s32[224,1]{1,0:T(8,128)}, u32[]{:S(2)}) copy-start(s32[224,1]{1,0:T(8,128)} %constant.58.clone.fsel) | copy-start | bytes 2692
  38.4 6.5 %copy-start.23 = (s32[144,1]{1,0:T(8,128)S(1)}, s32[144,1]{1,0:T(8,128)}, u32[]{:S(2)}) copy-start(s32[144,1]{1,0:T(8,128)} %constant.56.clone.ctake) | copy-start | bytes 1732
  38.5 6.5 %copy-start.26 = (s32[128,1]{1,0:T(8,128)S(1)}, s32[128,1]{1,0:T(8,128)}, u32[]{:S(2)}) copy-start(s32[128,1]{1,0:T(8,128)} %constant.57.clone.csel) | copy-start | bytes 1540
  54.8 4.9 %copy-start.27 = (bf16[288,384]{1,0:T(8,128)(2,1)}, bf16[288,384]{1,0:T(8,128)(2,1)S(1)}, u32[]{:S(2)}) copy-start(bf16[288,384]{1,0:T(8,128)(2,1)S(1)} %get-tuple-element.82.own) | copy-start | bytes 663556
  54.8 8.8 %collective-permute-start.11 = (bf16[2,32,192]{2,1,0:T(8,128)(2,1)S(1)}, bf16[2,32,192]{2,1,0:T(8,128)(2,1)S(1)}, u32[]{:S(2)}, u32[]{:S(2)}) collective-permute-start(bf16[2,32,192]{2,1,0:T(8,128)(2,1)S(1)} %get-tuple-element.93), channel_id=1, source_target_pairs={{0,9},{1,10},{2,11},{3,12},{4,13},{5,14},{6,15},{7,8},{8,17},{9,18... | collective-permute-start | bytes 73736 | tf_op jit(solution)/shard_map/ppermute | solution.py:531
  55.4 22.1 %collective-permute-start.13 = (bf16[2,32,384]{2,1,0:T(8,128)(2,1)S(1)}, bf16[2,32,384]{2,1,0:T(8,128)(2,1)S(1)}, u32[]{:S(2)}, u32[]{:S(2)}) collective-permute-start(bf16[2,32,384]{2,1,0:T(8,128)(2,1)S(1)} %get-tuple-element.104), channel_id=1, source_target_pairs={{0,8},{8,16},{16,24},{24,32},{32,40},{40,48},{48,56},{56,64},{64,7... | collective-permute-start | bytes 147464 | tf_op jit(solution)/shard_map/ppermute | solution.py:523
  56.9 20.6 %collective-permute-start.14 = (bf16[2,32,384]{2,1,0:T(8,128)(2,1)S(1)}, bf16[2,32,384]{2,1,0:T(8,128)(2,1)S(1)}, u32[]{:S(2)}, u32[]{:S(2)}) collective-permute-start(bf16[2,32,384]{2,1,0:T(8,128)(2,1)S(1)} %get-tuple-element.105), channel_id=1, source_target_pairs={{0,9},{1,10},{2,11},{3,12},{4,13},{5,14},{6,15},{7,8},{8,17},{9,18... | collective-permute-start | bytes 147464 | tf_op jit(solution)/shard_map/ppermute | solution.py:531
  57.2 7.6 %collective-permute-start.10 = (bf16[2,64,192]{2,1,0:T(8,128)(2,1)S(1)}, bf16[2,64,192]{2,1,0:T(8,128)(2,1)S(1)}, u32[]{:S(2)}, u32[]{:S(2)}) collective-permute-start(bf16[2,64,192]{2,1,0:T(8,128)(2,1)S(1)} %get-tuple-element.92), channel_id=1, source_target_pairs={{0,8},{8,16},{16,24},{24,32},{32,40},{40,48},{48,56},{56,64},{64,7... | collective-permute-start | bytes 147464 | tf_op jit(solution)/shard_map/ppermute | solution.py:523
  57.2 9.4 %collective-permute-start.9 = (bf16[2,128,192]{2,1,0:T(8,128)(2,1)S(1)}, bf16[2,128,192]{2,1,0:T(8,128)(2,1)S(1)}, u32[]{:S(2)}, u32[]{:S(2)}) collective-permute-start(bf16[2,128,192]{2,1,0:T(8,128)(2,1)S(1)} %get-tuple-element.91), channel_id=1, source_target_pairs={{0,1},{1,2},{2,3},{3,4},{4,5},{5,6},{6,7},{7,0},{8,9},{9,10},{10,1... | collective-permute-start | bytes 294920 | tf_op jit(solution)/shard_map/ppermute | solution.py:525
  59.8 6.8 %copy-start.14 = (s32[576,1]{1,0:T(8,128)S(1)}, s32[576,1]{1,0:T(8,128)}, u32[]{:S(2)}) copy-start(s32[576,1]{1,0:T(8,128)} %constant.59.clone.take) | copy-start | bytes 6916
  59.8 6.8 %copy-start.19 = (s32[224,1]{1,0:T(8,128)S(1)}, s32[224,1]{1,0:T(8,128)}, u32[]{:S(2)}) copy-start(s32[224,1]{1,0:T(8,128)} %constant.60.clone.sel) | copy-start | bytes 2692
  63.7 13.8 %collective-permute-start.12 = (bf16[2,64,384]{2,1,0:T(8,128)(2,1)S(1)}, bf16[2,64,384]{2,1,0:T(8,128)(2,1)S(1)}, u32[]{:S(2)}, u32[]{:S(2)}) collective-permute-start(bf16[2,64,384]{2,1,0:T(8,128)(2,1)S(1)} %get-tuple-element.103), channel_id=1, source_target_pairs={{0,1},{1,2},{2,3},{3,4},{4,5},{5,6},{6,7},{7,0},{8,9},{9,10},{10,1... | collective-permute-start | bytes 294920 | tf_op jit(solution)/shard_map/ppermute | solution.py:525
  77.5 40.6 %all-to-all-start = ((bf16[128,64,128]{2,1,0:T(8,128)(2,1)}), bf16[128,64,128]{2,1,0:T(8,128)(2,1)S(1)}, u32[]{:S(2)}, u32[]{:S(2)}) async-start(bf16[128,64,128]{2,1,0:T(8,128)(2,1)} %bitcast.14), calls=%async_computation | async-start | bytes 4194304 | tf_op jit(solution)/shard_map/all_to_all | solution.py:558
  84.9 33.1 %collective-permute-start.15 = (bf16[2,128,192]{2,1,0:T(8,128)(2,1)S(1)}, bf16[2,128,192]{2,1,0:T(8,128)(2,1)S(1)}, u32[]{:S(2)}, u32[]{:S(2)}) collective-permute-start(bf16[2,128,192]{2,1,0:T(8,128)(2,1)S(1)} %get-tuple-element.111), channel_id=1, source_target_pairs={{0,1},{1,2},{2,3},{3,4},{4,5},{5,6},{6,7},{7,0},{8,9},{9,10},{10,1... | collective-permute-start | bytes 294920 | tf_op jit(solution)/shard_map/ppermute | solution.py:525
  85.9 32.1 %collective-permute-start.16 = (bf16[2,64,192]{2,1,0:T(8,128)(2,1)S(1)}, bf16[2,64,192]{2,1,0:T(8,128)(2,1)S(1)}, u32[]{:S(2)}, u32[]{:S(2)}) collective-permute-start(bf16[2,64,192]{2,1,0:T(8,128)(2,1)S(1)} %get-tuple-element.112), channel_id=1, source_target_pairs={{0,8},{8,16},{16,24},{24,32},{32,40},{40,48},{48,56},{56,64},{64,7... | collective-permute-start | bytes 147464 | tf_op jit(solution)/shard_map/ppermute | solution.py:523
  85.9 32.1 %collective-permute-start.17 = (bf16[2,32,192]{2,1,0:T(8,128)(2,1)S(1)}, bf16[2,32,192]{2,1,0:T(8,128)(2,1)S(1)}, u32[]{:S(2)}, u32[]{:S(2)}) collective-permute-start(bf16[2,32,192]{2,1,0:T(8,128)(2,1)S(1)} %get-tuple-element.113), channel_id=1, source_target_pairs={{0,9},{1,10},{2,11},{3,12},{4,13},{5,14},{6,15},{7,8},{8,17},{9,18... | collective-permute-start | bytes 73736 | tf_op jit(solution)/shard_map/ppermute | solution.py:531
  118.5 1.3 copy-start
  119.9 4.8 %copy-start.22 = (s32[144,1]{1,0:T(8,128)S(1)}, s32[144,1]{1,0:T(8,128)}, u32[]{:S(2)}) copy-start(s32[144,1]{1,0:T(8,128)} %constant.61.clone.take) | copy-start | bytes 1732
  119.9 34.6 %all-to-all-start.1 = ((bf16[128,64,128]{2,1,0:T(8,128)(2,1)}), bf16[128,64,128]{2,1,0:T(8,128)(2,1)S(1)}, u32[]{:S(2)}, u32[]{:S(2)}) async-start(bf16[128,64,128]{2,1,0:T(8,128)(2,1)} %copy-done), calls=%async_computation.1 | async-start | bytes 4194304 | tf_op jit(solution)/shard_map/all_to_all | solution.py:561
  124.7 0.9 copy-start.28
  125.6 1.1 copy-start.13

commit v3 on v2

--- a/solution.py
+++ b/solution.py
@@ -15,7 +15,8 @@
 HEAD = 32
 SCALE = HEAD ** (-0.5)
 BLOCKED = -1e30
-UNROLL = 4
+UNROLL = 2
+TOGETHER = 2
 NT = (((1,), (1,)), ((), ()))
 TN = (((0,), (0,)), ((), ()))
 NN = (((1,), (0,)), ((), ()))
@@ -109,35 +110,55 @@
     ]
 
 
-def spread_heads(x, masks):
-    return jnp.concatenate([x * m for m in masks], axis=0).astype(BF16)
-
-
-def fold_heads(x, masks):
+def lane_groups(channels):
+    return [
+        (slice(c, min(c + 128, channels)), slice(0, 72 * ((min(c + 128, channels) - c) // HEAD)))
+        for c in range(0, channels, 128)
+    ]
+
+
+def spread_heads(x):
+    return jnp.concatenate([x * m for m in head_masks(x.shape[1])], axis=0).astype(BF16)
+
+
+def fold_heads(x):
+    masks = head_masks(x.shape[1])
     out = x[0:72] * masks[0]
     for h in range(1, len(masks)):
         out = out + x[72 * h : 72 * (h + 1)] * masks[h]
     return out
 
 
-def weights_of(k16, qbig, kinds16, types16, bias):
-    x = mm(k16, qbig, NT) * SCALE + (mm(kinds16, types16) + bias)
-    e = jnp.exp(x - jnp.max(x, axis=0, keepdims=True))
-    return (e * (1.0 / jnp.sum(e, axis=0, keepdims=True))).astype(BF16)
-
-
-def attention_back(q, k, v, p16, do, masks):
-    k16 = k.astype(BF16)
-    dobig = spread_heads(do, masks)
-    qbig = spread_heads(q, masks)
-    p = p16.astype(F32)
-    dv = mm(p16, dobig)
-    dp = round16(mm(v.astype(BF16), dobig, NT))
-    pd = p * dp
-    ds = ((pd - p * jnp.sum(pd, axis=0, keepdims=True)) * SCALE).astype(BF16)
-    dq = fold_heads(mm(ds, k16, TN), masks)
-    dk = mm(ds, qbig)
-    return dq, dk, dv
+def attention_forward(blocks, bias, scores):
+    spread = [spread_heads(q) for q, _, _ in blocks]
+    x = [mm(k.astype(BF16), s, NT) * SCALE for (_, k, _), s in zip(blocks, spread)]
+    x = [a + (t + b) for a, t, b in zip(x, scores, bias)]
+    e = [jnp.exp(a - jnp.max(a, axis=0, keepdims=True)) for a in x]
+    p = [(a * (1.0 / jnp.sum(a, axis=0, keepdims=True))).astype(BF16) for a in e]
+    mixed = [mm(a, v.astype(BF16), TN) for a, (_, _, v) in zip(p, blocks)]
+    return p, [fold_heads(m) for m in mixed]
+
+
+def attention_back(blocks, weights, deltas):
+    spread = [spread_heads(d) for d in deltas]
+    dp = [mm(v.astype(BF16), d, NT) for (_, _, v), d in zip(blocks, spread)]
+    dv = [mm(p, d) for p, d in zip(weights, spread)]
+    ds = []
+    for p16, d in zip(weights, dp):
+        p = p16.astype(F32)
+        pd = p * round16(d)
+        ds.append(((pd - p * jnp.sum(pd, axis=0, keepdims=True)) * SCALE).astype(BF16))
+    dq = [mm(d, k.astype(BF16), TN) for d, (_, k, _) in zip(ds, blocks)]
+    dk = [mm(d, spread_heads(q)) for d, (q, _, _) in zip(ds, blocks)]
+    return [(fold_heads(x), y, z) for x, y, z in zip(dq, dk, dv)]
+
+
+def window_rows(windows, first, count):
+    return [
+        (level, first + i, pl.ds(pl.multiple_of((level * windows + first + i) * 72, 8), 72))
+        for i in range(count)
+        for level in range(2)
+    ]
 
 
 def moments(parts):
@@ -184,11 +205,11 @@
 
 
 def bias_kernel(
-    level_rows, place, valid, index, table, surface, types, row, col,
-    bias, kinds, typed, raw, parts,
+    level_rows, size, place, valid, index, table, bias, raw, parts,
 ):
     lat, lon, lats = place[0], place[1], place[2]
-    windows, heads = bias.shape[1], bias.shape[3] // 72
+    windows, heads = bias.shape[1], table.shape[0]
+    run = bias.shape[4] // 72
     entries = table.shape[2]
     chunks = -(-entries // 128)
     count = windows * heads
@@ -238,7 +259,7 @@
     query = lax.broadcasted_iota(jnp.int32, (72, 72), 1)
     key_row = sum(jnp.where(key >= 12 * r, 1, 0) for r in range(1, 6))
     apart = jnp.where((key >= 36) != (query >= 36), 1, 0)
-    rows, columns = surface.shape[0] // level_rows, surface.shape[1] // level_rows
+    rows = size // level_rows
     at_end = jnp.where(lat == lats - 1, 1, 0)
     for rw in range(windows):
         real = jnp.zeros((72, 72), jnp.int32)
@@ -254,12 +275,15 @@
         for level in range(2):
             for h in range(heads):
                 at = (rw * heads + h) * 144 + level * 72
-                bias[level, rw, :, 72 * h : 72 * (h + 1)] = jnp.where(
+                bias[level, rw, h // run, :, 72 * (h % run) : 72 * (h % run + 1)] = jnp.where(
                     good, raw[at : at + 72, :][:, :72], BLOCKED
                 )
 
+
+def kinds_of(lat, lon, windows, level_rows, surface, row, col):
+    rows, columns = surface.shape[0] // level_rows, surface.shape[1] // level_rows
     codes = surface[...].astype(F32).astype(BF16)
-    tokens = kinds.shape[0]
+    tokens = row.shape[0]
     line = row[...] + lat * (6 * windows)
     line = jnp.where(line >= rows, line - rows, line) * level_rows
     spot = col[...] + lon * (12 * (tokens // 72 // windows))
@@ -268,22 +292,23 @@
     lanes = lax.broadcasted_iota(jnp.int32, lines.shape, 1)
     code = jnp.sum(jnp.where(lanes == spot, lines, 0.0), axis=1, keepdims=True).astype(jnp.int32)
     lanes = lax.broadcasted_iota(jnp.int32, (tokens, 128), 1)
-    kinds[...] = jnp.where((lanes == code) | (lanes == code + 3) | (lanes == code + 6), 1.0, 0.0)
-
+    return jnp.where((lanes == code) | (lanes == code + 3) | (lanes == code + 6), 1.0, 0.0)
+
+
+def types_of(types):
     t = types[...]
     high = round16(t)
     middle = round16(t - high)
     lanes = lax.broadcasted_iota(jnp.int32, t.shape, 1)
     split = jnp.where(lanes < 3, high, jnp.where(lanes < 6, middle, t - high - middle))
-    typed[...] = jnp.concatenate(
-        [jnp.broadcast_to(split[h : h + 1], (72, 128)) for h in range(heads)], axis=0
-    ).T.astype(BF16)
+    rows = [jnp.broadcast_to(split[h : h + 1], (72, 128)) for h in range(t.shape[0])]
+    return [jnp.concatenate(rows[h : h + 4], axis=0).T.astype(BF16) for h in range(0, len(rows), 4)]
 
 
 def fine_forward_kernel(
-    take, sel, tokens, ra, rb, rc, gain, project, combine, bias, kinds, types,
+    place, take, sel, tokens, ra, rb, rc, gain, project, combine, bias, surface, types, row, col,
     output, sa, sb, sc, kept_x, kept_p, kept_o,
-    q_s, k_s, v_s, o_s,
+    q_s, k_s, v_s, o_s, kinds,
 ):
     n = take.shape[0]
     width = tokens.shape[1]
@@ -300,23 +325,29 @@
     u = (centred * inverse * gain[...]).astype(BF16)
     for i, scratch in enumerate((q_s, k_s, v_s)):
         scratch[...] = round16(mm(u, project[:, i * width : (i + 1) * width]))
-    masks = head_masks(width)
     windows = n // 72
     across = windows // bias.shape[1]
-    types16 = types[...]
-
-    def window(w, carry):
-        kinds16 = kinds[pl.ds(pl.multiple_of(w * 72, 8), 72), :].astype(BF16)
-        for level in range(2):
-            b = level * windows + w
-            rows = pl.ds(pl.multiple_of(b * 72, 8), 72)
-            qbig = spread_heads(q_s[rows, :], masks)
-            p = weights_of(k_s[rows, :].astype(BF16), qbig, kinds16, types16, bias[level, w // across])
-            kept_p[b] = p
-            o_s[rows, :] = fold_heads(mm(p, v_s[rows, :].astype(BF16), TN), masks)
+    types16 = types_of(types)
+    kinds[...] = kinds_of(place[0], place[1], bias.shape[1], 1, surface, row, col)
+
+    def window(i, carry):
+        first = i * TOGETHER
+        places = window_rows(windows, first, TOGETHER)
+        work = [(place, g, lanes, n_g) for place in places for g, (lanes, n_g) in enumerate(lane_groups(width))]
+        terms = []
+        for j in range(TOGETHER):
+            kinds16 = kinds[pl.ds(pl.multiple_of((first + j) * 72, 8), 72), :].astype(BF16)
+            terms += [mm(kinds16, t) for t in types16] * 2
+        p, o = attention_forward(
+            [(q_s[x[2], lanes], k_s[x[2], lanes], v_s[x[2], lanes]) for x, _, lanes, _ in work],
+            [bias[x[0], x[1] // across, 0, :, 288 * g : 288 * g + n_g.stop] for x, g, _, n_g in work], terms,
+        )
+        for ((level, w, rows), g, lanes, n_g), a, x in zip(work, p, o):
+            kept_p[level * windows + w, g, :, n_g] = a
+            o_s[rows, lanes] = x
         return carry
 
-    lax.fori_loop(0, windows, window, 0, unroll=UNROLL)
+    lax.fori_loop(0, windows // TOGETHER, window, 0, unroll=UNROLL)
     o16 = o_s[...].astype(BF16)
     kept_o[...] = o16
     out = (x + mm(o16, combine[...])).astype(BF16)
@@ -326,8 +357,8 @@
 
 
 def coarse_kernel(
-    take, ctake, csel, fsel, fine, ra, rb, rc, cot, da, db, dc,
-    merge_gain, merge_weight, gain, project, combine, bias, kinds, types,
+    place, take, ctake, csel, fsel, fine, ra, rb, rc, cot, da, db, dc,
+    merge_gain, merge_weight, gain, project, combine, bias, surface, types, row, col,
     output, oa, ob, oc, delta_fine, sa, sb, sc, kept_merged, kept,
     q_s, k_s, v_s, o_s, do_s, dq_s, dk_s, dv_s,
 ):
@@ -364,24 +395,23 @@
     k_s[...] = round16(mm(u, wk))
     v_s[...] = round16(mm(u, wv))
     do_s[...] = round16(mm(d16, combine[...], NT))
-    masks = head_masks(width)
     windows = quarter // 72
-    types16 = types[...]
-
-    def window(w, carry):
-        kinds16 = kinds[pl.ds(pl.multiple_of(w * 72, 8), 72), :].astype(BF16)
-        for level in range(2):
-            rows = pl.ds(pl.multiple_of((level * windows + w) * 72, 8), 72)
-            q, k, v = q_s[rows, :], k_s[rows, :], v_s[rows, :]
-            p = weights_of(k.astype(BF16), spread_heads(q, masks), kinds16, types16, bias[level, 0])
-            o_s[rows, :] = fold_heads(mm(p, v.astype(BF16), TN), masks)
-            dq, dk, dv = attention_back(q, k, v, p, do_s[rows, :], masks)
-            dq_s[rows, :] = dq
-            dk_s[rows, :] = dk
-            dv_s[rows, :] = dv
-        return carry
-
-    lax.fori_loop(0, windows, window, 0, unroll=2)
+    types16 = types_of(types)
+    kinds = kinds_of(place[0], place[1], 1, 2, surface, row, col)
+
+    places = window_rows(windows, 0, windows)
+    work = [(place, g, lanes, n_g) for place in places for g, (lanes, n_g) in enumerate(lane_groups(width))]
+    blocks = [(q_s[x[2], lanes], k_s[x[2], lanes], v_s[x[2], lanes]) for x, _, lanes, _ in work]
+    terms = []
+    for j in range(windows):
+        terms += [mm(kinds[72 * j : 72 * (j + 1), :].astype(BF16), t) for t in types16] * 2
+    p, o = attention_forward(blocks, [bias[x[0], 0, g, :, n_g] for x, g, _, n_g in work], terms)
+    back = attention_back(blocks, p, [do_s[x[2], lanes] for x, _, lanes, _ in work])
+    for ((_, _, rows), _, lanes, _), mixed, (dq, dk, dv) in zip(work, o, back):
+        o_s[rows, lanes] = mixed
+        dq_s[rows, lanes] = dq
+        dk_s[rows, lanes] = dk
+        dv_s[rows, lanes] = dv
     o16 = o_s[...].astype(BF16)
     out = (x + mm(o16, combine[...])).astype(BF16)
     output[...] = out
@@ -445,22 +475,23 @@
     )
     d16 = d.astype(BF16)
     do_s[...] = round16(mm(d16, combine[...], NT))
-    masks = head_masks(width)
     windows = n // 72
 
-    def window(w, carry):
-        for level in range(2):
-            b = level * windows + w
-            rows = pl.ds(pl.multiple_of(b * 72, 8), 72)
-            dq, dk, dv = attention_back(
-                q_s[rows, :], k_s[rows, :], v_s[rows, :], kept_p[b], do_s[rows, :], masks
-            )
-            dq_s[rows, :] = dq
-            dk_s[rows, :] = dk
-            dv_s[rows, :] = dv
+    def window(i, carry):
+        places = window_rows(windows, i * TOGETHER, TOGETHER)
+        work = [(place, g, lanes, n_g) for place in places for g, (lanes, n_g) in enumerate(lane_groups(width))]
+        back = attention_back(
+            [(q_s[x[2], lanes], k_s[x[2], lanes], v_s[x[2], lanes]) for x, _, lanes, _ in work],
+            [kept_p[x[0] * windows + x[1], g, :, n_g] for x, g, _, n_g in work],
+            [do_s[x[2], lanes] for x, _, lanes, _ in work],
+        )
+        for ((_, _, rows), _, lanes, _), (dq, dk, dv) in zip(work, back):
+            dq_s[rows, lanes] = dq
+            dk_s[rows, lanes] = dk
+            dv_s[rows, lanes] = dv
         return carry
 
-    lax.fori_loop(0, windows, window, 0, unroll=UNROLL)
+    lax.fori_loop(0, windows // TOGETHER, window, 0, unroll=UNROLL)
     parts = [dq_s[...].astype(BF16), dk_s[...].astype(BF16), dv_s[...].astype(BF16)]
     delta_rolled = round16(
         sum(mm(a, project[:, i * width : (i + 1) * width], NT) for i, a in enumerate(parts))
@@ -609,8 +640,16 @@
     pairs = jnp.concatenate([bias_index[:72, :72].T, bias_index[72:, 72:].T], axis=0)
     pairs = jnp.pad(pairs.reshape(48, 216), ((0, 0), (0, 40)))[:, None]
 
-    def level_bias(name, where, table, types, level_rows, rows, cols):
+    def level_bias(name, where, table, types, level_rows, rows, cols, run):
         lists = jnp.transpose(table[0], (2, 0, 1))
+        count = lists.shape[0] * lists.shape[1]
+        chunks = -(-lists.shape[2] // 128)
+        (bias,) = call(
+            partial(bias_kernel, level_rows, surface_type.shape[0]), name,
+            [((2, rows // 6, types.shape[1] // run, 72, 72 * run), F32)],
+            [((pad8(count) * 144, 128), F32), ((count * chunks, 256), BF16)],
+            [where, latitude_valid, pairs, lists], smem=2, flops=4 * 10**9,
+        )
         t = types.T
         t = jnp.pad(jnp.concatenate([t, t, t], axis=1), ((0, 0), (0, 128 - 9)))
         order = windowed(cols)
@@ -618,33 +657,24 @@
         for a in range(rows):
             for b in range(cols):
                 r[order(a, b), 0], c[order(a, b), 0] = a + 3, b + 6
-        heads = types.shape[1]
-        count = lists.shape[0] * lists.shape[1]
-        chunks = -(-lists.shape[2] // 128)
-        return call(
-            partial(bias_kernel, level_rows), name,
-            [((2, rows // 6, 72, 72 * heads), F32), ((rows * cols, 128), F32), ((128, 72 * heads), BF16)],
-            [((pad8(count) * 144, 128), F32), ((count * chunks, 256), BF16)],
-            [where, latitude_valid, pairs, lists, surface_type, t, r, c],
-            smem=2, flops=4 * 10**9,
-        )
-
-    fbias, fkinds, ftyped = level_bias("fine_bias", place, fine_table, fine_types, 1, rows1, cols1)
+        return bias, surface_type, t, r, c
+
+    fine_bias = level_bias("fine_bias", place, fine_table, fine_types, 1, rows1, cols1, h1)
 
     token16 = lambda width: ((2 * n1, width), BF16)
     blocks1 = 2 * n1 // 72
     forward = call(
         fine_forward_kernel, "fine_forward",
-        [token16(d1)] + fine_halo + [token16(d1), ((blocks1, 72, 72 * h1), BF16), token16(d1)],
-        [((2 * n1, d1), F32)] * 4,
-        [enter.take, middle.send, tokens, *token_halo, fine_gain[None], fine_project, fine_combine,
-         fbias, fkinds, ftyped],
-        flops=4 * 10**9,
+        [token16(d1)] + fine_halo + [token16(d1), ((blocks1, -(-h1 // 4), 72, 288), BF16), token16(d1)],
+        [((2 * n1, d1), F32)] * 4 + [((n1, 128), F32)],
+        [place, enter.take, middle.send, tokens, *token_halo, fine_gain[None], fine_project, fine_combine,
+         *fine_bias],
+        smem=1, flops=4 * 10**9,
     )
     fine_output, kept = forward[0], forward[4:]
     halo = exchange(forward[1:4], -1)
     later, _ = lax.optimization_barrier((place, forward[1]))
-    cbias, ckinds, ctyped = level_bias("coarse_bias", later, coarse_table, coarse_types, 2, rows2, cols2)
+    coarse_bias = level_bias("coarse_bias", later, coarse_table, coarse_types, 2, rows2, cols2, 4)
 
     rows = (4 * d1 + 4 * d2) * d2 // 128
     coarse = call(
@@ -652,10 +682,10 @@
         [((2 * n2, d2), BF16)] + coarse_halo + [token16(d1)] + fine_halo
         + [((4, 2 * n2, d1), BF16), ((7, 2 * n2, d2), BF16)],
         [((2 * n2, d2), F32)] * 8,
-        [middle.take, centre.take, cleave.send, return_middle.send, fine_output, *halo, cot, *cot_halo,
+        [place, middle.take, centre.take, cleave.send, return_middle.send, fine_output, *halo, cot, *cot_halo,
          merge_gain.reshape(4, d1), merge_weight, coarse_gain[None], coarse_project, coarse_combine,
-         cbias, ckinds, ctyped],
-        flops=6 * 10**9,
+         *coarse_bias],
+        smem=1, flops=6 * 10**9,
     )
     delta_halo = exchange(coarse[5:8], 1)
     out_halo = exchange(coarse[1:4], 1)

time: 157 us -> 146 us (0.930)
  Pallas kernels: 52.3 us -> 44.3 us
  local copies, waits for them, and re-layouts: 6.23 us -> 3.03 us
    pallas_call x13, Pallas kernels: 52.3 us -> 44.3 us  [call(): pl.pallas_call(kernel, name=name, out_shape=[jax.ShapeDtypeStruct(s, d) f...]
    unnamed x80 -> x72, local copies, waits for them, and re-layouts: 5.86 us -> 2.65 us
  transfers between devices with their start and end apart: 20 -> 20, of which waited for: 4 -> 4; matrix products, arithmetic and copies ran while one was open for 1% -> 1% of each run, Pallas kernels for 24% -> 22%
where the time goes in v3:
time: 146 us; the launch traced here: 145 us
  waiting for transfers between devices  59.5 us (41%)
  Pallas kernels  44.3 us (30%)
  starting transfers between devices  37.1 us (25%)
  local copies, waits for them, and re-layouts  3.03 us (2%)
    pallas_call x13, Pallas kernels, call(): pl.pallas_call(kernel, name=name, out_shape=[jax.ShapeDtypeStruct(s, d) f...  44.3 us
    ppermute x6, waiting for transfers between devices, move(): return lax.ppermute(value, ('lon', 'lat'), pairs)  31.9 us
    all_to_all x1, waiting for transfers between devices, summed(): lax.all_to_all(total, ('lon', 'lat'), 0, 0, tiled=True).reshape(-1, 128)  26.1 us
    ppermute x6, starting transfers between devices, move(): return lax.ppermute(value, ('lon', 'lat'), pairs)  11.9 us
    all_to_all x1, starting transfers between devices, summed(): terms = lax.all_to_all(block, ('lon', 'lat'), 0, 0, tiled=True)  7.5 us
    ppermute x6, starting transfers between devices, move(): lax.ppermute(value, 'lat', [(s, (s + lat_step) % lats) for s in range(lat...  7.41 us
    ppermute x6, starting transfers between devices, move(): lax.ppermute(value, 'lon', [(s, (s + lon_step) % lons) for s in range(lon...  5.5 us
    all_to_all x1, starting transfers between devices, summed(): lax.all_to_all(total, ('lon', 'lat'), 0, 0, tiled=True).reshape(-1, 128)  4.78 us
  transfers between devices with their start and end apart: 20, of which 4 were waited for; matrix products, arithmetic and copies ran while one was open for 1% of the time, Pallas kernels for 22%

profile of v3, /device:TPU:0, one launch (start us, length us, event | category | flops | bytes accessed | tf_op | source)
XLA Modules:
  0.0 145.4 jit_solution(13333687165243918403)
XLA Ops:
  0.7 2.6 %prepare.1 = (bf16[2,128,192]{2,1,0:T(8,128)(2,1)}, bf16[2,64,192]{2,1,0:T(8,128)(2,1)}, bf16[2,32,192]{2,1,0:T(8,128)(2,1)}, bf16[2,64,384]{2,1,0:T(8,128)(2,1)...) custom-call(s32[224,1]{1,0:T(8,128)} %constant.47.clone.fsel, s32[128,1]{1,0:T(8,128)} %constant.48.clone.csel, ...), custom_call_target="tpu_custom_call" | custom-call | flops 1000000000 | bytes 4194304 | tf_op jit(solution)/shard_map/prepare/pallas_call | solution.py:539
  3.3 8.3 %collective-permute-start.2 = (bf16[2,32,192]{2,1,0:T(8,128)(2,1)}, bf16[2,32,192]{2,1,0:T(8,128)(2,1)S(1)}, u32[]{:S(2)}, u32[]{:S(2)}) collective-permute-start(bf16[2,32,192]{2,1,0:T(8,128)(2,1)} %get-tuple-element.61), channel_id=1, source_target_pairs={{0,127},{1,120},{2,121},{3,122},{4,123},{5,124},{6,125},{7,126},{8... | collective-permute-start | bytes 73736 | tf_op jit(solution)/shard_map/ppermute | solution.py:562
  11.5 1.7 %collective-permute-start.7 = (bf16[2,32,384]{2,1,0:T(8,128)(2,1)}, bf16[2,32,384]{2,1,0:T(8,128)(2,1)S(1)}, u32[]{:S(2)}, u32[]{:S(2)}) collective-permute-start(bf16[2,32,384]{2,1,0:T(8,128)(2,1)} %get-tuple-element.67), channel_id=1, source_target_pairs={{0,120},{8,0},{16,8},{24,16},{32,24},{40,32},{48,40},{56,48},{64,5... | collective-permute-start | bytes 147464 | tf_op jit(solution)/shard_map/ppermute | solution.py:554
  13.3 0.9 collective-permute-start.1
  14.2 0.1 copy.41
  14.3 0.1 copy.42
  14.4 0.1 select_maximum_fusion.types
  14.5 0.1 slice_bitcast_fusion.1
  14.6 0.1 pad_add_fusion
  14.7 0.1 copy.40
  14.8 0.1 reshape.40
  14.9 0.1 pad_add_fusion.1.place
  15.0 0.0 copy-start.30
  15.0 0.0 copy-start.34
  15.0 0.0 copy-start.2
  15.1 0.0 copy-start.4
  15.1 0.0 copy-start.6
  15.1 0.0 copy-start.16
  15.1 0.0 copy-start.17
  15.1 0.0 copy-start.18
  15.1 0.0 copy-start.21
  15.1 6.0 %fine_bias.1.bias = f32[2,2,1,72,432]{4,3,2,1,0:T(8,128)S(1)} custom-call(s32[3]{0:T(128)S(1)} %pad_add_fusion.1.place, s32[96]{0:T(128)S(1)} %copy-done.12, s32[48,1,256]{2,1,0:T(1,128)S(1)} %broadcast_in_dim.12.index, f32[6,2,3312]{2,1,0:T(2,128)S(1)} %bitcast.26), custom_call_target="tpu_custom_call" | custom-call | flops 4000000000 | bytes 4194304 | tf_op jit(solution)/shard_map/fine_bias/pallas_call | solution.py:539
  21.2 0.1 select_maximum_fusion.2.types
  21.3 0.1 reshape.41.merge_gain
  21.4 0.5 collective-permute-start.6
  22.0 0.0 copy-start.9
  22.0 6.2 %fine_forward.1 = (bf16[1152,192]{1,0:T(8,128)(2,1)S(1)}, bf16[2,128,192]{2,1,0:T(8,128)(2,1)S(1)}, bf16[2,64,192]{2,1,0:T(8,128)(2,1)S(1)}, bf16[2,32,192]{2,1,...) custom-call(s32[3]{0:T(128)S(1)} %pad_add_fusion.1.place, ...), custom_call_target="tpu_custom_call" | custom-call | flops 4000000000 | bytes 4194304 | tf_op jit(solution)/shard_map/fine_forward/pallas_call | solution.py:539
  28.2 3.0 %collective-permute-start.3 = (bf16[2,128,192]{2,1,0:T(8,128)(2,1)S(1)}, bf16[2,128,192]{2,1,0:T(8,128)(2,1)S(1)}, u32[]{:S(2)}, u32[]{:S(2)}) collective-permute-start(bf16[2,128,192]{2,1,0:T(8,128)(2,1)S(1)} %get-tuple-element.63), channel_id=1, source_target_pairs={{0,7},{1,0},{2,1},{3,2},{4,3},{5,4},{6,5},{7,6},{8,15},{9,8},{10,9... | collective-permute-start | bytes 294920 | tf_op jit(solution)/shard_map/ppermute | solution.py:556
  31.2 1.3 collective-permute-start.4
  32.5 0.0 copy-start.15
  32.5 0.0 copy-start.20
  32.5 0.0 copy-start.23
  32.5 0.0 copy-start.24
  32.5 0.0 copy-start.25
  32.5 0.0 copy-start.26
  32.5 6.0 %coarse_bias.1.bias = f32[2,1,3,72,288]{4,3,2,1,0:T(8,128)S(1)} custom-call(s32[3]{0:T(128)S(1)} %pad_add_fusion.1.place, s32[96]{0:T(128)S(1)} %copy-done.12, s32[48,1,256]{2,1,0:T(1,128)S(1)} %broadcast_in_dim.12.index, f32[12,1,3312]{2,1,0:T(1,128)S(1)} %bitcast.27), custom_call_target="tpu_custom_call" | custom-call | flops 4000000000 | bytes 4194304 | tf_op jit(solution)/shard_map/coarse_bias/pallas_call | solution.py:539
  38.7 7.5 %coarse.1 = (bf16[288,384]{1,0:T(8,128)(2,1)S(1)}, bf16[2,64,384]{2,1,0:T(8,128)(2,1)S(1)}, bf16[2,32,384]{2,1,0:T(8,128)(2,1)S(1)}, bf16[2,32,384]{2,1,0:T(8,12...) custom-call(s32[3]{0:T(128)S(1)} %pad_add_fusion.1.place, ...), custom_call_target="tpu_custom_call" | custom-call | flops 6000000000 | bytes 4194304 | tf_op jit(solution)/shard_map/coarse/pallas_call | solution.py:539
  46.2 0.6 collective-permute-start.11
  46.8 1.5 %collective-permute-start.13 = (bf16[2,32,384]{2,1,0:T(8,128)(2,1)S(1)}, bf16[2,32,384]{2,1,0:T(8,128)(2,1)S(1)}, u32[]{:S(2)}, u32[]{:S(2)}) collective-permute-start(bf16[2,32,384]{2,1,0:T(8,128)(2,1)S(1)} %get-tuple-element.92), channel_id=1, source_target_pairs={{0,8},{8,16},{16,24},{24,32},{32,40},{40,48},{48,56},{56,64},{64,7... | collective-permute-start | bytes 147464 | tf_op jit(solution)/shard_map/ppermute | solution.py:554
  48.4 0.2 collective-permute-start.14
  48.6 0.0 collective-permute-start.10
  48.6 1.5 %collective-permute-start.9 = (bf16[2,128,192]{2,1,0:T(8,128)(2,1)S(1)}, bf16[2,128,192]{2,1,0:T(8,128)(2,1)S(1)}, u32[]{:S(2)}, u32[]{:S(2)}) collective-permute-start(bf16[2,128,192]{2,1,0:T(8,128)(2,1)S(1)} %get-tuple-element.79), channel_id=1, source_target_pairs={{0,1},{1,2},{2,3},{3,4},{4,5},{5,6},{6,7},{7,0},{8,9},{9,10},{10,1... | collective-permute-start | bytes 294920 | tf_op jit(solution)/shard_map/ppermute | solution.py:556
  50.1 1.0 fine_again.1
  51.2 0.0 copy-start.14
  51.2 0.0 copy-start.19
  51.2 1.3 coarse_gradients.1.coarse
  52.5 2.6 %collective-permute-done.11.rc = bf16[2,32,192]{2,1,0:T(8,128)(2,1)S(1)} collective-permute-done((bf16[2,32,192]{2,1,0:T(8,128)(2,1)S(1)}, bf16[2,32,192]{2,1,0:T(8,128)(2,1)S(1)}, u32[]{:S(2)}, u32[]{:S(2)}) %collective-permute-start.11) | collective-permute-done | bytes 24608 | tf_op jit(solution)/shard_map/ppermute | solution.py:562
  55.1 1.4 collective-permute-start.12
  56.4 1.5 %collective-permute-done.9.ra = bf16[2,128,192]{2,1,0:T(8,128)(2,1)S(1)} collective-permute-done((bf16[2,128,192]{2,1,0:T(8,128)(2,1)S(1)}, bf16[2,128,192]{2,1,0:T(8,128)(2,1)S(1)}, u32[]{:S(2)}, u32[]{:S(2)}) %collective-permute-start.9) | collective-permute-done | bytes 98336 | tf_op jit(solution)/shard_map/ppermute | solution.py:556
  57.9 6.0 %fine_backward.1 = (bf16[1152,192]{1,0:T(8,128)(2,1)S(1)}, bf16[2,128,192]{2,1,0:T(8,128)(2,1)S(1)}, bf16[2,64,192]{2,1,0:T(8,128)(2,1)S(1)}, bf16[2,32,192]{2,1,0:T(8,128)(2,1)S(1)}, bf16[4,1152,192]{2,1,0:T(8,128)(2,1)S(1)}) custom-call(s32[576,1]{1,0:T(8,128)S(1)} %copy-done.14, s32[224,1]{1,0:T(8,128)S(1)} %copy-done.19, ...), custom_call_target="tpu_custom_call" | custom-call | flops 6000000000 | bytes 4194304 | tf_op jit(solution)/shard_map/fine_backward/pallas_call | solution.py:539
  63.9 2.2 %fine_gradients.1 = bf16[8192,128]{1,0:T(8,128)(2,1)} custom-call(bf16[1152,192]{1,0:T(8,128)(2,1)S(1)} %get-tuple-element.76.kept_u, bf16[1152,192]{1,0:T(8,128)(2,1)S(1)} %get-tuple-element.77.kept_o, bf16[4,1152,192]{2,1,0:T(8,128)(2,1)S(1)} %get-tuple-element.88.kept, bf16[6912,128]{1,0:T(8,128)(2,1)S(1)} %coarse_gradients.1.coarse), custom_call_target="tpu_custom_call" | custom-call | flops 2000000000 | bytes 4194304 | tf_op jit(solution)/shard_map/fine_gradients/pallas_call | solution.py:539
  66.1 7.5 %all-to-all-start = ((bf16[128,64,128]{2,1,0:T(8,128)(2,1)}), bf16[128,64,128]{2,1,0:T(8,128)(2,1)S(1)}, u32[]{:S(2)}, u32[]{:S(2)}) async-start(bf16[128,64,128]{2,1,0:T(8,128)(2,1)} %bitcast.14), calls=%async_computation | async-start | bytes 4194304 | tf_op jit(solution)/shard_map/all_to_all | solution.py:589
  73.7 1.0 collective-permute-start.15
  74.7 2.8 %collective-permute-start.17 = (bf16[2,32,192]{2,1,0:T(8,128)(2,1)S(1)}, bf16[2,32,192]{2,1,0:T(8,128)(2,1)S(1)}, u32[]{:S(2)}, u32[]{:S(2)}) collective-permute-start(bf16[2,32,192]{2,1,0:T(8,128)(2,1)S(1)} %get-tuple-element.101), channel_id=1, source_target_pairs={{0,9},{1,10},{2,11},{3,12},{4,13},{5,14},{6,15},{7,8},{8,17},{9,18... | collective-permute-start | bytes 73736 | tf_op jit(solution)/shard_map/ppermute | solution.py:562
  77.5 29.3 %collective-permute-done.17.rc = bf16[2,32,192]{2,1,0:T(8,128)(2,1)S(1)} collective-permute-done((bf16[2,32,192]{2,1,0:T(8,128)(2,1)S(1)}, bf16[2,32,192]{2,1,0:T(8,128)(2,1)S(1)}, u32[]{:S(2)}, u32[]{:S(2)}) %collective-permute-start.17) | collective-permute-done | bytes 24608 | tf_op jit(solution)/shard_map/ppermute | solution.py:562
  106.8 0.5 add.13
  107.3 1.3 copy-done
  108.7 4.8 %all-to-all-start.1 = ((bf16[128,64,128]{2,1,0:T(8,128)(2,1)}), bf16[128,64,128]{2,1,0:T(8,128)(2,1)S(1)}, u32[]{:S(2)}, u32[]{:S(2)}) async-start(bf16[128,64,128]{2,1,0:T(8,128)(2,1)} %copy-done), calls=%async_computation.1 | async-start | bytes 4194304 | tf_op jit(solution)/shard_map/all_to_all | solution.py:592
  113.5 0.0 copy-start.28
  113.5 0.9 copy-done.28
  114.4 1.1 restore_coarse.1
  115.5 1.7 %restore_fine.1 = bf16[1152,192]{1,0:T(8,128)(2,1)} custom-call(s32[576,1]{1,0:T(8,128)S(1)} %copy-done.13, bf16[1152,192]{1,0:T(8,128)(2,1)S(1)} %get-tuple-element.97.own, bf16[2,128,192]{2,1,0:T(8,128)(2,1)S(1)} %collective-permute-done.15.ra, bf16[2,64,192]{2,1,0:T(8,128)(2,1)S(1)} %collective-permute-done.16.rb, ...), custom_call_target="tpu_custom_call" | custom-call | flops 1000000000 | bytes 4194304 | tf_op jit(solution)/shard_map/restore_fine/pallas_call | solution.py:539
  117.2 26.1 %all-to-all-done.1 = bf16[128,64,128]{2,1,0:T(8,128)(2,1)S(1)} async-done(((bf16[128,64,128]{2,1,0:T(8,128)(2,1)}), bf16[128,64,128]{2,1,0:T(8,128)(2,1)S(1)}, u32[]{:S(2)}, u32[]{:S(2)}) %all-to-all-start.1) | async-done | bytes 2097184 | tf_op jit(solution)/shard_map/all_to_all | solution.py:592
  143.3 2.1 %finish.1 = (f32[192,576]{1,0:T(8,128)}, f32[192,192]{1,0:T(8,128)}, f32[768,384]{1,0:T(8,128)}, f32[384,1152]{1,0:T(8,128)}, f32[384,384]{1,0:T(8,128)}) custom-call(bf16[8192,128]{1,0:T(8,128)(2,1)S(1)} %bitcast.21), custom_call_target="tpu_custom_call" | custom-call | flops 1000000000 | bytes 4194304 | tf_op jit(solution)/shard_map/finish/pallas_call | solution.py:539
  (72 shorter events, 0.2 us)
Async XLA Ops:
  0.6 13.6 %copy-start.31 = (f32[3,6]{1,0:T(4,128)S(1)}, f32[3,6]{1,0:T(4,128)}, u32[]{:S(2)}) copy-start(f32[3,6]{1,0:T(4,128)} %param.39) | copy-start | bytes 220
  0.6 13.7 %copy-start.32 = (f32[3,12]{1,0:T(4,128)S(1)}, f32[3,12]{1,0:T(4,128)}, u32[]{:S(2)}) copy-start(f32[3,12]{1,0:T(4,128)} %param.46) | copy-start | bytes 436
  0.7 13.8 %copy-start.29 = (s32[144,144]{1,0:T(8,128)S(1)}, s32[144,144]{1,0:T(8,128)}, u32[]{:S(2)}) copy-start(s32[144,144]{1,0:T(8,128)} %param.49) | copy-start | bytes 248836
  0.7 14.3 %copy-start.8 = (f32[1,2,3312,6]{2,1,3,0:T(2,128)S(1)}, f32[1,2,3312,6]{2,1,3,0:T(2,128)}, u32[]{:S(2)}) copy-start(f32[1,2,3312,6]{2,1,3,0:T(2,128)} %param.38) | copy-start | bytes 476932
  0.7 14.3 %copy-start.12 = (s32[96]{0:T(128)S(1)}, s32[96]{0:T(128)}, u32[]{:S(2)}) copy-start(s32[96]{0:T(128)} %valid.3) | copy-start | bytes 1156
  3.3 18.1 %collective-permute-start.2 = (bf16[2,32,192]{2,1,0:T(8,128)(2,1)}, bf16[2,32,192]{2,1,0:T(8,128)(2,1)S(1)}, u32[]{:S(2)}, u32[]{:S(2)}) collective-permute-start(bf16[2,32,192]{2,1,0:T(8,128)(2,1)} %get-tuple-element.61), channel_id=1, source_target_pairs={{0,127},{1,120},{2,121},{3,122},{4,123},{5,124},{6,125},{7,126},{8... | collective-permute-start | bytes 73736 | tf_op jit(solution)/shard_map/ppermute | solution.py:562
  11.5 19.7 %collective-permute-start.7 = (bf16[2,32,384]{2,1,0:T(8,128)(2,1)}, bf16[2,32,384]{2,1,0:T(8,128)(2,1)S(1)}, u32[]{:S(2)}, u32[]{:S(2)}) collective-permute-start(bf16[2,32,384]{2,1,0:T(8,128)(2,1)} %get-tuple-element.67), channel_id=1, source_target_pairs={{0,120},{8,0},{16,8},{24,16},{32,24},{40,32},{48,40},{56,48},{64,5... | collective-permute-start | bytes 147464 | tf_op jit(solution)/shard_map/ppermute | solution.py:554
  13.3 25.3 %collective-permute-start.8 = (bf16[2,32,384]{2,1,0:T(8,128)(2,1)}, bf16[2,32,384]{2,1,0:T(8,128)(2,1)S(1)}, u32[]{:S(2)}, u32[]{:S(2)}) collective-permute-start(bf16[2,32,384]{2,1,0:T(8,128)(2,1)} %get-tuple-element.68), channel_id=1, source_target_pairs={{0,127},{1,120},{2,121},{3,122},{4,123},{5,124},{6,125},{7,126},{8... | collective-permute-start | bytes 147464 | tf_op jit(solution)/shard_map/ppermute | solution.py:562
  13.3 8.6 %collective-permute-start.1 = (bf16[2,64,192]{2,1,0:T(8,128)(2,1)}, bf16[2,64,192]{2,1,0:T(8,128)(2,1)S(1)}, u32[]{:S(2)}, u32[]{:S(2)}) collective-permute-start(bf16[2,64,192]{2,1,0:T(8,128)(2,1)} %get-tuple-element.60), channel_id=1, source_target_pairs={{0,120},{8,0},{16,8},{24,16},{32,24},{40,32},{48,40},{56,48},{64,5... | collective-permute-start | bytes 147464 | tf_op jit(solution)/shard_map/ppermute | solution.py:554
  14.2 7.7 %collective-permute-start = (bf16[2,128,192]{2,1,0:T(8,128)(2,1)}, bf16[2,128,192]{2,1,0:T(8,128)(2,1)S(1)}, u32[]{:S(2)}, u32[]{:S(2)}) collective-permute-start(bf16[2,128,192]{2,1,0:T(8,128)(2,1)} %get-tuple-element.59), channel_id=1, source_target_pairs={{0,7},{1,0},{2,1},{3,2},{4,3},{5,4},{6,5},{7,6},{8,15},{9,8},{10,9... | collective-permute-start | bytes 294920 | tf_op jit(solution)/shard_map/ppermute | solution.py:556
  15.0 6.3 %copy-start.33 = (f32[384]{0:T(512)S(1)}, f32[384]{0:T(512)}, u32[]{:S(2)}) copy-start(f32[384]{0:T(512)} %param.42) | copy-start | bytes 4612
  15.0 6.3 %copy-start.30 = (f32[768]{0:T(1024)S(1)}, f32[768]{0:T(1024)}, u32[]{:S(2)}) copy-start(f32[768]{0:T(1024)} %param.40) | copy-start | bytes 9220
  15.0 6.3 %copy-start.34 = (bf16[2,64,384]{2,1,0:T(8,128)(2,1)S(1)}, bf16[2,64,384]{2,1,0:T(8,128)(2,1)}, u32[]{:S(2)}) copy-start(bf16[2,64,384]{2,1,0:T(8,128)(2,1)} %get-tuple-element.66) | copy-start | bytes 294916
  15.0 6.9 %copy-start.2 = (bf16[2,12,48,192]{3,2,1,0:T(8,128)(2,1)S(1)}, bf16[2,12,48,192]{3,2,1,0:T(8,128)(2,1)}, u32[]{:S(2)}) copy-start(bf16[2,12,48,192]{3,2,1,0:T(8,128)(2,1)} %param.33) | copy-start | bytes 1327108
  15.1 6.9 %copy-start.4 = (s32[96,768]{1,0:T(8,128)S(1)}, s32[96,768]{1,0:T(8,128)}, u32[]{:S(2)}) copy-start(s32[96,768]{1,0:T(8,128)} %surface.3) | copy-start | bytes 884740
  15.1 6.8 %copy-start.6 = (bf16[192,576]{1,0:T(8,128)(2,1)S(1)}, bf16[192,576]{1,0:T(8,128)(2,1)}, u32[]{:S(2)}) copy-start(bf16[192,576]{1,0:T(8,128)(2,1)} %project.7) | copy-start | bytes 663556
  15.1 6.8 %copy-start.10 = (bf16[192,192]{1,0:T(8,128)(2,1)S(1)}, bf16[192,192]{1,0:T(8,128)(2,1)}, u32[]{:S(2)}) copy-start(bf16[192,192]{1,0:T(8,128)(2,1)} %combine.5) | copy-start | bytes 221188
  15.1 6.8 %copy-start.11 = (f32[192]{0:T(256)S(1)}, f32[192]{0:T(256)}, u32[]{:S(2)}) copy-start(f32[192]{0:T(256)} %param.35) | copy-start | bytes 2308
  15.1 6.8 %copy-start.16 = (s32[576,1]{1,0:T(8,128)S(1)}, s32[576,1]{1,0:T(8,128)}, u32[]{:S(2)}) copy-start(s32[576,1]{1,0:T(8,128)} %constant.52.clone.col) | copy-start | bytes 6916
  15.1 6.8 %copy-start.17 = (s32[576,1]{1,0:T(8,128)S(1)}, s32[576,1]{1,0:T(8,128)}, u32[]{:S(2)}) copy-start(s32[576,1]{1,0:T(8,128)} %constant.51.clone.row) | copy-start | bytes 6916
  15.1 6.8 %copy-start.18 = (s32[576,1]{1,0:T(8,128)S(1)}, s32[576,1]{1,0:T(8,128)}, u32[]{:S(2)}) copy-start(s32[576,1]{1,0:T(8,128)} %constant.49.clone.take) | copy-start | bytes 6916
  15.1 6.8 %copy-start.21 = (s32[224,1]{1,0:T(8,128)S(1)}, s32[224,1]{1,0:T(8,128)}, u32[]{:S(2)}) copy-start(s32[224,1]{1,0:T(8,128)} %constant.50.clone.sel) | copy-start | bytes 2692
  21.4 17.2 %collective-permute-start.6 = (bf16[2,64,384]{2,1,0:T(8,128)(2,1)S(1)}, bf16[2,64,384]{2,1,0:T(8,128)(2,1)S(1)}, u32[]{:S(2)}, u32[]{:S(2)}) collective-permute-start(bf16[2,64,384]{2,1,0:T(8,128)(2,1)S(1)} %copy-done.34), channel_id=1, source_target_pairs={{0,7},{1,0},{2,1},{3,2},{4,3},{5,4},{6,5},{7,6},{8,15},{9,8},{10,9... | collective-permute-start | bytes 294920 | tf_op jit(solution)/shard_map/ppermute | solution.py:556
  22.0 10.5 %copy-start.9 = (f32[1,1,3312,12]{2,1,3,0:T(1,128)S(1)}, f32[1,1,3312,12]{2,1,3,0:T(1,128)}, u32[]{:S(2)}) copy-start(f32[1,1,3312,12]{2,1,3,0:T(1,128)} %param.45) | copy-start | bytes 476932
  28.2 10.4 %collective-permute-start.3 = (bf16[2,128,192]{2,1,0:T(8,128)(2,1)S(1)}, bf16[2,128,192]{2,1,0:T(8,128)(2,1)S(1)}, u32[]{:S(2)}, u32[]{:S(2)}) collective-permute-start(bf16[2,128,192]{2,1,0:T(8,128)(2,1)S(1)} %get-tuple-element.63), channel_id=1, source_target_pairs={{0,7},{1,0},{2,1},{3,2},{4,3},{5,4},{6,5},{7,6},{8,15},{9,8},{10,9... | collective-permute-start | bytes 294920 | tf_op jit(solution)/shard_map/ppermute | solution.py:556
  31.2 7.4 %collective-permute-start.5 = (bf16[2,32,192]{2,1,0:T(8,128)(2,1)S(1)}, bf16[2,32,192]{2,1,0:T(8,128)(2,1)S(1)}, u32[]{:S(2)}, u32[]{:S(2)}) collective-permute-start(bf16[2,32,192]{2,1,0:T(8,128)(2,1)S(1)} %get-tuple-element.65), channel_id=1, source_target_pairs={{0,127},{1,120},{2,121},{3,122},{4,123},{5,124},{6,125},{7,126},{8... | collective-permute-start | bytes 73736 | tf_op jit(solution)/shard_map/ppermute | solution.py:562
  31.2 7.4 %collective-permute-start.4 = (bf16[2,64,192]{2,1,0:T(8,128)(2,1)S(1)}, bf16[2,64,192]{2,1,0:T(8,128)(2,1)S(1)}, u32[]{:S(2)}, u32[]{:S(2)}) collective-permute-start(bf16[2,64,192]{2,1,0:T(8,128)(2,1)S(1)} %get-tuple-element.64), channel_id=1, source_target_pairs={{0,120},{8,0},{16,8},{24,16},{32,24},{40,32},{48,40},{56,48},{64,5... | collective-permute-start | bytes 147464 | tf_op jit(solution)/shard_map/ppermute | solution.py:554
  32.4 6.2 %copy-start.1 = (bf16[384,1152]{1,0:T(8,128)(2,1)S(1)}, bf16[384,1152]{1,0:T(8,128)(2,1)}, u32[]{:S(2)}) copy-start(bf16[384,1152]{1,0:T(8,128)(2,1)} %project.5) | copy-start | bytes 2654212
  32.4 6.2 %copy-start.3 = (bf16[768,384]{1,0:T(8,128)(2,1)S(1)}, bf16[768,384]{1,0:T(8,128)(2,1)}, u32[]{:S(2)}) copy-start(bf16[768,384]{1,0:T(8,128)(2,1)} %merge_weight.1) | copy-start | bytes 1769476
  32.4 6.2 %copy-start.5 = (bf16[384,384]{1,0:T(8,128)(2,1)S(1)}, bf16[384,384]{1,0:T(8,128)(2,1)}, u32[]{:S(2)}) copy-start(bf16[384,384]{1,0:T(8,128)(2,1)} %combine.4) | copy-start | bytes 884740
  32.4 6.2 %copy-start.7 = (bf16[2,6,24,384]{3,2,1,0:T(8,128)(2,1)S(1)}, bf16[2,6,24,384]{3,2,1,0:T(8,128)(2,1)}, u32[]{:S(2)}) copy-start(bf16[2,6,24,384]{3,2,1,0:T(8,128)(2,1)} %param.34) | copy-start | bytes 663556
  32.5 6.2 %copy-start.15 = (s32[576,1]{1,0:T(8,128)S(1)}, s32[576,1]{1,0:T(8,128)}, u32[]{:S(2)}) copy-start(s32[576,1]{1,0:T(8,128)} %constant.53.clone.take) | copy-start | bytes 6916
  32.5 6.2 %copy-start.20 = (s32[224,1]{1,0:T(8,128)S(1)}, s32[224,1]{1,0:T(8,128)}, u32[]{:S(2)}) copy-start(s32[224,1]{1,0:T(8,128)} %constant.56.clone.fsel) | copy-start | bytes 2692
  32.5 6.2 %copy-start.23 = (s32[144,1]{1,0:T(8,128)S(1)}, s32[144,1]{1,0:T(8,128)}, u32[]{:S(2)}) copy-start(s32[144,1]{1,0:T(8,128)} %constant.58.clone.col) | copy-start | bytes 1732
  32.5 6.2 %copy-start.24 = (s32[144,1]{1,0:T(8,128)S(1)}, s32[144,1]{1,0:T(8,128)}, u32[]{:S(2)}) copy-start(s32[144,1]{1,0:T(8,128)} %constant.57.clone.row) | copy-start | bytes 1732
  32.5 6.2 %copy-start.25 = (s32[144,1]{1,0:T(8,128)S(1)}, s32[144,1]{1,0:T(8,128)}, u32[]{:S(2)}) copy-start(s32[144,1]{1,0:T(8,128)} %constant.54.clone.ctake) | copy-start | bytes 1732
  32.5 6.2 %copy-start.26 = (s32[128,1]{1,0:T(8,128)S(1)}, s32[128,1]{1,0:T(8,128)}, u32[]{:S(2)}) copy-start(s32[128,1]{1,0:T(8,128)} %constant.55.clone.csel) | copy-start | bytes 1540
  46.2 5.0 %copy-start.27 = (bf16[288,384]{1,0:T(8,128)(2,1)}, bf16[288,384]{1,0:T(8,128)(2,1)S(1)}, u32[]{:S(2)}) copy-start(bf16[288,384]{1,0:T(8,128)(2,1)S(1)} %get-tuple-element.70.own) | copy-start | bytes 663556
  46.2 8.8 %collective-permute-start.11 = (bf16[2,32,192]{2,1,0:T(8,128)(2,1)S(1)}, bf16[2,32,192]{2,1,0:T(8,128)(2,1)S(1)}, u32[]{:S(2)}, u32[]{:S(2)}) collective-permute-start(bf16[2,32,192]{2,1,0:T(8,128)(2,1)S(1)} %get-tuple-element.81), channel_id=1, source_target_pairs={{0,9},{1,10},{2,11},{3,12},{4,13},{5,14},{6,15},{7,8},{8,17},{9,18... | collective-permute-start | bytes 73736 | tf_op jit(solution)/shard_map/ppermute | solution.py:562
  46.8 19.3 %collective-permute-start.13 = (bf16[2,32,384]{2,1,0:T(8,128)(2,1)S(1)}, bf16[2,32,384]{2,1,0:T(8,128)(2,1)S(1)}, u32[]{:S(2)}, u32[]{:S(2)}) collective-permute-start(bf16[2,32,384]{2,1,0:T(8,128)(2,1)S(1)} %get-tuple-element.92), channel_id=1, source_target_pairs={{0,8},{8,16},{16,24},{24,32},{32,40},{40,48},{48,56},{56,64},{64,7... | collective-permute-start | bytes 147464 | tf_op jit(solution)/shard_map/ppermute | solution.py:554
  48.4 17.8 %collective-permute-start.14 = (bf16[2,32,384]{2,1,0:T(8,128)(2,1)S(1)}, bf16[2,32,384]{2,1,0:T(8,128)(2,1)S(1)}, u32[]{:S(2)}, u32[]{:S(2)}) collective-permute-start(bf16[2,32,384]{2,1,0:T(8,128)(2,1)S(1)} %get-tuple-element.93), channel_id=1, source_target_pairs={{0,9},{1,10},{2,11},{3,12},{4,13},{5,14},{6,15},{7,8},{8,17},{9,18... | collective-permute-start | bytes 147464 | tf_op jit(solution)/shard_map/ppermute | solution.py:562
  48.6 7.8 %collective-permute-start.10 = (bf16[2,64,192]{2,1,0:T(8,128)(2,1)S(1)}, bf16[2,64,192]{2,1,0:T(8,128)(2,1)S(1)}, u32[]{:S(2)}, u32[]{:S(2)}) collective-permute-start(bf16[2,64,192]{2,1,0:T(8,128)(2,1)S(1)} %get-tuple-element.80), channel_id=1, source_target_pairs={{0,8},{8,16},{16,24},{24,32},{32,40},{40,48},{48,56},{56,64},{64,7... | collective-permute-start | bytes 147464 | tf_op jit(solution)/shard_map/ppermute | solution.py:554
  48.6 9.3 %collective-permute-start.9 = (bf16[2,128,192]{2,1,0:T(8,128)(2,1)S(1)}, bf16[2,128,192]{2,1,0:T(8,128)(2,1)S(1)}, u32[]{:S(2)}, u32[]{:S(2)}) collective-permute-start(bf16[2,128,192]{2,1,0:T(8,128)(2,1)S(1)} %get-tuple-element.79), channel_id=1, source_target_pairs={{0,1},{1,2},{2,3},{3,4},{4,5},{5,6},{6,7},{7,0},{8,9},{9,10},{10,1... | collective-permute-start | bytes 294920 | tf_op jit(solution)/shard_map/ppermute | solution.py:556
  51.2 6.7 %copy-start.14 = (s32[576,1]{1,0:T(8,128)S(1)}, s32[576,1]{1,0:T(8,128)}, u32[]{:S(2)}) copy-start(s32[576,1]{1,0:T(8,128)} %constant.59.clone.take) | copy-start | bytes 6916
  51.2 6.7 %copy-start.19 = (s32[224,1]{1,0:T(8,128)S(1)}, s32[224,1]{1,0:T(8,128)}, u32[]{:S(2)}) copy-start(s32[224,1]{1,0:T(8,128)} %constant.60.clone.sel) | copy-start | bytes 2692
  55.1 11.1 %collective-permute-start.12 = (bf16[2,64,384]{2,1,0:T(8,128)(2,1)S(1)}, bf16[2,64,384]{2,1,0:T(8,128)(2,1)S(1)}, u32[]{:S(2)}, u32[]{:S(2)}) collective-permute-start(bf16[2,64,384]{2,1,0:T(8,128)(2,1)S(1)} %get-tuple-element.91), channel_id=1, source_target_pairs={{0,1},{1,2},{2,3},{3,4},{4,5},{5,6},{6,7},{7,0},{8,9},{9,10},{10,1... | collective-permute-start | bytes 294920 | tf_op jit(solution)/shard_map/ppermute | solution.py:556
  66.1 40.7 %all-to-all-start = ((bf16[128,64,128]{2,1,0:T(8,128)(2,1)}), bf16[128,64,128]{2,1,0:T(8,128)(2,1)S(1)}, u32[]{:S(2)}, u32[]{:S(2)}) async-start(bf16[128,64,128]{2,1,0:T(8,128)(2,1)} %bitcast.14), calls=%async_computation | async-start | bytes 4194304 | tf_op jit(solution)/shard_map/all_to_all | solution.py:589
  73.7 33.1 %collective-permute-start.15 = (bf16[2,128,192]{2,1,0:T(8,128)(2,1)S(1)}, bf16[2,128,192]{2,1,0:T(8,128)(2,1)S(1)}, u32[]{:S(2)}, u32[]{:S(2)}) collective-permute-start(bf16[2,128,192]{2,1,0:T(8,128)(2,1)S(1)} %get-tuple-element.99), channel_id=1, source_target_pairs={{0,1},{1,2},{2,3},{3,4},{4,5},{5,6},{6,7},{7,0},{8,9},{9,10},{10,1... | collective-permute-start | bytes 294920 | tf_op jit(solution)/shard_map/ppermute | solution.py:556
  74.7 32.1 %collective-permute-start.16 = (bf16[2,64,192]{2,1,0:T(8,128)(2,1)S(1)}, bf16[2,64,192]{2,1,0:T(8,128)(2,1)S(1)}, u32[]{:S(2)}, u32[]{:S(2)}) collective-permute-start(bf16[2,64,192]{2,1,0:T(8,128)(2,1)S(1)} %get-tuple-element.100), channel_id=1, source_target_pairs={{0,8},{8,16},{16,24},{24,32},{32,40},{40,48},{48,56},{56,64},{64,7... | collective-permute-start | bytes 147464 | tf_op jit(solution)/shard_map/ppermute | solution.py:554
  74.7 32.1 %collective-permute-start.17 = (bf16[2,32,192]{2,1,0:T(8,128)(2,1)S(1)}, bf16[2,32,192]{2,1,0:T(8,128)(2,1)S(1)}, u32[]{:S(2)}, u32[]{:S(2)}) collective-permute-start(bf16[2,32,192]{2,1,0:T(8,128)(2,1)S(1)} %get-tuple-element.101), channel_id=1, source_target_pairs={{0,9},{1,10},{2,11},{3,12},{4,13},{5,14},{6,15},{7,8},{8,17},{9,18... | collective-permute-start | bytes 73736 | tf_op jit(solution)/shard_map/ppermute | solution.py:562
  107.3 1.4 copy-start
  108.7 4.8 %copy-start.22 = (s32[144,1]{1,0:T(8,128)S(1)}, s32[144,1]{1,0:T(8,128)}, u32[]{:S(2)}) copy-start(s32[144,1]{1,0:T(8,128)} %constant.61.clone.take) | copy-start | bytes 1732
  108.7 34.6 %all-to-all-start.1 = ((bf16[128,64,128]{2,1,0:T(8,128)(2,1)}), bf16[128,64,128]{2,1,0:T(8,128)(2,1)S(1)}, u32[]{:S(2)}, u32[]{:S(2)}) async-start(bf16[128,64,128]{2,1,0:T(8,128)(2,1)} %copy-done), calls=%async_computation.1 | async-start | bytes 4194304 | tf_op jit(solution)/shard_map/all_to_all | solution.py:592
  113.5 0.9 copy-start.28
  114.4 1.1 copy-start.13

commit v4 on v3

--- a/solution.py
+++ b/solution.py
@@ -505,15 +505,18 @@
         kept[i] = x
 
 
-def fine_gradient_kernel(kept_u, kept_o, kept, coarse, gradients):
-    width, at = kept_u.shape[1], coarse.shape[0]
-    gradients[:at, :] = coarse[...]
+def fine_gradient_kernel(kept_u, kept_o, kept, coarse, gradients, rows, sems):
+    width = kept_u.shape[1]
     pieces = [mm(kept_u[...], kept[i], TN) for i in range(3)] + [mm(kept_o[...], kept[3], TN)]
     pieces = jnp.concatenate(pieces, axis=1).astype(BF16)
-    for j in range(pieces.shape[1] // 128):
-        gradients[at : at + width, :] = pieces[:, j * 128 : (j + 1) * 128]
-        at += width
-    gradients[at:, :] = jnp.zeros((gradients.shape[0] - at, 128), BF16)
+    count = pieces.shape[1] // 128
+    for j in range(count):
+        rows[j * width : (j + 1) * width, :] = pieces[:, j * 128 : (j + 1) * 128]
+    rows[count * width :, :] = jnp.zeros((rows.shape[0] - count * width, 128), BF16)
+    at = gradients.shape[0] - rows.shape[0]
+    copy = pltpu.make_async_copy(rows, gradients.at[at:, :], sems.at[0])
+    copy.start()
+    copy.wait()
 
 
 def restore_kernel(take, own, ra, rb, rc, output):
@@ -690,8 +693,11 @@
     delta_halo = exchange(coarse[5:8], 1)
     out_halo = exchange(coarse[1:4], 1)
     kept_x, kept_p, kept_o, after = lax.optimization_barrier((*kept, coarse[8]))
+    count = lons * lats
+    chunk = pad16(-(-(rows + 4 * d1 * d1 // 128) // count))
     (coarse_sums,) = call(
-        coarse_gradient_kernel, "coarse_gradients", [((rows, 128), BF16)], [], [after, coarse[9]], flops=2 * 10**9,
+        coarse_gradient_kernel, "coarse_gradients", [((count * chunk, 128), BF16)], [], [after, coarse[9]],
+        flops=2 * 10**9,
     )
     wide = ((2 * n1, d1), F32)
     u, unit, inverse, q, k, v = call(
@@ -707,12 +713,18 @@
         flops=6 * 10**9,
     )
     last_halo = exchange(backward[1:4], 1)
-    count = lons * lats
-    chunk = pad16(-(-(rows + 4 * d1 * d1 // 128) // count))
-    (sums,) = call(
-        fine_gradient_kernel, "fine_gradients", [((count * chunk, 128), BF16)], [],
-        [u, kept_o, backward[4], coarse_sums], flops=2 * 10**9,
-    )
+    anywhere = pl.BlockSpec(memory_space=pl.ANY)
+    sums = pl.pallas_call(
+        fine_gradient_kernel,
+        name="fine_gradients",
+        out_shape=jax.ShapeDtypeStruct(coarse_sums.shape, BF16),
+        in_specs=[VMEM] * 3 + [anywhere],
+        out_specs=anywhere,
+        scratch_shapes=[pltpu.VMEM((count * chunk - rows, 128), BF16), pltpu.SemaphoreType.DMA((1,))],
+        input_output_aliases={3: 0},
+        cost_estimate=pl.CostEstimate(flops=2 * 10**9, bytes_accessed=4 << 20, transcendentals=0),
+        compiler_params=pltpu.CompilerParams(vmem_limit_bytes=6 << 20),
+    )(u, kept_o, backward[4], coarse_sums)
     sums, *out_halo = lax.optimization_barrier((sums, *out_halo))
     sums, last_halo = summed(sums, last_halo)
 

time: 146 us -> 148 us (1.014)
  local copies, waits for them, and re-layouts: 3.03 us -> 6.21 us
    unnamed x72 -> x78, local copies, waits for them, and re-layouts: 2.65 us -> 5.84 us
    pallas_call x13 -> x12, Pallas kernels: 44.3 us -> 42.1 us  [call(): pl.pallas_call(kernel, name=name, out_shape=[jax.ShapeDtypeStruct(s, d) f...]
  transfers between devices with their start and end apart: 20 -> 20, of which waited for: 4 -> 4; matrix products, arithmetic and copies ran while one was open for 1% -> 1% of each run, Pallas kernels for 22% -> 21%
where the time goes in v4:
time: 148 us; the launch traced here: 147 us
  waiting for transfers between devices  59.5 us (40%)
  Pallas kernels  43 us (29%)
  starting transfers between devices  37.1 us (25%)
  local copies, waits for them, and re-layouts  6.21 us (4%)
    pallas_call x12, Pallas kernels, call(): pl.pallas_call(kernel, name=name, out_shape=[jax.ShapeDtypeStruct(s, d) f...  42.1 us
    ppermute x6, waiting for transfers between devices, move(): return lax.ppermute(value, ('lon', 'lat'), pairs)  31.9 us
    all_to_all x1, waiting for transfers between devices, summed(): lax.all_to_all(total, ('lon', 'lat'), 0, 0, tiled=True).reshape(-1, 128)  26.1 us
    ppermute x6, starting transfers between devices, move(): return lax.ppermute(value, ('lon', 'lat'), pairs)  11.9 us
    all_to_all x1, starting transfers between devices, summed(): terms = lax.all_to_all(block, ('lon', 'lat'), 0, 0, tiled=True)  7.5 us
    ppermute x6, starting transfers between devices, move(): lax.ppermute(value, 'lat', [(s, (s + lat_step) % lats) for s in range(lat...  7.39 us
    unnamed x78, local copies, waits for them, and re-layouts  5.84 us
    ppermute x6, starting transfers between devices, move(): lax.ppermute(value, 'lon', [(s, (s + lon_step) % lons) for s in range(lon...  5.51 us
  transfers between devices with their start and end apart: 20, of which 4 were waited for; matrix products, arithmetic and copies ran while one was open for 1% of the time, Pallas kernels for 21%

profile of v4, /device:TPU:0, one launch (start us, length us, event | category | flops | bytes accessed | tf_op | source)
XLA Modules:
  0.0 147.4 jit_solution(1369197755687951609)
XLA Ops:
  0.7 2.6 %prepare.1 = (bf16[2,128,192]{2,1,0:T(8,128)(2,1)}, bf16[2,64,192]{2,1,0:T(8,128)(2,1)}, bf16[2,32,192]{2,1,0:T(8,128)(2,1)}, bf16[2,64,384]{2,1,0:T(8,128)(2,1)...) custom-call(s32[224,1]{1,0:T(8,128)} %constant.47.clone.fsel, s32[128,1]{1,0:T(8,128)} %constant.48.clone.csel, ...), custom_call_target="tpu_custom_call" | custom-call | flops 1000000000 | bytes 4194304 | tf_op jit(solution)/shard_map/prepare/pallas_call | solution.py:542
  3.3 8.3 %collective-permute-start.2 = (bf16[2,32,192]{2,1,0:T(8,128)(2,1)}, bf16[2,32,192]{2,1,0:T(8,128)(2,1)S(1)}, u32[]{:S(2)}, u32[]{:S(2)}) collective-permute-start(bf16[2,32,192]{2,1,0:T(8,128)(2,1)} %get-tuple-element.61), channel_id=1, source_target_pairs={{0,127},{1,120},{2,121},{3,122},{4,123},{5,124},{6,125},{7,126},{8... | collective-permute-start | bytes 73736 | tf_op jit(solution)/shard_map/ppermute | solution.py:565
  11.5 1.7 %collective-permute-start.7 = (bf16[2,32,384]{2,1,0:T(8,128)(2,1)}, bf16[2,32,384]{2,1,0:T(8,128)(2,1)S(1)}, u32[]{:S(2)}, u32[]{:S(2)}) collective-permute-start(bf16[2,32,384]{2,1,0:T(8,128)(2,1)} %get-tuple-element.67), channel_id=1, source_target_pairs={{0,120},{8,0},{16,8},{24,16},{32,24},{40,32},{48,40},{56,48},{64,5... | collective-permute-start | bytes 147464 | tf_op jit(solution)/shard_map/ppermute | solution.py:557
  13.3 0.9 collective-permute-start.1
  14.2 0.1 copy.42
  14.3 0.1 copy.43
  14.4 0.1 select_maximum_fusion.types
  14.5 0.1 slice_bitcast_fusion.1
  14.6 0.1 pad_add_fusion
  14.7 0.1 copy.41
  14.8 0.1 reshape.40
  14.9 0.1 pad_add_fusion.1.place
  15.0 0.0 copy-start.33
  15.1 0.0 copy-start.5
  15.1 0.0 copy-start.7
  15.1 0.0 copy-start.17
  15.1 0.0 copy-start.18
  15.1 0.0 copy-start.19
  15.1 0.0 copy-start.22
  15.1 6.0 %fine_bias.1.bias = f32[2,2,1,72,432]{4,3,2,1,0:T(8,128)S(1)} custom-call(s32[3]{0:T(128)S(1)} %pad_add_fusion.1.place, s32[96]{0:T(128)S(1)} %copy-done.13, s32[48,1,256]{2,1,0:T(1,128)S(1)} %broadcast_in_dim.12.index, f32[6,2,3312]{2,1,0:T(2,128)S(1)} %bitcast.27), custom_call_target="tpu_custom_call" | custom-call | flops 4000000000 | bytes 4194304 | tf_op jit(solution)/shard_map/fine_bias/pallas_call | solution.py:542
  21.2 0.0 copy-start.30
  21.2 0.8 copy-done.30
  22.0 0.1 select_maximum_fusion.2.types
  22.1 0.1 reshape.41.merge_gain
  22.2 0.5 collective-permute-start.6
  22.8 1.1 copy-done.31
  23.9 6.1 %fine_forward.1 = (bf16[1152,192]{1,0:T(8,128)(2,1)S(1)}, bf16[2,128,192]{2,1,0:T(8,128)(2,1)S(1)}, bf16[2,64,192]{2,1,0:T(8,128)(2,1)S(1)}, bf16[2,32,192]{2,1,...) custom-call(s32[3]{0:T(128)S(1)} %pad_add_fusion.1.place, ...), custom_call_target="tpu_custom_call" | custom-call | flops 4000000000 | bytes 4194304 | tf_op jit(solution)/shard_map/fine_forward/pallas_call | solution.py:542
  30.0 3.0 %collective-permute-start.3 = (bf16[2,128,192]{2,1,0:T(8,128)(2,1)S(1)}, bf16[2,128,192]{2,1,0:T(8,128)(2,1)S(1)}, u32[]{:S(2)}, u32[]{:S(2)}) collective-permute-start(bf16[2,128,192]{2,1,0:T(8,128)(2,1)S(1)} %get-tuple-element.63), channel_id=1, source_target_pairs={{0,7},{1,0},{2,1},{3,2},{4,3},{5,4},{6,5},{7,6},{8,15},{9,8},{10,9... | collective-permute-start | bytes 294920 | tf_op jit(solution)/shard_map/ppermute | solution.py:559
  33.0 1.3 collective-permute-start.4
  34.3 0.0 copy-start.16
  34.3 0.0 copy-start.21
  34.3 0.0 copy-start.24
  34.3 0.0 copy-start.25
  34.3 0.0 copy-start.26
  34.3 0.0 copy-start.27
  34.3 6.0 %coarse_bias.1.bias = f32[2,1,3,72,288]{4,3,2,1,0:T(8,128)S(1)} custom-call(s32[3]{0:T(128)S(1)} %pad_add_fusion.1.place, s32[96]{0:T(128)S(1)} %copy-done.13, s32[48,1,256]{2,1,0:T(1,128)S(1)} %broadcast_in_dim.12.index, f32[12,1,3312]{2,1,0:T(1,128)S(1)} %bitcast.28), custom_call_target="tpu_custom_call" | custom-call | flops 4000000000 | bytes 4194304 | tf_op jit(solution)/shard_map/coarse_bias/pallas_call | solution.py:542
  40.5 7.5 %coarse.1 = (bf16[288,384]{1,0:T(8,128)(2,1)S(1)}, bf16[2,64,384]{2,1,0:T(8,128)(2,1)S(1)}, bf16[2,32,384]{2,1,0:T(8,128)(2,1)S(1)}, bf16[2,32,384]{2,1,0:T(8,12...) custom-call(s32[3]{0:T(128)S(1)} %pad_add_fusion.1.place, ...), custom_call_target="tpu_custom_call" | custom-call | flops 6000000000 | bytes 4194304 | tf_op jit(solution)/shard_map/coarse/pallas_call | solution.py:542
  48.0 0.6 collective-permute-start.11
  48.6 1.5 %collective-permute-start.13 = (bf16[2,32,384]{2,1,0:T(8,128)(2,1)S(1)}, bf16[2,32,384]{2,1,0:T(8,128)(2,1)S(1)}, u32[]{:S(2)}, u32[]{:S(2)}) collective-permute-start(bf16[2,32,384]{2,1,0:T(8,128)(2,1)S(1)} %get-tuple-element.92), channel_id=1, source_target_pairs={{0,8},{8,16},{16,24},{24,32},{32,40},{40,48},{48,56},{56,64},{64,7... | collective-permute-start | bytes 147464 | tf_op jit(solution)/shard_map/ppermute | solution.py:557
  50.2 0.2 collective-permute-start.14
  50.4 0.0 collective-permute-start.10
  50.4 1.5 %collective-permute-start.9 = (bf16[2,128,192]{2,1,0:T(8,128)(2,1)S(1)}, bf16[2,128,192]{2,1,0:T(8,128)(2,1)S(1)}, u32[]{:S(2)}, u32[]{:S(2)}) collective-permute-start(bf16[2,128,192]{2,1,0:T(8,128)(2,1)S(1)} %get-tuple-element.79), channel_id=1, source_target_pairs={{0,1},{1,2},{2,3},{3,4},{4,5},{5,6},{6,7},{7,0},{8,9},{9,10},{10,1... | collective-permute-start | bytes 294920 | tf_op jit(solution)/shard_map/ppermute | solution.py:559
  51.9 1.0 fine_again.1
  53.0 0.0 copy-start.15
  53.0 0.0 copy-start.20
  53.0 1.3 coarse_gradients.1.coarse
  54.3 2.5 %collective-permute-done.11.rc = bf16[2,32,192]{2,1,0:T(8,128)(2,1)S(1)} collective-permute-done((bf16[2,32,192]{2,1,0:T(8,128)(2,1)S(1)}, bf16[2,32,192]{2,1,0:T(8,128)(2,1)S(1)}, u32[]{:S(2)}, u32[]{:S(2)}) %collective-permute-start.11) | collective-permute-done | bytes 24608 | tf_op jit(solution)/shard_map/ppermute | solution.py:565
  56.9 1.4 collective-permute-start.12
  58.2 1.5 %collective-permute-done.9.ra = bf16[2,128,192]{2,1,0:T(8,128)(2,1)S(1)} collective-permute-done((bf16[2,128,192]{2,1,0:T(8,128)(2,1)S(1)}, bf16[2,128,192]{2,1,0:T(8,128)(2,1)S(1)}, u32[]{:S(2)}, u32[]{:S(2)}) %collective-permute-start.9) | collective-permute-done | bytes 98336 | tf_op jit(solution)/shard_map/ppermute | solution.py:559
  59.7 6.1 %fine_backward.1 = (bf16[1152,192]{1,0:T(8,128)(2,1)S(1)}, bf16[2,128,192]{2,1,0:T(8,128)(2,1)S(1)}, bf16[2,64,192]{2,1,0:T(8,128)(2,1)S(1)}, bf16[2,32,192]{2,1,0:T(8,128)(2,1)S(1)}, bf16[4,1152,192]{2,1,0:T(8,128)(2,1)S(1)}) custom-call(s32[576,1]{1,0:T(8,128)S(1)} %copy-done.15, s32[224,1]{1,0:T(8,128)S(1)} %copy-done.20, ...), custom_call_target="tpu_custom_call" | custom-call | flops 6000000000 | bytes 4194304 | tf_op jit(solution)/shard_map/fine_backward/pallas_call | solution.py:542
  65.8 0.9 fine_gradients.1
  66.7 1.3 copy-done.1
  68.1 7.5 %all-to-all-start = ((bf16[128,64,128]{2,1,0:T(8,128)(2,1)}), bf16[128,64,128]{2,1,0:T(8,128)(2,1)S(1)}, u32[]{:S(2)}, u32[]{:S(2)}) async-start(bf16[128,64,128]{2,1,0:T(8,128)(2,1)} %bitcast.21), calls=%async_computation | async-start | bytes 4194304 | tf_op jit(solution)/shard_map/all_to_all | solution.py:592
  75.6 1.0 collective-permute-start.15
  76.6 2.8 %collective-permute-start.17 = (bf16[2,32,192]{2,1,0:T(8,128)(2,1)S(1)}, bf16[2,32,192]{2,1,0:T(8,128)(2,1)S(1)}, u32[]{:S(2)}, u32[]{:S(2)}) collective-permute-start(bf16[2,32,192]{2,1,0:T(8,128)(2,1)S(1)} %get-tuple-element.101), channel_id=1, source_target_pairs={{0,9},{1,10},{2,11},{3,12},{4,13},{5,14},{6,15},{7,8},{8,17},{9,18... | collective-permute-start | bytes 73736 | tf_op jit(solution)/shard_map/ppermute | solution.py:565
  79.4 29.3 %collective-permute-done.17.rc = bf16[2,32,192]{2,1,0:T(8,128)(2,1)S(1)} collective-permute-done((bf16[2,32,192]{2,1,0:T(8,128)(2,1)S(1)}, bf16[2,32,192]{2,1,0:T(8,128)(2,1)S(1)}, u32[]{:S(2)}, u32[]{:S(2)}) %collective-permute-start.17) | collective-permute-done | bytes 24608 | tf_op jit(solution)/shard_map/ppermute | solution.py:565
  108.7 0.5 add.13
  109.2 1.3 copy-done
  110.6 4.8 %all-to-all-start.1 = ((bf16[128,64,128]{2,1,0:T(8,128)(2,1)}), bf16[128,64,128]{2,1,0:T(8,128)(2,1)S(1)}, u32[]{:S(2)}, u32[]{:S(2)}) async-start(bf16[128,64,128]{2,1,0:T(8,128)(2,1)} %copy-done), calls=%async_computation.1 | async-start | bytes 4194304 | tf_op jit(solution)/shard_map/all_to_all | solution.py:595
  115.4 0.9 copy-done.29
  116.3 1.1 restore_coarse.1
  117.4 1.7 %restore_fine.1 = bf16[1152,192]{1,0:T(8,128)(2,1)} custom-call(s32[576,1]{1,0:T(8,128)S(1)} %copy-done.14, bf16[1152,192]{1,0:T(8,128)(2,1)S(1)} %get-tuple-element.97.own, bf16[2,128,192]{2,1,0:T(8,128)(2,1)S(1)} %collective-permute-done.15.ra, bf16[2,64,192]{2,1,0:T(8,128)(2,1)S(1)} %collective-permute-done.16.rb, ...), custom_call_target="tpu_custom_call" | custom-call | flops 1000000000 | bytes 4194304 | tf_op jit(solution)/shard_map/restore_fine/pallas_call | solution.py:542
  119.1 26.1 %all-to-all-done.1 = bf16[128,64,128]{2,1,0:T(8,128)(2,1)S(1)} async-done(((bf16[128,64,128]{2,1,0:T(8,128)(2,1)}), bf16[128,64,128]{2,1,0:T(8,128)(2,1)S(1)}, u32[]{:S(2)}, u32[]{:S(2)}) %all-to-all-start.1) | async-done | bytes 2097184 | tf_op jit(solution)/shard_map/all_to_all | solution.py:595
  145.2 2.1 %finish.1 = (f32[192,576]{1,0:T(8,128)}, f32[192,192]{1,0:T(8,128)}, f32[768,384]{1,0:T(8,128)}, f32[384,1152]{1,0:T(8,128)}, f32[384,384]{1,0:T(8,128)}) custom-call(bf16[8192,128]{1,0:T(8,128)(2,1)S(1)} %bitcast.22), custom_call_target="tpu_custom_call" | custom-call | flops 1000000000 | bytes 4194304 | tf_op jit(solution)/shard_map/finish/pallas_call | solution.py:542
  (78 shorter events, 0.2 us)
Async XLA Ops:
  0.6 13.6 %copy-start.34 = (f32[3,6]{1,0:T(4,128)S(1)}, f32[3,6]{1,0:T(4,128)}, u32[]{:S(2)}) copy-start(f32[3,6]{1,0:T(4,128)} %param.39) | copy-start | bytes 220
  0.6 13.7 %copy-start.35 = (f32[3,12]{1,0:T(4,128)S(1)}, f32[3,12]{1,0:T(4,128)}, u32[]{:S(2)}) copy-start(f32[3,12]{1,0:T(4,128)} %param.46) | copy-start | bytes 436
  0.7 13.8 %copy-start.32 = (s32[144,144]{1,0:T(8,128)S(1)}, s32[144,144]{1,0:T(8,128)}, u32[]{:S(2)}) copy-start(s32[144,144]{1,0:T(8,128)} %param.49) | copy-start | bytes 248836
  0.7 14.3 %copy-start.9 = (f32[1,2,3312,6]{2,1,3,0:T(2,128)S(1)}, f32[1,2,3312,6]{2,1,3,0:T(2,128)}, u32[]{:S(2)}) copy-start(f32[1,2,3312,6]{2,1,3,0:T(2,128)} %param.38) | copy-start | bytes 476932
  0.7 14.3 %copy-start.13 = (s32[96]{0:T(128)S(1)}, s32[96]{0:T(128)}, u32[]{:S(2)}) copy-start(s32[96]{0:T(128)} %valid.3) | copy-start | bytes 1156
  3.3 18.9 %collective-permute-start.2 = (bf16[2,32,192]{2,1,0:T(8,128)(2,1)}, bf16[2,32,192]{2,1,0:T(8,128)(2,1)S(1)}, u32[]{:S(2)}, u32[]{:S(2)}) collective-permute-start(bf16[2,32,192]{2,1,0:T(8,128)(2,1)} %get-tuple-element.61), channel_id=1, source_target_pairs={{0,127},{1,120},{2,121},{3,122},{4,123},{5,124},{6,125},{7,126},{8... | collective-permute-start | bytes 73736 | tf_op jit(solution)/shard_map/ppermute | solution.py:565
  11.5 21.4 %collective-permute-start.7 = (bf16[2,32,384]{2,1,0:T(8,128)(2,1)}, bf16[2,32,384]{2,1,0:T(8,128)(2,1)S(1)}, u32[]{:S(2)}, u32[]{:S(2)}) collective-permute-start(bf16[2,32,384]{2,1,0:T(8,128)(2,1)} %get-tuple-element.67), channel_id=1, source_target_pairs={{0,120},{8,0},{16,8},{24,16},{32,24},{40,32},{48,40},{56,48},{64,5... | collective-permute-start | bytes 147464 | tf_op jit(solution)/shard_map/ppermute | solution.py:557
  13.3 27.1 %collective-permute-start.8 = (bf16[2,32,384]{2,1,0:T(8,128)(2,1)}, bf16[2,32,384]{2,1,0:T(8,128)(2,1)S(1)}, u32[]{:S(2)}, u32[]{:S(2)}) collective-permute-start(bf16[2,32,384]{2,1,0:T(8,128)(2,1)} %get-tuple-element.68), channel_id=1, source_target_pairs={{0,127},{1,120},{2,121},{3,122},{4,123},{5,124},{6,125},{7,126},{8... | collective-permute-start | bytes 147464 | tf_op jit(solution)/shard_map/ppermute | solution.py:565
  13.3 9.4 %collective-permute-start.1 = (bf16[2,64,192]{2,1,0:T(8,128)(2,1)}, bf16[2,64,192]{2,1,0:T(8,128)(2,1)S(1)}, u32[]{:S(2)}, u32[]{:S(2)}) collective-permute-start(bf16[2,64,192]{2,1,0:T(8,128)(2,1)} %get-tuple-element.60), channel_id=1, source_target_pairs={{0,120},{8,0},{16,8},{24,16},{32,24},{40,32},{48,40},{56,48},{64,5... | collective-permute-start | bytes 147464 | tf_op jit(solution)/shard_map/ppermute | solution.py:557
  14.2 8.5 %collective-permute-start = (bf16[2,128,192]{2,1,0:T(8,128)(2,1)}, bf16[2,128,192]{2,1,0:T(8,128)(2,1)S(1)}, u32[]{:S(2)}, u32[]{:S(2)}) collective-permute-start(bf16[2,128,192]{2,1,0:T(8,128)(2,1)} %get-tuple-element.59), channel_id=1, source_target_pairs={{0,7},{1,0},{2,1},{3,2},{4,3},{5,4},{6,5},{7,6},{8,15},{9,8},{10,9... | collective-permute-start | bytes 294920 | tf_op jit(solution)/shard_map/ppermute | solution.py:559
  15.0 7.1 %copy-start.36 = (f32[384]{0:T(512)S(1)}, f32[384]{0:T(512)}, u32[]{:S(2)}) copy-start(f32[384]{0:T(512)} %param.42) | copy-start | bytes 4612
  15.0 7.1 %copy-start.33 = (f32[768]{0:T(1024)S(1)}, f32[768]{0:T(1024)}, u32[]{:S(2)}) copy-start(f32[768]{0:T(1024)} %param.40) | copy-start | bytes 9220
  15.0 7.2 %copy-start.37 = (bf16[2,64,384]{2,1,0:T(8,128)(2,1)S(1)}, bf16[2,64,384]{2,1,0:T(8,128)(2,1)}, u32[]{:S(2)}) copy-start(bf16[2,64,384]{2,1,0:T(8,128)(2,1)} %get-tuple-element.66) | copy-start | bytes 294916
  15.0 7.7 %copy-start.3 = (bf16[2,12,48,192]{3,2,1,0:T(8,128)(2,1)S(1)}, bf16[2,12,48,192]{3,2,1,0:T(8,128)(2,1)}, u32[]{:S(2)}) copy-start(bf16[2,12,48,192]{3,2,1,0:T(8,128)(2,1)} %param.33) | copy-start | bytes 1327108
  15.1 7.7 %copy-start.5 = (s32[96,768]{1,0:T(8,128)S(1)}, s32[96,768]{1,0:T(8,128)}, u32[]{:S(2)}) copy-start(s32[96,768]{1,0:T(8,128)} %surface.3) | copy-start | bytes 884740
  15.1 7.7 %copy-start.7 = (bf16[192,576]{1,0:T(8,128)(2,1)S(1)}, bf16[192,576]{1,0:T(8,128)(2,1)}, u32[]{:S(2)}) copy-start(bf16[192,576]{1,0:T(8,128)(2,1)} %project.7) | copy-start | bytes 663556
  15.1 7.7 %copy-start.11 = (bf16[192,192]{1,0:T(8,128)(2,1)S(1)}, bf16[192,192]{1,0:T(8,128)(2,1)}, u32[]{:S(2)}) copy-start(bf16[192,192]{1,0:T(8,128)(2,1)} %combine.5) | copy-start | bytes 221188
  15.1 7.7 %copy-start.12 = (f32[192]{0:T(256)S(1)}, f32[192]{0:T(256)}, u32[]{:S(2)}) copy-start(f32[192]{0:T(256)} %param.35) | copy-start | bytes 2308
  15.1 7.7 %copy-start.17 = (s32[576,1]{1,0:T(8,128)S(1)}, s32[576,1]{1,0:T(8,128)}, u32[]{:S(2)}) copy-start(s32[576,1]{1,0:T(8,128)} %constant.52.clone.col) | copy-start | bytes 6916
  15.1 7.7 %copy-start.18 = (s32[576,1]{1,0:T(8,128)S(1)}, s32[576,1]{1,0:T(8,128)}, u32[]{:S(2)}) copy-start(s32[576,1]{1,0:T(8,128)} %constant.51.clone.row) | copy-start | bytes 6916
  15.1 7.7 %copy-start.19 = (s32[576,1]{1,0:T(8,128)S(1)}, s32[576,1]{1,0:T(8,128)}, u32[]{:S(2)}) copy-start(s32[576,1]{1,0:T(8,128)} %constant.49.clone.take) | copy-start | bytes 6916
  15.1 7.7 %copy-start.22 = (s32[224,1]{1,0:T(8,128)S(1)}, s32[224,1]{1,0:T(8,128)}, u32[]{:S(2)}) copy-start(s32[224,1]{1,0:T(8,128)} %constant.50.clone.sel) | copy-start | bytes 2692
  21.2 0.8 copy-start.30
  22.2 18.2 %collective-permute-start.6 = (bf16[2,64,384]{2,1,0:T(8,128)(2,1)S(1)}, bf16[2,64,384]{2,1,0:T(8,128)(2,1)S(1)}, u32[]{:S(2)}, u32[]{:S(2)}) collective-permute-start(bf16[2,64,384]{2,1,0:T(8,128)(2,1)S(1)} %copy-done.37), channel_id=1, source_target_pairs={{0,7},{1,0},{2,1},{3,2},{4,3},{5,4},{6,5},{7,6},{8,15},{9,8},{10,9... | collective-permute-start | bytes 294920 | tf_op jit(solution)/shard_map/ppermute | solution.py:559
  22.8 1.1 copy-start.31
  23.9 10.4 %copy-start.10 = (f32[1,1,3312,12]{2,1,3,0:T(1,128)S(1)}, f32[1,1,3312,12]{2,1,3,0:T(1,128)}, u32[]{:S(2)}) copy-start(f32[1,1,3312,12]{2,1,3,0:T(1,128)} %param.45) | copy-start | bytes 476932
  30.0 10.4 %collective-permute-start.3 = (bf16[2,128,192]{2,1,0:T(8,128)(2,1)S(1)}, bf16[2,128,192]{2,1,0:T(8,128)(2,1)S(1)}, u32[]{:S(2)}, u32[]{:S(2)}) collective-permute-start(bf16[2,128,192]{2,1,0:T(8,128)(2,1)S(1)} %get-tuple-element.63), channel_id=1, source_target_pairs={{0,7},{1,0},{2,1},{3,2},{4,3},{5,4},{6,5},{7,6},{8,15},{9,8},{10,9... | collective-permute-start | bytes 294920 | tf_op jit(solution)/shard_map/ppermute | solution.py:559
  33.0 7.4 %collective-permute-start.5 = (bf16[2,32,192]{2,1,0:T(8,128)(2,1)S(1)}, bf16[2,32,192]{2,1,0:T(8,128)(2,1)S(1)}, u32[]{:S(2)}, u32[]{:S(2)}) collective-permute-start(bf16[2,32,192]{2,1,0:T(8,128)(2,1)S(1)} %get-tuple-element.65), channel_id=1, source_target_pairs={{0,127},{1,120},{2,121},{3,122},{4,123},{5,124},{6,125},{7,126},{8... | collective-permute-start | bytes 73736 | tf_op jit(solution)/shard_map/ppermute | solution.py:565
  33.0 7.4 %collective-permute-start.4 = (bf16[2,64,192]{2,1,0:T(8,128)(2,1)S(1)}, bf16[2,64,192]{2,1,0:T(8,128)(2,1)S(1)}, u32[]{:S(2)}, u32[]{:S(2)}) collective-permute-start(bf16[2,64,192]{2,1,0:T(8,128)(2,1)S(1)} %get-tuple-element.64), channel_id=1, source_target_pairs={{0,120},{8,0},{16,8},{24,16},{32,24},{40,32},{48,40},{56,48},{64,5... | collective-permute-start | bytes 147464 | tf_op jit(solution)/shard_map/ppermute | solution.py:557
  34.2 6.2 %copy-start.2 = (bf16[384,1152]{1,0:T(8,128)(2,1)S(1)}, bf16[384,1152]{1,0:T(8,128)(2,1)}, u32[]{:S(2)}) copy-start(bf16[384,1152]{1,0:T(8,128)(2,1)} %project.5) | copy-start | bytes 2654212
  34.2 6.2 %copy-start.4 = (bf16[768,384]{1,0:T(8,128)(2,1)S(1)}, bf16[768,384]{1,0:T(8,128)(2,1)}, u32[]{:S(2)}) copy-start(bf16[768,384]{1,0:T(8,128)(2,1)} %merge_weight.1) | copy-start | bytes 1769476
  34.2 6.2 %copy-start.6 = (bf16[384,384]{1,0:T(8,128)(2,1)S(1)}, bf16[384,384]{1,0:T(8,128)(2,1)}, u32[]{:S(2)}) copy-start(bf16[384,384]{1,0:T(8,128)(2,1)} %combine.4) | copy-start | bytes 884740
  34.2 6.2 %copy-start.8 = (bf16[2,6,24,384]{3,2,1,0:T(8,128)(2,1)S(1)}, bf16[2,6,24,384]{3,2,1,0:T(8,128)(2,1)}, u32[]{:S(2)}) copy-start(bf16[2,6,24,384]{3,2,1,0:T(8,128)(2,1)} %param.34) | copy-start | bytes 663556
  34.3 6.2 %copy-start.16 = (s32[576,1]{1,0:T(8,128)S(1)}, s32[576,1]{1,0:T(8,128)}, u32[]{:S(2)}) copy-start(s32[576,1]{1,0:T(8,128)} %constant.53.clone.take) | copy-start | bytes 6916
  34.3 6.2 %copy-start.21 = (s32[224,1]{1,0:T(8,128)S(1)}, s32[224,1]{1,0:T(8,128)}, u32[]{:S(2)}) copy-start(s32[224,1]{1,0:T(8,128)} %constant.56.clone.fsel) | copy-start | bytes 2692
  34.3 6.2 %copy-start.24 = (s32[144,1]{1,0:T(8,128)S(1)}, s32[144,1]{1,0:T(8,128)}, u32[]{:S(2)}) copy-start(s32[144,1]{1,0:T(8,128)} %constant.58.clone.col) | copy-start | bytes 1732
  34.3 6.2 %copy-start.25 = (s32[144,1]{1,0:T(8,128)S(1)}, s32[144,1]{1,0:T(8,128)}, u32[]{:S(2)}) copy-start(s32[144,1]{1,0:T(8,128)} %constant.57.clone.row) | copy-start | bytes 1732
  34.3 6.2 %copy-start.26 = (s32[144,1]{1,0:T(8,128)S(1)}, s32[144,1]{1,0:T(8,128)}, u32[]{:S(2)}) copy-start(s32[144,1]{1,0:T(8,128)} %constant.54.clone.ctake) | copy-start | bytes 1732
  34.3 6.2 %copy-start.27 = (s32[128,1]{1,0:T(8,128)S(1)}, s32[128,1]{1,0:T(8,128)}, u32[]{:S(2)}) copy-start(s32[128,1]{1,0:T(8,128)} %constant.55.clone.csel) | copy-start | bytes 1540
  48.0 5.0 %copy-start.28 = (bf16[288,384]{1,0:T(8,128)(2,1)}, bf16[288,384]{1,0:T(8,128)(2,1)S(1)}, u32[]{:S(2)}) copy-start(bf16[288,384]{1,0:T(8,128)(2,1)S(1)} %get-tuple-element.70.own) | copy-start | bytes 663556
  48.0 8.8 %collective-permute-start.11 = (bf16[2,32,192]{2,1,0:T(8,128)(2,1)S(1)}, bf16[2,32,192]{2,1,0:T(8,128)(2,1)S(1)}, u32[]{:S(2)}, u32[]{:S(2)}) collective-permute-start(bf16[2,32,192]{2,1,0:T(8,128)(2,1)S(1)} %get-tuple-element.81), channel_id=1, source_target_pairs={{0,9},{1,10},{2,11},{3,12},{4,13},{5,14},{6,15},{7,8},{8,17},{9,18... | collective-permute-start | bytes 73736 | tf_op jit(solution)/shard_map/ppermute | solution.py:565
  48.6 19.4 %collective-permute-start.13 = (bf16[2,32,384]{2,1,0:T(8,128)(2,1)S(1)}, bf16[2,32,384]{2,1,0:T(8,128)(2,1)S(1)}, u32[]{:S(2)}, u32[]{:S(2)}) collective-permute-start(bf16[2,32,384]{2,1,0:T(8,128)(2,1)S(1)} %get-tuple-element.92), channel_id=1, source_target_pairs={{0,8},{8,16},{16,24},{24,32},{32,40},{40,48},{48,56},{56,64},{64,7... | collective-permute-start | bytes 147464 | tf_op jit(solution)/shard_map/ppermute | solution.py:557
  50.2 17.9 %collective-permute-start.14 = (bf16[2,32,384]{2,1,0:T(8,128)(2,1)S(1)}, bf16[2,32,384]{2,1,0:T(8,128)(2,1)S(1)}, u32[]{:S(2)}, u32[]{:S(2)}) collective-permute-start(bf16[2,32,384]{2,1,0:T(8,128)(2,1)S(1)} %get-tuple-element.93), channel_id=1, source_target_pairs={{0,9},{1,10},{2,11},{3,12},{4,13},{5,14},{6,15},{7,8},{8,17},{9,18... | collective-permute-start | bytes 147464 | tf_op jit(solution)/shard_map/ppermute | solution.py:565
  50.4 7.8 %collective-permute-start.10 = (bf16[2,64,192]{2,1,0:T(8,128)(2,1)S(1)}, bf16[2,64,192]{2,1,0:T(8,128)(2,1)S(1)}, u32[]{:S(2)}, u32[]{:S(2)}) collective-permute-start(bf16[2,64,192]{2,1,0:T(8,128)(2,1)S(1)} %get-tuple-element.80), channel_id=1, source_target_pairs={{0,8},{8,16},{16,24},{24,32},{32,40},{40,48},{48,56},{56,64},{64,7... | collective-permute-start | bytes 147464 | tf_op jit(solution)/shard_map/ppermute | solution.py:557
  50.4 9.3 %collective-permute-start.9 = (bf16[2,128,192]{2,1,0:T(8,128)(2,1)S(1)}, bf16[2,128,192]{2,1,0:T(8,128)(2,1)S(1)}, u32[]{:S(2)}, u32[]{:S(2)}) collective-permute-start(bf16[2,128,192]{2,1,0:T(8,128)(2,1)S(1)} %get-tuple-element.79), channel_id=1, source_target_pairs={{0,1},{1,2},{2,3},{3,4},{4,5},{5,6},{6,7},{7,0},{8,9},{9,10},{10,1... | collective-permute-start | bytes 294920 | tf_op jit(solution)/shard_map/ppermute | solution.py:559
  53.0 6.7 %copy-start.15 = (s32[576,1]{1,0:T(8,128)S(1)}, s32[576,1]{1,0:T(8,128)}, u32[]{:S(2)}) copy-start(s32[576,1]{1,0:T(8,128)} %constant.59.clone.take) | copy-start | bytes 6916
  53.0 6.7 %copy-start.20 = (s32[224,1]{1,0:T(8,128)S(1)}, s32[224,1]{1,0:T(8,128)}, u32[]{:S(2)}) copy-start(s32[224,1]{1,0:T(8,128)} %constant.60.clone.sel) | copy-start | bytes 2692
  56.9 11.2 %collective-permute-start.12 = (bf16[2,64,384]{2,1,0:T(8,128)(2,1)S(1)}, bf16[2,64,384]{2,1,0:T(8,128)(2,1)S(1)}, u32[]{:S(2)}, u32[]{:S(2)}) collective-permute-start(bf16[2,64,384]{2,1,0:T(8,128)(2,1)S(1)} %get-tuple-element.91), channel_id=1, source_target_pairs={{0,1},{1,2},{2,3},{3,4},{4,5},{5,6},{6,7},{7,0},{8,9},{9,10},{10,1... | collective-permute-start | bytes 294920 | tf_op jit(solution)/shard_map/ppermute | solution.py:559
  66.7 1.3 copy-start.1
  68.1 40.7 %all-to-all-start = ((bf16[128,64,128]{2,1,0:T(8,128)(2,1)}), bf16[128,64,128]{2,1,0:T(8,128)(2,1)S(1)}, u32[]{:S(2)}, u32[]{:S(2)}) async-start(bf16[128,64,128]{2,1,0:T(8,128)(2,1)} %bitcast.21), calls=%async_computation | async-start | bytes 4194304 | tf_op jit(solution)/shard_map/all_to_all | solution.py:592
  75.6 33.1 %collective-permute-start.15 = (bf16[2,128,192]{2,1,0:T(8,128)(2,1)S(1)}, bf16[2,128,192]{2,1,0:T(8,128)(2,1)S(1)}, u32[]{:S(2)}, u32[]{:S(2)}) collective-permute-start(bf16[2,128,192]{2,1,0:T(8,128)(2,1)S(1)} %get-tuple-element.99), channel_id=1, source_target_pairs={{0,1},{1,2},{2,3},{3,4},{4,5},{5,6},{6,7},{7,0},{8,9},{9,10},{10,1... | collective-permute-start | bytes 294920 | tf_op jit(solution)/shard_map/ppermute | solution.py:559
  76.6 32.1 %collective-permute-start.16 = (bf16[2,64,192]{2,1,0:T(8,128)(2,1)S(1)}, bf16[2,64,192]{2,1,0:T(8,128)(2,1)S(1)}, u32[]{:S(2)}, u32[]{:S(2)}) collective-permute-start(bf16[2,64,192]{2,1,0:T(8,128)(2,1)S(1)} %get-tuple-element.100), channel_id=1, source_target_pairs={{0,8},{8,16},{16,24},{24,32},{32,40},{40,48},{48,56},{56,64},{64,7... | collective-permute-start | bytes 147464 | tf_op jit(solution)/shard_map/ppermute | solution.py:557
  76.6 32.1 %collective-permute-start.17 = (bf16[2,32,192]{2,1,0:T(8,128)(2,1)S(1)}, bf16[2,32,192]{2,1,0:T(8,128)(2,1)S(1)}, u32[]{:S(2)}, u32[]{:S(2)}) collective-permute-start(bf16[2,32,192]{2,1,0:T(8,128)(2,1)S(1)} %get-tuple-element.101), channel_id=1, source_target_pairs={{0,9},{1,10},{2,11},{3,12},{4,13},{5,14},{6,15},{7,8},{8,17},{9,18... | collective-permute-start | bytes 73736 | tf_op jit(solution)/shard_map/ppermute | solution.py:565
  109.2 1.3 copy-start
  110.6 4.8 %copy-start.23 = (s32[144,1]{1,0:T(8,128)S(1)}, s32[144,1]{1,0:T(8,128)}, u32[]{:S(2)}) copy-start(s32[144,1]{1,0:T(8,128)} %constant.61.clone.take) | copy-start | bytes 1732
  110.6 34.6 %all-to-all-start.1 = ((bf16[128,64,128]{2,1,0:T(8,128)(2,1)}), bf16[128,64,128]{2,1,0:T(8,128)(2,1)S(1)}, u32[]{:S(2)}, u32[]{:S(2)}) async-start(bf16[128,64,128]{2,1,0:T(8,128)(2,1)} %copy-done), calls=%async_computation.1 | async-start | bytes 4194304 | tf_op jit(solution)/shard_map/all_to_all | solution.py:595
  115.4 0.9 copy-start.29
  116.3 1.1 copy-start.14
